TPU v7x, 512 devices: a whole 4x4x16 slice. The times are simulated.
512 devices in a mesh: visit: 128 (over z, x_hi, y), patch: 4 (over x_lo, core).
Axes of the slice: x: 4 (x_hi: 2, x_lo: 2; x = x_hi * 2 + x_lo), y: 4, z: 16, core: 2. Of those that a mesh axis runs over, the one named last changes fastest.
Arguments:
- template: float32 [4, 8192, 512], P('patch', 'visit'), may hold values from -24 to 24
- science: float32 [128, 4, 64, 512], P('visit', 'patch'), may hold values from -28 to 28
- inverse_variance: float32 [128, 4, 64, 512], P('visit', 'patch'), may hold values from 0.2 to 5
- intersections: int32 [128, 4, 3], P('visit', 'patch'), may hold values from -6 to 127, as said below
Outputs:
- difference: float32 [128, 4, 64, 512], P('visit', 'patch')
- coadd_difference: float32 [4, 8192, 512], P('patch', 'visit')
Inputs may be any that keep to these rules, and one draw needn't show every extreme that they name: Entry 0 of intersections[v, p] is the tile of patch p under visit v's stamp, at most 6 away from v, and that distance is reached; entries 1 and 2 are the stamp's row and column offsets against the tile, from -6 to 6, both ends reached.
All inputs are finite; a program needn't handle non-finite values.
Results may differ from a plain program's by a relative error of at most 0.0003.
Values sent between devices are 32-bit elements; how exact they have to be, the bound alone decides.
No kernel may reach another device: no remote copies, remote signals or barrier semaphores. Data moves between devices by JAX's collectives and lax.ppermute only.
A program may use at most 128 MiB of HBM per device.

v0:
```python
import math

import jax
import jax.numpy as jnp
import numpy as np
from jax import lax
from jax.sharding import PartitionSpec as P

KHALF = 10
SHIFT = 6
REACH = 6
NBASIS = 28
HALO = 16


SIGMAS = (1.0, 2.0, 4.0)
DEGREES = (4, 2, 2)
ridge_weight = 0.01


def with_halo(block, sides, width):
    for axis, dim in sides:
        count = lax.axis_size(axis)
        forward = [(i, i + 1) for i in range(count - 1)]
        backward = [(target, source) for source, target in forward]
        low = lax.ppermute(
            lax.slice_in_dim(block, block.shape[dim] - width, None, axis=dim), axis, forward
        )
        high = lax.ppermute(lax.slice_in_dim(block, 0, width, axis=dim), axis, backward)
        block = jnp.concatenate([low, block, high], axis=dim)
    return block


def from_behind(shard, axis, by):
    peers = lax.axis_size(axis)
    pairs = [(i, i + by) for i in range(peers) if 0 <= i + by < peers]
    return lax.ppermute(shard, axis, pairs)


def factor_table(khalf):
    listed = []
    for width_sigma, degree in zip(SIGMAS, DEGREES):
        for exponent in range(degree + 1):
            values = [
                math.exp(-(offset * offset) / (2.0 * width_sigma * width_sigma))
                * (offset / khalf) ** exponent
                for offset in range(-khalf, khalf + 1)
            ]
            scale_norm = math.sqrt(sum((entry * entry for entry in values)))
            listed.append([entry / scale_norm for entry in values])
    return np.array(listed, dtype=np.float32)


def basis_pairs():
    pairs = []
    first_index = 0
    for degree in DEGREES:
        for power_row in range(degree + 1):
            for power_col in range(degree + 1 - power_row):
                pairs.append((first_index + power_row, first_index + power_col))
        first_index += degree + 1
    return pairs


def column_bands(table, block_width):
    distance = (
        np.arange(block_width + table.shape[1] - 1)[:, None] - np.arange(block_width)[None, :]
    )
    band_table = np.zeros((table.shape[0], distance.shape[0], block_width), np.float32)
    for offset_index in range(table.shape[1]):
        band_table = (
            band_table + table[:, offset_index, None, None] * (distance == offset_index)[None]
        )
    return band_table


def row_bands(table, height):
    distance = np.arange(height + table.shape[1] - 1)[None, :] - np.arange(height)[:, None]
    band_table = np.zeros((table.shape[0], height, distance.shape[1]), np.float32)
    for offset_index in range(table.shape[1]):
        band_table = (
            band_table + table[:, offset_index, None, None] * (distance == offset_index)[None]
        )
    return band_table


def shards(template, science, inverse_variance, intersections):
    tile_rows = template.shape[1]
    tile_cols = template.shape[2]
    visits = lax.axis_size("visit")
    own_visit = lax.axis_index("visit")
    entries = intersections[0, 0]
    own_tile = entries[0]
    row_shift = entries[1]
    col_shift = entries[2]
    tile_list = lax.all_gather(intersections[:, 0, 0], "visit", axis=0, tiled=True)
    relation = own_tile - own_visit
    bare = template[0]
    extended = with_halo(bare, (("visit", 0),), HALO)
    below_list = [extended]
    above_list = [extended]
    for step_size in range(1, REACH + 1):
        below_list.append(from_behind(extended, "visit", step_size))
        above_list.append(from_behind(extended, "visit", -step_size))
    window = jnp.stack(below_list[::-1] + above_list[1:])
    chosen = lax.dynamic_index_in_dim(window, relation + REACH, 0, keepdims=False)
    padded = jnp.pad(chosen, ((0, 0), (HALO, HALO)))
    cutout = lax.dynamic_slice(
        padded,
        (SHIFT + row_shift, SHIFT + col_shift),
        (tile_rows + 2 * KHALF, tile_cols + 2 * KHALF),
    )
    table = factor_table(KHALF)
    block_width = min(128, tile_cols)
    col_table = jnp.asarray(column_bands(table, block_width))
    row_table = jnp.asarray(row_bands(table, tile_rows))
    blocks = jnp.stack(
        [
            cutout[:, index * block_width : index * block_width + block_width + 2 * KHALF]
            for index in range(tile_cols // block_width)
        ]
    )
    across = jnp.einsum("nrc,qcb->qrnb", blocks, col_table, precision=lax.Precision.HIGHEST)
    across = across.reshape(table.shape[0], tile_rows + 2 * KHALF, tile_cols)
    planes = [
        jnp.dot(row_table[pair[0]], across[pair[1]], precision=lax.Precision.HIGHEST)
        for pair in basis_pairs()
    ]
    planes.append(jnp.ones((tile_rows, tile_cols), jnp.float32))
    basis = jnp.stack(planes)
    weight = inverse_variance[0, 0]
    observed = science[0, 0]
    flattened = basis.reshape(NBASIS, tile_rows * tile_cols)
    weighted = flattened * weight.reshape(1, tile_rows * tile_cols)
    normal = jnp.einsum("kn,ln->kl", weighted, flattened, precision=lax.Precision.HIGHEST)
    moments = jnp.einsum(
        "kn,n->k",
        weighted,
        observed.reshape(tile_rows * tile_cols),
        precision=lax.Precision.HIGHEST,
    )
    normal, moments = lax.psum((normal, moments), "patch")
    regular = normal + ridge_weight * jnp.trace(normal) / NBASIS * jnp.eye(
        NBASIS, dtype=jnp.float32
    )
    lower_factor = jnp.linalg.cholesky(regular)
    coefficients = jax.scipy.linalg.cho_solve((lower_factor, True), moments)
    model = jnp.einsum("k,kab->ab", coefficients, basis, precision=lax.Precision.HIGHEST)
    difference = (observed - model) * jnp.sqrt(weight)
    placed = lax.dynamic_slice(
        jnp.pad(difference, SHIFT), (SHIFT - row_shift, SHIFT - col_shift), (tile_rows, tile_cols)
    )
    total = jnp.where(own_tile == own_visit, placed, 0.0)
    for step_size in range(1, REACH + 1):
        from_below = from_behind(placed, "visit", step_size)
        from_above = from_behind(placed, "visit", -step_size)
        low_source = jnp.clip(own_visit - step_size, 0, visits - 1)
        high_source = jnp.clip(own_visit + step_size, 0, visits - 1)
        total = total + jnp.where(tile_list[low_source] == own_visit, from_below, 0.0)
        total = total + jnp.where(tile_list[high_source] == own_visit, from_above, 0.0)
    counted = jnp.sum((tile_list == own_visit).astype(jnp.int32))
    coadd = total / jnp.maximum(counted, 1).astype(jnp.float32)
    return (difference[None, None], coadd[None])


def solution(mesh):
    in_specs = (
        P("patch", "visit", None),
        P("visit", "patch", None, None),
        P("visit", "patch", None, None),
        P("visit", "patch", None),
    )
    out_specs = (P("visit", "patch", None, None), P("patch", "visit", None))
    return jax.shard_map(shards, mesh=mesh, in_specs=in_specs, out_specs=out_specs, check_vma=False)
```

profile of v0, /device:TPU:118, one launch (start us, length us, event | category | flops | bytes accessed | tf_op | source)
XLA Modules:
  0.0 275.4 jit_solution(14040916121996973324)
XLA Ops:
  1.4 3.2 %collective-permute-start = (f32[16,512]{1,0:T(8,128)S(1)}, f32[16,512]{1,0:T(8,128)S(1)}, u32[]{:S(2)}, u32[]{:S(2)}) collective-permute-start(f32[16,512]{1,0:T(8,128)S(1)} %get-tuple-element.19), channel_id=1, source_target_pairs={{0,4},{4,8},{8,12},{12,16},{16,20},{20,24},{24,28},{28,32},{32,36}... | collective-permute-start | bytes 98312 | tf_op jit(solution)/shard_map/ppermute | solution.py:26
  7.3 4.8 %collective-permute-done.1 = f32[16,512]{1,0:T(8,128)S(1)} collective-permute-done((f32[16,512]{1,0:T(8,128)S(1)}, f32[16,512]{1,0:T(8,128)S(1)}, u32[]{:S(2)}, u32[]{:S(2)}) %collective-permute-start.1) | collective-permute-done | bytes 32800 | tf_op jit(solution)/shard_map/ppermute | solution.py:29
  13.0 5.4 %collective-permute-start.2 = (f32[96,512]{1,0:T(8,128)S(1)}, f32[96,512]{1,0:T(8,128)S(1)}, u32[]{:S(2)}, u32[]{:S(2)}) collective-permute-start(f32[96,512]{1,0:T(8,128)S(1)} %pad_maximum_fusion), channel_id=1, source_target_pairs={{0,24},{4,28},{8,32},{12,36},{16,40},{20,44},{24,48},{28,52},{32,5... | collective-permute-start | bytes 589832 | tf_op jit(solution)/shard_map/ppermute | solution.py:37
  28.2 5.8 %collective-permute-start.3 = (f32[96,512]{1,0:T(8,128)S(1)}, f32[96,512]{1,0:T(8,128)S(1)}, u32[]{:S(2)}, u32[]{:S(2)}) collective-permute-start(f32[96,512]{1,0:T(8,128)S(1)} %pad_maximum_fusion), channel_id=1, source_target_pairs={{0,20},{4,24},{8,28},{12,32},{16,36},{20,40},{24,44},{28,48},{32,5... | collective-permute-start | bytes 589832 | tf_op jit(solution)/shard_map/ppermute | solution.py:37
  34.0 5.6 %collective-permute-start.4 = (f32[96,512]{1,0:T(8,128)S(1)}, f32[96,512]{1,0:T(8,128)S(1)}, u32[]{:S(2)}, u32[]{:S(2)}) collective-permute-start(f32[96,512]{1,0:T(8,128)S(1)} %pad_maximum_fusion), channel_id=1, source_target_pairs={{0,16},{4,20},{8,24},{12,28},{16,32},{20,36},{24,40},{28,44},{32,4... | collective-permute-start | bytes 589832 | tf_op jit(solution)/shard_map/ppermute | solution.py:37
  39.6 4.0 %collective-permute-start.5 = (f32[96,512]{1,0:T(8,128)S(1)}, f32[96,512]{1,0:T(8,128)S(1)}, u32[]{:S(2)}, u32[]{:S(2)}) collective-permute-start(f32[96,512]{1,0:T(8,128)S(1)} %pad_maximum_fusion), channel_id=1, source_target_pairs={{0,12},{4,16},{8,20},{12,24},{16,28},{20,32},{24,36},{28,40},{32,4... | collective-permute-start | bytes 589832 | tf_op jit(solution)/shard_map/ppermute | solution.py:37
  43.7 6.5 %collective-permute-start.6 = (f32[96,512]{1,0:T(8,128)S(1)}, f32[96,512]{1,0:T(8,128)S(1)}, u32[]{:S(2)}, u32[]{:S(2)}) collective-permute-start(f32[96,512]{1,0:T(8,128)S(1)} %pad_maximum_fusion), channel_id=1, source_target_pairs={{0,8},{4,12},{8,16},{12,20},{16,24},{20,28},{24,32},{28,36},{32,40... | collective-permute-start | bytes 589832 | tf_op jit(solution)/shard_map/ppermute | solution.py:37
  50.1 5.2 %collective-permute-start.7 = (f32[96,512]{1,0:T(8,128)S(1)}, f32[96,512]{1,0:T(8,128)S(1)}, u32[]{:S(2)}, u32[]{:S(2)}) collective-permute-start(f32[96,512]{1,0:T(8,128)S(1)} %pad_maximum_fusion), channel_id=1, source_target_pairs={{0,4},{4,8},{8,12},{12,16},{16,20},{20,24},{24,28},{28,32},{32,36}... | collective-permute-start | bytes 589832 | tf_op jit(solution)/shard_map/ppermute | solution.py:37
  57.3 5.7 %collective-permute-start.9 = (f32[96,512]{1,0:T(8,128)S(1)}, f32[96,512]{1,0:T(8,128)S(1)}, u32[]{:S(2)}, u32[]{:S(2)}) collective-permute-start(f32[96,512]{1,0:T(8,128)S(1)} %pad_maximum_fusion), channel_id=1, source_target_pairs={{8,0},{12,4},{16,8},{20,12},{24,16},{28,20},{32,24},{36,28},{40,32... | collective-permute-start | bytes 589832 | tf_op jit(solution)/shard_map/ppermute | solution.py:37
  67.8 7.0 %collective-permute-start.12 = (f32[96,512]{1,0:T(8,128)S(1)}, f32[96,512]{1,0:T(8,128)S(1)}, u32[]{:S(2)}, u32[]{:S(2)}) collective-permute-start(f32[96,512]{1,0:T(8,128)S(1)} %pad_maximum_fusion), channel_id=1, source_target_pairs={{20,0},{24,4},{28,8},{32,12},{36,16},{40,20},{44,24},{48,28},{52,3... | collective-permute-start | bytes 589832 | tf_op jit(solution)/shard_map/ppermute | solution.py:37
  75.8 4.0 %collective-permute-start.13 = (f32[96,512]{1,0:T(8,128)S(1)}, f32[96,512]{1,0:T(8,128)S(1)}, u32[]{:S(2)}, u32[]{:S(2)}) collective-permute-start(f32[96,512]{1,0:T(8,128)S(1)} %pad_maximum_fusion), channel_id=1, source_target_pairs={{24,0},{28,4},{32,8},{36,12},{40,16},{44,20},{48,24},{52,28},{56,3... | collective-permute-start | bytes 589832 | tf_op jit(solution)/shard_map/ppermute | solution.py:37
  80.4 6.5 %collective-permute-done.13 = f32[96,512]{1,0:T(8,128)S(1)} collective-permute-done((f32[96,512]{1,0:T(8,128)S(1)}, f32[96,512]{1,0:T(8,128)S(1)}, u32[]{:S(2)}, u32[]{:S(2)}) %collective-permute-start.13) | collective-permute-done | bytes 196640 | tf_op jit(solution)/shard_map/ppermute | solution.py:37
  121.0 12.1 %stack.243 = f32[28,32768]{1,0:T(8,128)} concatenate(f32[1,32768]{1,0:T(1,128)} %bitcast.433, f32[1,32768]{1,0:T(1,128)S(1)} %bitcast.432, f32[1,32768]{1,0:T(1,128)S(1)} %bitcast.431, f32[1,32768]{1,0:T(1,128)S(1)} %bitcast.430, f32[1,32768]{1,0:T(1,128)S(1)} %bitcast.429, f32[1,32768]{1,0:T(1,128)S(1)} %bitcast.428, f32[1,32768]{1,0:T(1,128)S(1)} %bitcast.427, ...), dimensions={0} | concatenate | bytes 7340032 | tf_op jit(solution)/shard_map/stack | solution.py:130
  133.0 7.2 %fusion.2 = f32[28,28]{1,0:T(8,128)S(1)} fusion(f32[28,32768]{1,0:T(8,128)} %stack.243, f32[32768]{0:T(1024)S(1)} %bitcast.386), kind=kOutput, calls=%fused_computation.2 | convolution fusion | flops 309198848 | bytes 3804224 | tf_op jit(solution)/shard_map/kn,ln->kl/dot_general | solution.py:135
  140.3 3.3 %fusion.8 = f32[28]{0:T(128)S(1)} fusion(f32[32768,1]{0,1:T(1,128)S(1)} %bitcast.434, f32[28,32768]{1,0:T(8,128)S(1)} %copy-done, f32[32768]{0:T(1024)S(1)} %bitcast.387), kind=kOutput, calls=%fused_computation.9 | convolution fusion | flops 11927552 | bytes 3932272 | tf_op jit(solution)/shard_map/kn,n->k/dot_general | solution.py:136
  143.7 10.5 %all-reduce.3 = (f32[28,28]{1,0:T(8,128)S(1)}, f32[28]{0:T(128)S(1)}) all-reduce(f32[28,28]{1,0:T(8,128)S(1)} %fusion.2, f32[28]{0:T(128)S(1)} %fusion.8), channel_id=1, replica_groups=mesh['visit'=128,'patch'=4] {'patch'}, use_global_device_ids=true, to_apply=%region_0.1 | all-reduce | flops 812 | bytes 6496 | tf_op jit(solution)/shard_map/psum | solution.py:142
  162.5 6.1 %fusion.4 = f32[1,64,512]{2,0,1:T(1,128)S(1)} fusion(f32[28,1,1]{0,1,2:T(1,128)S(1)} %convolution_bitcast_fusion.1, f32[28,64,512]{2,1,0:T(8,128)} %constant_dynamic-update-slice_fusion), kind=kOutput, calls=%fused_computation.4 | convolution fusion | flops 11010048 | bytes 3801200 | tf_op jit(solution)/shard_map/k,kab->ab/dot_general | solution.py:148
  171.1 4.4 %collective-permute-start.15 = (f32[64,512]{1,0:T(8,128)S(1)}, f32[64,512]{1,0:T(8,128)S(1)}, u32[]{:S(2)}, u32[]{:S(2)}) collective-permute-start(f32[64,512]{1,0:T(8,128)S(1)} %pad_dynamic-slice_fusion.4), channel_id=1, source_target_pairs={{4,0},{8,4},{12,8},{16,12},{20,16},{24,20},{28,24},{32,28},{36,32}... | collective-permute-start | bytes 393224 | tf_op jit(solution)/shard_map/ppermute | solution.py:37
  175.5 10.5 %collective-permute-start.16 = (f32[64,512]{1,0:T(8,128)S(1)}, f32[64,512]{1,0:T(8,128)S(1)}, u32[]{:S(2)}, u32[]{:S(2)}) collective-permute-start(f32[64,512]{1,0:T(8,128)S(1)} %pad_dynamic-slice_fusion.4), channel_id=1, source_target_pairs={{0,8},{4,12},{8,16},{12,20},{16,24},{20,28},{24,32},{28,36},{32,40... | collective-permute-start | bytes 393224 | tf_op jit(solution)/shard_map/ppermute | solution.py:37
  188.0 5.4 %collective-permute-start.18 = (f32[64,512]{1,0:T(8,128)S(1)}, f32[64,512]{1,0:T(8,128)S(1)}, u32[]{:S(2)}, u32[]{:S(2)}) collective-permute-start(f32[64,512]{1,0:T(8,128)S(1)} %pad_dynamic-slice_fusion.4), channel_id=1, source_target_pairs={{0,12},{4,16},{8,20},{12,24},{16,28},{20,32},{24,36},{28,40},{32,4... | collective-permute-start | bytes 393224 | tf_op jit(solution)/shard_map/ppermute | solution.py:37
  196.2 4.6 %collective-permute-start.20 = (f32[64,512]{1,0:T(8,128)S(1)}, f32[64,512]{1,0:T(8,128)S(1)}, u32[]{:S(2)}, u32[]{:S(2)}) collective-permute-start(f32[64,512]{1,0:T(8,128)S(1)} %pad_dynamic-slice_fusion.4), channel_id=1, source_target_pairs={{0,16},{4,20},{8,24},{12,28},{16,32},{20,36},{24,40},{28,44},{32,4... | collective-permute-start | bytes 393224 | tf_op jit(solution)/shard_map/ppermute | solution.py:37
  203.6 8.8 %collective-permute-start.22 = (f32[64,512]{1,0:T(8,128)S(1)}, f32[64,512]{1,0:T(8,128)S(1)}, u32[]{:S(2)}, u32[]{:S(2)}) collective-permute-start(f32[64,512]{1,0:T(8,128)S(1)} %pad_dynamic-slice_fusion.4), channel_id=1, source_target_pairs={{0,20},{4,24},{8,28},{12,32},{16,36},{20,40},{24,44},{28,48},{32,5... | collective-permute-start | bytes 393224 | tf_op jit(solution)/shard_map/ppermute | solution.py:37
  214.4 7.5 %collective-permute-start.24 = (f32[64,512]{1,0:T(8,128)S(1)}, f32[64,512]{1,0:T(8,128)S(1)}, u32[]{:S(2)}, u32[]{:S(2)}) collective-permute-start(f32[64,512]{1,0:T(8,128)S(1)} %pad_dynamic-slice_fusion.4), channel_id=1, source_target_pairs={{0,24},{4,28},{8,32},{12,36},{16,40},{20,44},{24,48},{28,52},{32,5... | collective-permute-start | bytes 393224 | tf_op jit(solution)/shard_map/ppermute | solution.py:37
  227.5 37.4 %all-reduce.2 = s32[128]{0:T(128)S(1)} all-reduce(s32[128]{0:T(128)S(1)} %bitcast_dynamic-update-slice_fusion.40), channel_id=2, replica_groups=mesh['visit'=128,'patch'=4] {'visit'}, use_global_device_ids=true, to_apply=%add.2 | all-reduce | flops 128 | bytes 1024
  (194 shorter events, 76.8 us)
Async XLA Ops:
  13.0 37.2 %collective-permute-start.2 = (f32[96,512]{1,0:T(8,128)S(1)}, f32[96,512]{1,0:T(8,128)S(1)}, u32[]{:S(2)}, u32[]{:S(2)}) collective-permute-start(f32[96,512]{1,0:T(8,128)S(1)} %pad_maximum_fusion), channel_id=1, source_target_pairs={{0,24},{4,28},{8,32},{12,36},{16,40},{20,44},{24,48},{28,52},{32,5... | collective-permute-start | bytes 589832 | tf_op jit(solution)/shard_map/ppermute | solution.py:37
  28.2 27.1 %collective-permute-start.3 = (f32[96,512]{1,0:T(8,128)S(1)}, f32[96,512]{1,0:T(8,128)S(1)}, u32[]{:S(2)}, u32[]{:S(2)}) collective-permute-start(f32[96,512]{1,0:T(8,128)S(1)} %pad_maximum_fusion), channel_id=1, source_target_pairs={{0,20},{4,24},{8,28},{12,32},{16,36},{20,40},{24,44},{28,48},{32,5... | collective-permute-start | bytes 589832 | tf_op jit(solution)/shard_map/ppermute | solution.py:37
  34.0 23.3 %collective-permute-start.4 = (f32[96,512]{1,0:T(8,128)S(1)}, f32[96,512]{1,0:T(8,128)S(1)}, u32[]{:S(2)}, u32[]{:S(2)}) collective-permute-start(f32[96,512]{1,0:T(8,128)S(1)} %pad_maximum_fusion), channel_id=1, source_target_pairs={{0,16},{4,20},{8,24},{12,28},{16,32},{20,36},{24,40},{28,44},{32,4... | collective-permute-start | bytes 589832 | tf_op jit(solution)/shard_map/ppermute | solution.py:37
  39.6 23.5 %collective-permute-start.5 = (f32[96,512]{1,0:T(8,128)S(1)}, f32[96,512]{1,0:T(8,128)S(1)}, u32[]{:S(2)}, u32[]{:S(2)}) collective-permute-start(f32[96,512]{1,0:T(8,128)S(1)} %pad_maximum_fusion), channel_id=1, source_target_pairs={{0,12},{4,16},{8,20},{12,24},{16,28},{20,32},{24,36},{28,40},{32,4... | collective-permute-start | bytes 589832 | tf_op jit(solution)/shard_map/ppermute | solution.py:37
  43.7 21.4 %collective-permute-start.6 = (f32[96,512]{1,0:T(8,128)S(1)}, f32[96,512]{1,0:T(8,128)S(1)}, u32[]{:S(2)}, u32[]{:S(2)}) collective-permute-start(f32[96,512]{1,0:T(8,128)S(1)} %pad_maximum_fusion), channel_id=1, source_target_pairs={{0,8},{4,12},{8,16},{12,20},{16,24},{20,28},{24,32},{28,36},{32,40... | collective-permute-start | bytes 589832 | tf_op jit(solution)/shard_map/ppermute | solution.py:37
  50.1 17.6 %collective-permute-start.7 = (f32[96,512]{1,0:T(8,128)S(1)}, f32[96,512]{1,0:T(8,128)S(1)}, u32[]{:S(2)}, u32[]{:S(2)}) collective-permute-start(f32[96,512]{1,0:T(8,128)S(1)} %pad_maximum_fusion), channel_id=1, source_target_pairs={{0,4},{4,8},{8,12},{12,16},{16,20},{20,24},{24,28},{28,32},{32,36}... | collective-permute-start | bytes 589832 | tf_op jit(solution)/shard_map/ppermute | solution.py:37
  55.4 20.4 %collective-permute-start.8 = (f32[96,512]{1,0:T(8,128)S(1)}, f32[96,512]{1,0:T(8,128)S(1)}, u32[]{:S(2)}, u32[]{:S(2)}) collective-permute-start(f32[96,512]{1,0:T(8,128)S(1)} %pad_maximum_fusion), channel_id=1, source_target_pairs={{4,0},{8,4},{12,8},{16,12},{20,16},{24,20},{28,24},{32,28},{36,32}... | collective-permute-start | bytes 589832 | tf_op jit(solution)/shard_map/ppermute | solution.py:37
  57.3 22.4 %collective-permute-start.9 = (f32[96,512]{1,0:T(8,128)S(1)}, f32[96,512]{1,0:T(8,128)S(1)}, u32[]{:S(2)}, u32[]{:S(2)}) collective-permute-start(f32[96,512]{1,0:T(8,128)S(1)} %pad_maximum_fusion), channel_id=1, source_target_pairs={{8,0},{12,4},{16,8},{20,12},{24,16},{28,20},{32,24},{36,28},{40,32... | collective-permute-start | bytes 589832 | tf_op jit(solution)/shard_map/ppermute | solution.py:37
  63.1 16.7 %collective-permute-start.10 = (f32[96,512]{1,0:T(8,128)S(1)}, f32[96,512]{1,0:T(8,128)S(1)}, u32[]{:S(2)}, u32[]{:S(2)}) collective-permute-start(f32[96,512]{1,0:T(8,128)S(1)} %pad_maximum_fusion), channel_id=1, source_target_pairs={{12,0},{16,4},{20,8},{24,12},{28,16},{32,20},{36,24},{40,28},{44,3... | collective-permute-start | bytes 589832 | tf_op jit(solution)/shard_map/ppermute | solution.py:37
  65.1 14.8 %collective-permute-start.11 = (f32[96,512]{1,0:T(8,128)S(1)}, f32[96,512]{1,0:T(8,128)S(1)}, u32[]{:S(2)}, u32[]{:S(2)}) collective-permute-start(f32[96,512]{1,0:T(8,128)S(1)} %pad_maximum_fusion), channel_id=1, source_target_pairs={{16,0},{20,4},{24,8},{28,12},{32,16},{36,20},{40,24},{44,28},{48,3... | collective-permute-start | bytes 589832 | tf_op jit(solution)/shard_map/ppermute | solution.py:37
  67.8 12.6 %collective-permute-start.12 = (f32[96,512]{1,0:T(8,128)S(1)}, f32[96,512]{1,0:T(8,128)S(1)}, u32[]{:S(2)}, u32[]{:S(2)}) collective-permute-start(f32[96,512]{1,0:T(8,128)S(1)} %pad_maximum_fusion), channel_id=1, source_target_pairs={{20,0},{24,4},{28,8},{32,12},{36,16},{40,20},{44,24},{48,28},{52,3... | collective-permute-start | bytes 589832 | tf_op jit(solution)/shard_map/ppermute | solution.py:37
  75.8 11.2 %collective-permute-start.13 = (f32[96,512]{1,0:T(8,128)S(1)}, f32[96,512]{1,0:T(8,128)S(1)}, u32[]{:S(2)}, u32[]{:S(2)}) collective-permute-start(f32[96,512]{1,0:T(8,128)S(1)} %pad_maximum_fusion), channel_id=1, source_target_pairs={{24,0},{28,4},{32,8},{36,12},{40,16},{44,20},{48,24},{52,28},{56,3... | collective-permute-start | bytes 589832 | tf_op jit(solution)/shard_map/ppermute | solution.py:37
  168.8 24.5 %collective-permute-start.14 = (f32[64,512]{1,0:T(8,128)S(1)}, f32[64,512]{1,0:T(8,128)S(1)}, u32[]{:S(2)}, u32[]{:S(2)}) collective-permute-start(f32[64,512]{1,0:T(8,128)S(1)} %pad_dynamic-slice_fusion.4), channel_id=1, source_target_pairs={{0,4},{4,8},{8,12},{12,16},{16,20},{20,24},{24,28},{28,32},{32,36}... | collective-permute-start | bytes 393224 | tf_op jit(solution)/shard_map/ppermute | solution.py:37
  171.1 25.2 %collective-permute-start.15 = (f32[64,512]{1,0:T(8,128)S(1)}, f32[64,512]{1,0:T(8,128)S(1)}, u32[]{:S(2)}, u32[]{:S(2)}) collective-permute-start(f32[64,512]{1,0:T(8,128)S(1)} %pad_dynamic-slice_fusion.4), channel_id=1, source_target_pairs={{4,0},{8,4},{12,8},{16,12},{20,16},{24,20},{28,24},{32,28},{36,32}... | collective-permute-start | bytes 393224 | tf_op jit(solution)/shard_map/ppermute | solution.py:37
  175.5 25.3 %collective-permute-start.16 = (f32[64,512]{1,0:T(8,128)S(1)}, f32[64,512]{1,0:T(8,128)S(1)}, u32[]{:S(2)}, u32[]{:S(2)}) collective-permute-start(f32[64,512]{1,0:T(8,128)S(1)} %pad_dynamic-slice_fusion.4), channel_id=1, source_target_pairs={{0,8},{4,12},{8,16},{12,20},{16,24},{20,28},{24,32},{28,36},{32,40... | collective-permute-start | bytes 393224 | tf_op jit(solution)/shard_map/ppermute | solution.py:37
  186.0 17.6 %collective-permute-start.17 = (f32[64,512]{1,0:T(8,128)S(1)}, f32[64,512]{1,0:T(8,128)S(1)}, u32[]{:S(2)}, u32[]{:S(2)}) collective-permute-start(f32[64,512]{1,0:T(8,128)S(1)} %pad_dynamic-slice_fusion.4), channel_id=1, source_target_pairs={{8,0},{12,4},{16,8},{20,12},{24,16},{28,20},{32,24},{36,28},{40,32... | collective-permute-start | bytes 393224 | tf_op jit(solution)/shard_map/ppermute | solution.py:37
  188.0 24.5 %collective-permute-start.18 = (f32[64,512]{1,0:T(8,128)S(1)}, f32[64,512]{1,0:T(8,128)S(1)}, u32[]{:S(2)}, u32[]{:S(2)}) collective-permute-start(f32[64,512]{1,0:T(8,128)S(1)} %pad_dynamic-slice_fusion.4), channel_id=1, source_target_pairs={{0,12},{4,16},{8,20},{12,24},{16,28},{20,32},{24,36},{28,40},{32,4... | collective-permute-start | bytes 393224 | tf_op jit(solution)/shard_map/ppermute | solution.py:37
  193.3 21.0 %collective-permute-start.19 = (f32[64,512]{1,0:T(8,128)S(1)}, f32[64,512]{1,0:T(8,128)S(1)}, u32[]{:S(2)}, u32[]{:S(2)}) collective-permute-start(f32[64,512]{1,0:T(8,128)S(1)} %pad_dynamic-slice_fusion.4), channel_id=1, source_target_pairs={{12,0},{16,4},{20,8},{24,12},{28,16},{32,20},{36,24},{40,28},{44,3... | collective-permute-start | bytes 393224 | tf_op jit(solution)/shard_map/ppermute | solution.py:37
  196.2 25.7 %collective-permute-start.20 = (f32[64,512]{1,0:T(8,128)S(1)}, f32[64,512]{1,0:T(8,128)S(1)}, u32[]{:S(2)}, u32[]{:S(2)}) collective-permute-start(f32[64,512]{1,0:T(8,128)S(1)} %pad_dynamic-slice_fusion.4), channel_id=1, source_target_pairs={{0,16},{4,20},{8,24},{12,28},{16,32},{20,36},{24,40},{28,44},{32,4... | collective-permute-start | bytes 393224 | tf_op jit(solution)/shard_map/ppermute | solution.py:37
  200.8 73.6 %collective-permute-start.21 = (f32[64,512]{1,0:T(8,128)S(1)}, f32[64,512]{1,0:T(8,128)S(1)}, u32[]{:S(2)}, u32[]{:S(2)}) collective-permute-start(f32[64,512]{1,0:T(8,128)S(1)} %pad_dynamic-slice_fusion.4), channel_id=1, source_target_pairs={{16,0},{20,4},{24,8},{28,12},{32,16},{36,20},{40,24},{44,28},{48,3... | collective-permute-start | bytes 393224 | tf_op jit(solution)/shard_map/ppermute | solution.py:37
  203.6 70.8 %collective-permute-start.22 = (f32[64,512]{1,0:T(8,128)S(1)}, f32[64,512]{1,0:T(8,128)S(1)}, u32[]{:S(2)}, u32[]{:S(2)}) collective-permute-start(f32[64,512]{1,0:T(8,128)S(1)} %pad_dynamic-slice_fusion.4), channel_id=1, source_target_pairs={{0,20},{4,24},{8,28},{12,32},{16,36},{20,40},{24,44},{28,48},{32,5... | collective-permute-start | bytes 393224 | tf_op jit(solution)/shard_map/ppermute | solution.py:37
  212.4 62.0 %collective-permute-start.23 = (f32[64,512]{1,0:T(8,128)S(1)}, f32[64,512]{1,0:T(8,128)S(1)}, u32[]{:S(2)}, u32[]{:S(2)}) collective-permute-start(f32[64,512]{1,0:T(8,128)S(1)} %pad_dynamic-slice_fusion.4), channel_id=1, source_target_pairs={{20,0},{24,4},{28,8},{32,12},{36,16},{40,20},{44,24},{48,28},{52,3... | collective-permute-start | bytes 393224 | tf_op jit(solution)/shard_map/ppermute | solution.py:37
  214.4 60.1 %collective-permute-start.24 = (f32[64,512]{1,0:T(8,128)S(1)}, f32[64,512]{1,0:T(8,128)S(1)}, u32[]{:S(2)}, u32[]{:S(2)}) collective-permute-start(f32[64,512]{1,0:T(8,128)S(1)} %pad_dynamic-slice_fusion.4), channel_id=1, source_target_pairs={{0,24},{4,28},{8,32},{12,36},{16,40},{20,44},{24,48},{28,52},{32,5... | collective-permute-start | bytes 393224 | tf_op jit(solution)/shard_map/ppermute | solution.py:37
  221.9 52.5 %collective-permute-start.25 = (f32[64,512]{1,0:T(8,128)S(1)}, f32[64,512]{1,0:T(8,128)S(1)}, u32[]{:S(2)}, u32[]{:S(2)}) collective-permute-start(f32[64,512]{1,0:T(8,128)S(1)} %pad_dynamic-slice_fusion.4), channel_id=1, source_target_pairs={{24,0},{28,4},{32,8},{36,12},{40,16},{44,20},{48,24},{52,28},{56,3... | collective-permute-start | bytes 393224 | tf_op jit(solution)/shard_map/ppermute | solution.py:37
  (19 other events, 344.1 us)
where the time goes:
time: 277 us; the launch traced here: 275 us
  starting transfers between devices  117 us (42%)
  blocking collectives  47.8 us (17%)
  matrix products  43.5 us (16%)
  local copies, waits for them, and re-layouts  28.2 us (10%)
  between operations  17.2 us (6%)
  waiting for transfers between devices  11.9 us (4%)
  other arithmetic  10.1 us (4%)
    ppermute x24, starting transfers between devices, from_behind(): return lax.ppermute(shard, axis, pairs)  111 us
    unnamed x1, blocking collectives  37.4 us
    dot_general x27, matrix products, shards(): jnp.dot(row_table[pair[0]], across[pair[1]], precision=lax.Precision.HIGH...  24.5 us
    another operation x3, local copies, waits for them, and re-layouts, shards(): basis = jnp.stack(planes)  13.5 us
    unnamed x104, local copies, waits for them, and re-layouts  11.2 us
    psum x1, blocking collectives, shards(): normal, moments = lax.psum((normal, moments), 'patch')  10.5 us
    dot_general x1, matrix products, shards(): jnp.einsum('kn,ln->kl', weighted, flattened, precision=lax.Precision.HIGH...  7.24 us
    ppermute x24, waiting for transfers between devices, from_behind(): return lax.ppermute(shard, axis, pairs)  7.11 us
  transfers between devices with their start and end apart: 26, of which 3 were waited for; matrix products, arithmetic and copies ran while one was open for 3% of the time, Pallas kernels for 0%

commit v1 on v0

v1 whole, which is shorter than its diff:
```python
import functools
import math

import jax
import jax.numpy as jnp
import ml_dtypes
import numpy as np
from jax import lax
from jax.experimental import pallas as pl
from jax.experimental.pallas import tpu as pltpu
from jax.sharding import PartitionSpec as P

KHALF = 10
SHIFT = 6
REACH = 6
NBASIS = 28
ROWS = 64
COLS = 512
PLANE = 8
SPAN = 96
SLOTS = 32
BLOCK = 128
BLOCKS = COLS // BLOCK
USED = NBASIS + 1
HALF = 32
DEPTH = 64

SIGMAS = (1.0, 2.0, 4.0)
DEGREES = (4, 2, 2)
RIDGE = 0.01
LIMIT = 32 * 1024 * 1024

SMEM = pl.BlockSpec(memory_space=pltpu.SMEM)
VMEM = pl.BlockSpec(memory_space=pltpu.VMEM)
ANY = pl.BlockSpec(memory_space=pl.ANY)


def factor_table():
    listed = []
    for width_sigma, degree in zip(SIGMAS, DEGREES):
        for exponent in range(degree + 1):
            values = [
                math.exp(-(offset * offset) / (2.0 * width_sigma * width_sigma))
                * (offset / KHALF) ** exponent
                for offset in range(-KHALF, KHALF + 1)
            ]
            scale_norm = math.sqrt(sum((entry * entry for entry in values)))
            listed.append([entry / scale_norm for entry in values])
    return np.array(listed, dtype=np.float32)


def row_factors_by_column_factor():
    groups = []
    first = 0
    for degree in DEGREES:
        for power_col in range(degree + 1):
            groups.append([first + power_row for power_row in range(degree + 1 - power_col)])
        first += degree + 1
    return groups


GROUPS = row_factors_by_column_factor()
NFACTORS = len(GROUPS)


def split_constant(values):
    high = values.astype(ml_dtypes.bfloat16)
    low = (values - high.astype(np.float32)).astype(ml_dtypes.bfloat16)
    return high, low


def column_tables():
    table = factor_table()
    distance = np.arange(2 * BLOCK)[:, None] - np.arange(BLOCK)[None, :]
    bands = np.zeros((2 * BLOCK, NFACTORS, BLOCK), np.float32)
    for offset in range(2 * KHALF + 1):
        bands += table[None, :, offset, None] * (distance == offset)[:, None, :]
    return split_constant(bands.reshape(2 * BLOCK, NFACTORS * BLOCK))


def row_tables():
    table = factor_table()
    distance = np.arange(DEPTH)[None, :] - np.arange(HALF)[:, None]
    planes = [index for group in GROUPS for index in group]
    bands = np.zeros((len(planes), HALF, DEPTH), np.float32)
    for offset in range(2 * KHALF + 1):
        bands += table[planes, offset][:, None, None] * (distance == offset)[None]
    high, low = split_constant(bands.reshape(len(planes) * HALF, DEPTH))
    return np.concatenate([high, high, low], axis=1)


def split(values):
    high = values.astype(jnp.bfloat16)
    low = (values - high.astype(jnp.float32)).astype(jnp.bfloat16)
    return high, low


def put_plane(planes, slot, row, values):
    for block in range(BLOCKS):
        at = (block * SLOTS + slot) * ROWS + row
        planes[at : at + values.shape[0], :] = values[:, block * BLOCK : (block + 1) * BLOCK]


def serve_kernel(window, own, below, above, piece_own, piece_up, piece_down):
    base = (lax.axis_index("visit") // PLANE) * PLANE
    for entries, piece in ((own, piece_own), (below, piece_down), (above, piece_up)):
        start = (entries[0, 0] - base) * ROWS + entries[0, 1] - KHALF
        first = lax.shift_right_arithmetic(start, 3)
        for part in range(SPAN // 8):
            index = first + part
            inside = jnp.logical_and(index >= 0, index < PLANE * ROWS // 8)
            source = pl.multiple_of(jnp.clip(index, 0, PLANE * ROWS // 8 - 1) * 8, 8)
            rows = window[pl.ds(source, 8), :]
            piece[8 * part : 8 * part + 8, :] = jnp.where(inside, rows, 0.0)


def serve(window, own, below, above):
    shape = jax.ShapeDtypeStruct((SPAN, COLS), jnp.float32)
    return pl.pallas_call(
        serve_kernel,
        out_shape=(shape, shape, shape),
        in_specs=[VMEM, SMEM, SMEM, SMEM],
        out_specs=(VMEM, VMEM, VMEM),
        compiler_params=pltpu.CompilerParams(vmem_limit_bytes=LIMIT),
        name="serve",
    )(window, own, below, above)


def basis_kernel(
    piece_a, piece_b, piece_c, science, weight, col_high, col_low, row_table, entries,
    planes_out, gram_out,
    high_rows, low_rows, planes, sems,
):
    remainder = lax.bitwise_and(entries[0, 1] + SHIFT, 7)
    rows = piece_a[...] + piece_b[...] + piece_c[...]
    rows = pltpu.roll(rows, lax.rem(SPAN - remainder, SPAN), axis=0)
    padded = jnp.concatenate([rows, jnp.zeros((SPAN, BLOCK), jnp.float32)], axis=1)
    cutout = pltpu.roll(padded, KHALF - entries[0, 2], axis=1)
    cut_high, cut_low = split(cutout)
    for block in range(COLS // BLOCK):
        cols = slice(block * BLOCK, (block + 2) * BLOCK)
        both = jnp.concatenate([cut_high[:, cols], cut_low[:, cols]], axis=0)
        main = jnp.dot(both, col_high[...], preferred_element_type=jnp.float32)
        rest = jnp.dot(cut_high[:, cols], col_low[...], preferred_element_type=jnp.float32)
        across = main[:SPAN] + main[SPAN:] + rest
        across_high, across_low = split(across)
        for factor in range(NFACTORS):
            take = slice(factor * BLOCK, (factor + 1) * BLOCK)
            put = slice(block * BLOCK, (block + 1) * BLOCK)
            high_rows[factor, :, put] = across_high[:, take]
            low_rows[factor, :, put] = across_low[:, take]
    root = jnp.sqrt(weight[...])
    first = 0
    for factor, group in enumerate(GROUPS):
        table = row_table[first * HALF : (first + len(group)) * HALF, :]
        for half in range(ROWS // HALF):
            take = slice(half * HALF, half * HALF + DEPTH)
            high = high_rows[factor, take, :]
            stacked = jnp.concatenate([high, low_rows[factor, take, :], high], axis=0)
            out = jnp.dot(table, stacked, preferred_element_type=jnp.float32)
            for member in range(len(group)):
                scaled = (
                    out[member * HALF : (member + 1) * HALF] * root[half * HALF : (half + 1) * HALF]
                )
                put_plane(planes, first + member, half * HALF, scaled)
        first += len(group)
    put_plane(planes, NBASIS - 1, 0, root)
    put_plane(planes, NBASIS, 0, root * science[...])
    for slot in range(USED, SLOTS):
        put_plane(planes, slot, 0, jnp.zeros((ROWS, COLS), jnp.float32))
    copies = [
        pltpu.make_async_copy(
            planes.at[pl.ds(block * SLOTS * ROWS, USED * ROWS), :],
            planes_out.at[block],
            sems.at[block],
        )
        for block in range(BLOCKS)
    ]
    for copy in copies:
        copy.start()

    def gram_step(chunk, total):
        highs, lows = [], []
        for inner in range(8):
            for block in range(BLOCKS):
                row = block * SLOTS * ROWS + chunk * 8 + inner
                high, low = split(planes[pl.ds(row, SLOTS, stride=ROWS), :])
                highs.append(high)
                lows.append(low)
        high = jnp.concatenate(highs, axis=1)
        low = jnp.concatenate(lows, axis=1)
        both = jnp.concatenate([high, low], axis=0)
        return total + lax.dot_general(
            high, both, (((1,), (1,)), ((), ())), preferred_element_type=jnp.float32
        )

    total = lax.fori_loop(0, ROWS // 8, gram_step, jnp.zeros((SLOTS, 2 * SLOTS), jnp.float32))
    gram_out[...] = jnp.concatenate(
        [total, jnp.zeros((SLOTS, BLOCK - 2 * SLOTS), jnp.float32)], axis=1
    )
    for copy in copies:
        copy.wait()


def basis(pieces, science, weight, entries):
    col_high, col_low = column_tables()
    return pl.pallas_call(
        basis_kernel,
        out_shape=(
            jax.ShapeDtypeStruct((BLOCKS, USED * ROWS, BLOCK), jnp.float32),
            jax.ShapeDtypeStruct((SLOTS, BLOCK), jnp.float32),
        ),
        in_specs=[VMEM] * 8 + [SMEM],
        out_specs=(ANY, VMEM),
        scratch_shapes=[
            pltpu.VMEM((NFACTORS, SPAN, COLS), jnp.bfloat16),
            pltpu.VMEM((NFACTORS, SPAN, COLS), jnp.bfloat16),
            pltpu.VMEM((BLOCKS * SLOTS * ROWS, BLOCK), jnp.float32),
            pltpu.SemaphoreType.DMA((BLOCKS,)),
        ],
        compiler_params=pltpu.CompilerParams(vmem_limit_bytes=LIMIT),
        name="basis",
    )(
        *pieces, science, weight, jnp.asarray(col_high), jnp.asarray(col_low),
        jnp.asarray(row_tables()), entries,
    )


def solve_kernel(grams, planes_in, entries, difference, placed, planes, sem):
    copy = pltpu.make_async_copy(planes_in, planes, sem)
    copy.start()
    total = grams[0] + grams[1] + grams[2] + grams[3]
    cross = total[:, SLOTS : 2 * SLOTS]
    normal = total[:, :SLOTS] + cross + cross.T
    row_id = lax.broadcasted_iota(jnp.int32, (SLOTS, SLOTS), 0)
    col_id = lax.broadcasted_iota(jnp.int32, (SLOTS, SLOTS), 1)
    diagonal = jnp.logical_and(row_id == col_id, row_id < NBASIS)
    trace = jnp.sum(jnp.where(diagonal, normal, 0.0), keepdims=True)
    matrix = normal + jnp.where(diagonal, RIDGE * trace / NBASIS, 0.0)
    for step in range(NBASIS):
        row = matrix[step : step + 1, :]
        inverse = 1.0 / row[:, step : step + 1]
        scaled = row * inverse
        column = jnp.where(row_id[:, :1] == step, 0.0, matrix[:, step : step + 1])
        matrix = jnp.where(row_id == step, scaled, matrix - column * scaled)
    answer = jnp.broadcast_to(matrix[:, NBASIS : NBASIS + 1], (SLOTS, BLOCK))
    copy.wait()
    for block in range(BLOCKS):
        total = planes[block, NBASIS * ROWS : USED * ROWS, :]
        for plane in range(NBASIS):
            factor = jnp.broadcast_to(answer[plane : plane + 1, :], (ROWS, BLOCK))
            total = total - factor * planes[block, plane * ROWS : (plane + 1) * ROWS, :]
        difference[:, block * BLOCK : (block + 1) * BLOCK] = total
    row_move, col_move = entries[0, 1], entries[0, 2]
    moved = pltpu.roll(difference[...], lax.rem(row_move + ROWS, ROWS), axis=0)
    moved = pltpu.roll(moved, lax.rem(col_move + COLS, COLS), axis=1)
    from_row = lax.broadcasted_iota(jnp.int32, (ROWS, COLS), 0) - row_move
    from_col = lax.broadcasted_iota(jnp.int32, (ROWS, COLS), 1) - col_move
    inside = (from_row >= 0) & (from_row < ROWS) & (from_col >= 0) & (from_col < COLS)
    placed[...] = jnp.where(inside, moved, 0.0)


def solve(grams, planes, entries):
    shape = jax.ShapeDtypeStruct((ROWS, COLS), jnp.float32)
    return pl.pallas_call(
        solve_kernel,
        out_shape=(shape, shape),
        in_specs=[VMEM, ANY, SMEM],
        out_specs=(VMEM, VMEM),
        scratch_shapes=[
            pltpu.VMEM((BLOCKS, USED * ROWS, BLOCK), jnp.float32),
            pltpu.SemaphoreType.DMA,
        ],
        compiler_params=pltpu.CompilerParams(vmem_limit_bytes=LIMIT),
        name="solve",
    )(grams, planes, entries)


def gather_kernel(stamp_own, stamp_below, stamp_above, own, below, above, tiles):
    base = (lax.axis_index("visit") // PLANE) * PLANE
    hits = [entries[0, 0] - base for entries in (own, below, above)]
    for tile in range(PLANE):
        total = jnp.zeros((ROWS, COLS), jnp.float32)
        count = jnp.float32(0.0)
        for hit, stamp in zip(hits, (stamp_own, stamp_below, stamp_above)):
            total = total + jnp.where(hit == tile, stamp[...], 0.0)
            count = count + jnp.where(hit == tile, 1.0, 0.0)
        tiles[tile, :ROWS, :] = total
        tiles[tile, ROWS:, :] = jnp.full((8, COLS), count, jnp.float32)


def gather(stamps, own, below, above):
    return pl.pallas_call(
        gather_kernel,
        out_shape=jax.ShapeDtypeStruct((PLANE, ROWS + 8, COLS), jnp.float32),
        in_specs=[VMEM] * 3 + [SMEM] * 3,
        out_specs=VMEM,
        compiler_params=pltpu.CompilerParams(vmem_limit_bytes=LIMIT),
        name="gather",
    )(*stamps, own, below, above)


def mean_kernel(parts, coadd):
    total = parts[0]
    for index in range(1, PLANE):
        total = total + parts[index]
    count = jnp.maximum(total[ROWS : ROWS + 1, :], 1.0)
    coadd[...] = total[:ROWS] / count


def mean(parts):
    return pl.pallas_call(
        mean_kernel,
        out_shape=jax.ShapeDtypeStruct((ROWS, COLS), jnp.float32),
        in_specs=[VMEM],
        out_specs=VMEM,
        compiler_params=pltpu.CompilerParams(vmem_limit_bytes=LIMIT),
        name="mean",
    )(parts)


def shards(template, science, inverse_variance, intersections):
    visits = lax.axis_size("visit")
    groups = [list(range(first, first + PLANE)) for first in range(0, visits, PLANE)]
    upward = [(i, (i + PLANE) % visits) for i in range(visits)]
    downward = [(target, source) for source, target in upward]
    own = intersections[0]
    below = lax.ppermute(own, "visit", upward)
    above = lax.ppermute(own, "visit", downward)
    copies = jnp.broadcast_to(template, (PLANE, ROWS, COLS))
    window = lax.all_to_all(copies, "visit", 0, 0, axis_index_groups=groups)
    piece_own, piece_up, piece_down = serve(
        window.reshape(PLANE * ROWS, COLS), own, below, above
    )
    from_above = lax.ppermute(piece_down, "visit", downward)
    from_below = lax.ppermute(piece_up, "visit", upward)
    planes, gram = basis(
        (piece_own, from_above, from_below), science[0, 0], inverse_variance[0, 0], own
    )
    grams = lax.all_gather(gram, "patch")
    difference, placed = solve(grams, planes, own)
    stamp_below = lax.ppermute(placed, "visit", upward)
    stamp_above = lax.ppermute(placed, "visit", downward)
    tiles = gather((placed, stamp_below, stamp_above), own, below, above)
    parts = lax.all_to_all(tiles, "visit", 0, 0, axis_index_groups=groups)
    return (difference[None, None], mean(parts)[None])


def solution(mesh):
    in_specs = (
        P("patch", "visit", None),
        P("visit", "patch", None, None),
        P("visit", "patch", None, None),
        P("visit", "patch", None),
    )
    out_specs = (P("visit", "patch", None, None), P("patch", "visit", None))
    return jax.shard_map(shards, mesh=mesh, in_specs=in_specs, out_specs=out_specs, check_vma=False)
```

time: 277 us -> 100 us (0.36)
  the two profiles are of different devices: /device:TPU:118 before, /device:TPU:2 now
where the time goes in v1:
time: 100 us; the launch traced here: 99.7 us
  starting transfers between devices  36.4 us (36%)
  blocking collectives  28.4 us (28%)
  waiting for transfers between devices  16.5 us (16%)
  Pallas kernels  15.6 us (16%)
  local copies, waits for them, and re-layouts  2.04 us (2%)
    all_to_all x1, blocking collectives, shards(): parts = lax.all_to_all(tiles, 'visit', 0, 0, axis_index_groups=groups)  23.1 us
    ppermute x1, starting transfers between devices, shards(): above = lax.ppermute(own, 'visit', downward)  11.4 us
    ppermute x1, starting transfers between devices, shards(): from_above = lax.ppermute(piece_down, 'visit', downward)  9.18 us
    pallas_call x1, Pallas kernels, basis(): pl.pallas_call(basis_kernel, out_shape=(jax.ShapeDtypeStruct((BLOCKS, USE...  8.82 us
    all_to_all x1, starting transfers between devices, shards(): window = lax.all_to_all(copies, 'visit', 0, 0, axis_index_groups=groups)  6.18 us
    ppermute x1, waiting for transfers between devices, shards(): from_below = lax.ppermute(piece_up, 'visit', upward)  5.61 us
    all_gather x1, blocking collectives, shards(): grams = lax.all_gather(gram, 'patch')  5.25 us
    ppermute x1, waiting for transfers between devices, shards(): below = lax.ppermute(own, 'visit', upward)  4.71 us
  transfers between devices with their start and end apart: 7, of which 5 were waited for; matrix products, arithmetic and copies ran while one was open for 0% of the time, Pallas kernels for 0%

profile of v1, /device:TPU:2, one launch (start us, length us, event | category | flops | bytes accessed | tf_op | source)
XLA Modules:
  0.0 99.7 jit_solution(13075044473316714530)
XLA Ops:
  0.6 2.0 %broadcast_in_dim.14 = f32[8,64,512]{2,1,0:T(8,128)} broadcast(f32[64,512]{1,0:T(8,128)} %bitcast.18), dimensions={1,2} | broadcast | bytes 1179648 | tf_op jit(solution)/shard_map/broadcast_in_dim | solution.py:330
  2.7 0.0 copy-start.4
  2.7 6.2 %all-to-all-start = ((f32[8,64,512]{2,1,0:T(8,128)}), f32[8,64,512]{2,1,0:T(8,128)S(1)}, u32[]{:S(2)}, u32[]{:S(2)}) async-start(f32[8,64,512]{2,1,0:T(8,128)} %broadcast_in_dim.14), calls=%async_computation | async-start | bytes 2097152 | tf_op jit(solution)/shard_map/all_to_all | solution.py:331
  8.8 0.0 copy-done.5
  8.9 11.4 %collective-permute-start.1 = (s32[1,3]{1,0:T(1,128)S(1)}, s32[1,3]{1,0:T(1,128)S(1)}, u32[]{:S(2)}, u32[]{:S(2)}) collective-permute-start(s32[1,3]{1,0:T(1,128)S(1)} %bitcast.12), channel_id=1, source_target_pairs={{32,0},{36,4},{40,8},{44,12},{48,16},{52,20},{56,24},{60,28},{64,3... | collective-permute-start | bytes 44 | tf_op jit(solution)/shard_map/ppermute | solution.py:329
  20.3 1.9 %collective-permute-start = (s32[1,3]{1,0:T(1,128)S(1)}, s32[1,3]{1,0:T(1,128)S(1)}, u32[]{:S(2)}, u32[]{:S(2)}) collective-permute-start(s32[1,3]{1,0:T(1,128)S(1)} %bitcast.13), channel_id=1, source_target_pairs={{0,32},{4,36},{8,40},{12,44},{16,48},{20,52},{24,56},{28,60},{32,6... | collective-permute-start | bytes 44 | tf_op jit(solution)/shard_map/ppermute | solution.py:328
  22.2 0.0 collective-permute-done.1.above
  22.2 4.7 %collective-permute-done.below = s32[1,3]{1,0:T(1,128)S(1)} collective-permute-done((s32[1,3]{1,0:T(1,128)S(1)}, s32[1,3]{1,0:T(1,128)S(1)}, u32[]{:S(2)}, u32[]{:S(2)}) %collective-permute-start) | collective-permute-done | bytes 44 | tf_op jit(solution)/shard_map/ppermute | solution.py:328
  26.9 0.0 all-to-all-done
  26.9 0.7 serve.1
  27.7 9.2 %collective-permute-start.2 = (f32[96,512]{1,0:T(8,128)S(1)}, f32[96,512]{1,0:T(8,128)S(1)}, u32[]{:S(2)}, u32[]{:S(2)}) collective-permute-start(f32[96,512]{1,0:T(8,128)S(1)} %get-tuple-element.10), channel_id=1, source_target_pairs={{32,0},{36,4},{40,8},{44,12},{48,16},{52,20},{56,24},{60,28},{64,3... | collective-permute-start | bytes 589832 | tf_op jit(solution)/shard_map/ppermute | solution.py:335
  36.9 1.9 %collective-permute-start.3 = (f32[96,512]{1,0:T(8,128)S(1)}, f32[96,512]{1,0:T(8,128)S(1)}, u32[]{:S(2)}, u32[]{:S(2)}) collective-permute-start(f32[96,512]{1,0:T(8,128)S(1)} %get-tuple-element.11), channel_id=1, source_target_pairs={{0,32},{4,36},{8,40},{12,44},{16,48},{20,52},{24,56},{28,60},{32,6... | collective-permute-start | bytes 589832 | tf_op jit(solution)/shard_map/ppermute | solution.py:336
  38.8 1.2 %collective-permute-done.2.piece_b = f32[96,512]{1,0:T(8,128)S(1)} collective-permute-done((f32[96,512]{1,0:T(8,128)S(1)}, f32[96,512]{1,0:T(8,128)S(1)}, u32[]{:S(2)}, u32[]{:S(2)}) %collective-permute-start.2) | collective-permute-done | bytes 196640 | tf_op jit(solution)/shard_map/ppermute | solution.py:335
  40.0 5.6 %collective-permute-done.3.piece_c = f32[96,512]{1,0:T(8,128)S(1)} collective-permute-done((f32[96,512]{1,0:T(8,128)S(1)}, f32[96,512]{1,0:T(8,128)S(1)}, u32[]{:S(2)}, u32[]{:S(2)}) %collective-permute-start.3) | collective-permute-done | bytes 196640 | tf_op jit(solution)/shard_map/ppermute | solution.py:336
  45.7 8.8 %basis.1 = (f32[4,1856,128]{2,1,0:T(8,128)S(1)}, f32[32,128]{1,0:T(8,128)S(1)}) custom-call(f32[96,512]{1,0:T(8,128)S(1)} %get-tuple-element.9.piece_a, f32[96,512]{1,0:T(8,128)S(1)} %collective-permute-done.2.piece_b, f32[96,512]{1,0:T(8,128)S(1)} %collective-permute-done.3.piece_c, f32[64,512]{1,0:T(8,128)S(1)} %bitcast.10, f32[64,512]{1,0:T(8,128)S(1)} %bitcast.11, ...), custom_call_target="tpu_custom_call" | custom-call | tf_op jit(solution)/shard_map/basis/pallas_call | solution.py:207
  54.5 5.2 %all-gather = f32[128,128]{1,0:T(8,128)S(1)} all-gather(f32[32,128]{1,0:T(8,128)S(1)} %get-tuple-element.12), channel_id=2, replica_groups=mesh['visit'=128,'patch'=4] {'patch'}, dimensions={0}, use_global_device_ids=true | all-gather | bytes 81920 | tf_op jit(solution)/shard_map/all_gather | solution.py:340
  59.7 4.6 %solve.1 = (f32[64,512]{1,0:T(8,128)}, f32[64,512]{1,0:T(8,128)S(1)}) custom-call(f32[4,32,128]{2,1,0:T(8,128)S(1)} %bitcast.9, f32[4,1856,128]{2,1,0:T(8,128)S(1)} %get-tuple-element.13.planes_in, s32[1,3]{1,0:T(1,128)S(1)} %bitcast.16), custom_call_target="tpu_custom_call" | custom-call | tf_op jit(solution)/shard_map/solve/pallas_call | solution.py:265
  64.3 1.9 %collective-permute-start.5 = (f32[64,512]{1,0:T(8,128)S(1)}, f32[64,512]{1,0:T(8,128)S(1)}, u32[]{:S(2)}, u32[]{:S(2)}) collective-permute-start(f32[64,512]{1,0:T(8,128)S(1)} %get-tuple-element.15.stamp_own), channel_id=1, source_target_pairs={{32,0},{36,4},{40,8},{44,12},{48,16},{52,20},{56,24},{60,28},{64,3... | collective-permute-start | bytes 393224 | tf_op jit(solution)/shard_map/ppermute | solution.py:343
  66.2 3.9 %collective-permute-start.4 = (f32[64,512]{1,0:T(8,128)S(1)}, f32[64,512]{1,0:T(8,128)S(1)}, u32[]{:S(2)}, u32[]{:S(2)}) collective-permute-start(f32[64,512]{1,0:T(8,128)S(1)} %get-tuple-element.15.stamp_own), channel_id=1, source_target_pairs={{0,32},{4,36},{8,40},{12,44},{16,48},{20,52},{24,56},{28,60},{32,6... | collective-permute-start | bytes 393224 | tf_op jit(solution)/shard_map/ppermute | solution.py:342
  70.2 1.8 %collective-permute-done.5.stamp_above = f32[64,512]{1,0:T(8,128)S(1)} collective-permute-done((f32[64,512]{1,0:T(8,128)S(1)}, f32[64,512]{1,0:T(8,128)S(1)}, u32[]{:S(2)}, u32[]{:S(2)}) %collective-permute-start.5) | collective-permute-done | bytes 131104 | tf_op jit(solution)/shard_map/ppermute | solution.py:343
  71.9 3.1 %collective-permute-done.4.stamp_below = f32[64,512]{1,0:T(8,128)S(1)} collective-permute-done((f32[64,512]{1,0:T(8,128)S(1)}, f32[64,512]{1,0:T(8,128)S(1)}, u32[]{:S(2)}, u32[]{:S(2)}) %collective-permute-start.4) | collective-permute-done | bytes 131104 | tf_op jit(solution)/shard_map/ppermute | solution.py:342
  75.1 0.8 gather.1
  75.8 23.1 %all_to_all.10.parts = f32[8,72,512]{2,1,0:T(8,128)S(1)} all-to-all(f32[8,72,512]{2,1,0:T(8,128)S(1)} %gather.1), channel_id=1, replica_groups={{0,4,8,12,16,20,24,28},{32,36,40,44,48,52,56,60},{64,68,72,76,80,84,88,..., dimensions={0} | all-to-all | bytes 2359296 | tf_op jit(solution)/shard_map/all_to_all | solution.py:345
  99.0 0.7 mean.1
  (10 shorter events, 0.0 us)
Async XLA Ops:
  0.6 8.2 %copy-start.5 = (s32[1,1,3]{2,1,0:T(1,128)S(1)}, s32[1,1,3]{2,1,0:T(1,128)}, u32[]{:S(2)}) copy-start(s32[1,1,3]{2,1,0:T(1,128)} %param.10) | copy-start | bytes 40
  2.7 43.0 %copy-start = (bf16[256,1408]{1,0:T(8,128)(2,1)S(1)}, bf16[256,1408]{1,0:T(8,128)(2,1)}, u32[]{:S(2)}) copy-start(bf16[256,1408]{1,0:T(8,128)(2,1)} %constant.7.clone.col_low) | copy-start | bytes 2162692
  2.7 43.0 %copy-start.1 = (bf16[256,1408]{1,0:T(8,128)(2,1)S(1)}, bf16[256,1408]{1,0:T(8,128)(2,1)}, u32[]{:S(2)}) copy-start(bf16[256,1408]{1,0:T(8,128)(2,1)} %constant.6.clone.col_high) | copy-start | bytes 2162692
  2.7 43.0 %copy-start.2 = (bf16[864,192]{1,0:T(8,128)(2,1)S(1)}, bf16[864,192]{1,0:T(8,128)(2,1)}, u32[]{:S(2)}) copy-start(bf16[864,192]{1,0:T(8,128)(2,1)} %constant.8.clone.row_table) | copy-start | bytes 995332
  2.7 43.0 %copy-start.3 = (f32[1,1,64,512]{3,2,1,0:T(8,128)S(1)}, f32[1,1,64,512]{3,2,1,0:T(8,128)}, u32[]{:S(2)}) copy-start(f32[1,1,64,512]{3,2,1,0:T(8,128)} %param.8) | copy-start | bytes 393220
  2.7 43.0 %copy-start.4 = (f32[1,1,64,512]{3,2,1,0:T(8,128)S(1)}, f32[1,1,64,512]{3,2,1,0:T(8,128)}, u32[]{:S(2)}) copy-start(f32[1,1,64,512]{3,2,1,0:T(8,128)} %param.9) | copy-start | bytes 393220
  2.7 24.2 %all-to-all-start = ((f32[8,64,512]{2,1,0:T(8,128)}), f32[8,64,512]{2,1,0:T(8,128)S(1)}, u32[]{:S(2)}, u32[]{:S(2)}) async-start(f32[8,64,512]{2,1,0:T(8,128)} %broadcast_in_dim.14), calls=%async_computation | async-start | bytes 2097152 | tf_op jit(solution)/shard_map/all_to_all | solution.py:331
  8.9 13.3 %collective-permute-start.1 = (s32[1,3]{1,0:T(1,128)S(1)}, s32[1,3]{1,0:T(1,128)S(1)}, u32[]{:S(2)}, u32[]{:S(2)}) collective-permute-start(s32[1,3]{1,0:T(1,128)S(1)} %bitcast.12), channel_id=1, source_target_pairs={{32,0},{36,4},{40,8},{44,12},{48,16},{52,20},{56,24},{60,28},{64,3... | collective-permute-start | bytes 44 | tf_op jit(solution)/shard_map/ppermute | solution.py:329
  20.3 6.6 %collective-permute-start = (s32[1,3]{1,0:T(1,128)S(1)}, s32[1,3]{1,0:T(1,128)S(1)}, u32[]{:S(2)}, u32[]{:S(2)}) collective-permute-start(s32[1,3]{1,0:T(1,128)S(1)} %bitcast.13), channel_id=1, source_target_pairs={{0,32},{4,36},{8,40},{12,44},{16,48},{20,52},{24,56},{28,60},{32,6... | collective-permute-start | bytes 44 | tf_op jit(solution)/shard_map/ppermute | solution.py:328
  27.7 12.4 %collective-permute-start.2 = (f32[96,512]{1,0:T(8,128)S(1)}, f32[96,512]{1,0:T(8,128)S(1)}, u32[]{:S(2)}, u32[]{:S(2)}) collective-permute-start(f32[96,512]{1,0:T(8,128)S(1)} %get-tuple-element.10), channel_id=1, source_target_pairs={{32,0},{36,4},{40,8},{44,12},{48,16},{52,20},{56,24},{60,28},{64,3... | collective-permute-start | bytes 589832 | tf_op jit(solution)/shard_map/ppermute | solution.py:335
  36.9 8.8 %collective-permute-start.3 = (f32[96,512]{1,0:T(8,128)S(1)}, f32[96,512]{1,0:T(8,128)S(1)}, u32[]{:S(2)}, u32[]{:S(2)}) collective-permute-start(f32[96,512]{1,0:T(8,128)S(1)} %get-tuple-element.11), channel_id=1, source_target_pairs={{0,32},{4,36},{8,40},{12,44},{16,48},{20,52},{24,56},{28,60},{32,6... | collective-permute-start | bytes 589832 | tf_op jit(solution)/shard_map/ppermute | solution.py:336
  64.3 7.6 %collective-permute-start.5 = (f32[64,512]{1,0:T(8,128)S(1)}, f32[64,512]{1,0:T(8,128)S(1)}, u32[]{:S(2)}, u32[]{:S(2)}) collective-permute-start(f32[64,512]{1,0:T(8,128)S(1)} %get-tuple-element.15.stamp_own), channel_id=1, source_target_pairs={{32,0},{36,4},{40,8},{44,12},{48,16},{52,20},{56,24},{60,28},{64,3... | collective-permute-start | bytes 393224 | tf_op jit(solution)/shard_map/ppermute | solution.py:343
  66.2 8.8 %collective-permute-start.4 = (f32[64,512]{1,0:T(8,128)S(1)}, f32[64,512]{1,0:T(8,128)S(1)}, u32[]{:S(2)}, u32[]{:S(2)}) collective-permute-start(f32[64,512]{1,0:T(8,128)S(1)} %get-tuple-element.15.stamp_own), channel_id=1, source_target_pairs={{0,32},{4,36},{8,40},{12,44},{16,48},{20,52},{24,56},{28,60},{32,6... | collective-permute-start | bytes 393224 | tf_op jit(solution)/shard_map/ppermute | solution.py:342

commit v2 on v1

--- a/solution.py
+++ b/solution.py
@@ -21,7 +21,8 @@
 SLOTS = 32
 BLOCK = 128
 BLOCKS = COLS // BLOCK
-USED = NBASIS + 1
+PITCH = 72
+TALL = BLOCKS * ROWS
 HALF = 32
 DEPTH = 64
 
@@ -32,7 +33,6 @@
 
 SMEM = pl.BlockSpec(memory_space=pltpu.SMEM)
 VMEM = pl.BlockSpec(memory_space=pltpu.VMEM)
-ANY = pl.BlockSpec(memory_space=pl.ANY)
 
 
 def factor_table():
@@ -97,8 +97,27 @@
 
 def put_plane(planes, slot, row, values):
     for block in range(BLOCKS):
-        at = (block * SLOTS + slot) * ROWS + row
+        at = (block * SLOTS + slot) * PITCH + row
         planes[at : at + values.shape[0], :] = values[:, block * BLOCK : (block + 1) * BLOCK]
+
+
+def spread_kernel(tile, copies):
+    for copy in range(PLANE):
+        for block in range(BLOCKS):
+            copies[copy, block * ROWS : (block + 1) * ROWS, :] = tile[
+                :, block * BLOCK : (block + 1) * BLOCK
+            ]
+
+
+def spread(tile):
+    return pl.pallas_call(
+        spread_kernel,
+        out_shape=jax.ShapeDtypeStruct((PLANE, TALL, BLOCK), jnp.float32),
+        in_specs=[VMEM],
+        out_specs=VMEM,
+        compiler_params=pltpu.CompilerParams(vmem_limit_bytes=LIMIT),
+        name="spread",
+    )(tile)
 
 
 def serve_kernel(window, own, below, above, piece_own, piece_up, piece_down):
@@ -109,9 +128,14 @@
         for part in range(SPAN // 8):
             index = first + part
             inside = jnp.logical_and(index >= 0, index < PLANE * ROWS // 8)
-            source = pl.multiple_of(jnp.clip(index, 0, PLANE * ROWS // 8 - 1) * 8, 8)
-            rows = window[pl.ds(source, 8), :]
-            piece[8 * part : 8 * part + 8, :] = jnp.where(inside, rows, 0.0)
+            index = jnp.clip(index, 0, PLANE * ROWS // 8 - 1)
+            tile = lax.shift_right_logical(index, 3)
+            row = pl.multiple_of(lax.bitwise_and(index, 7) * 8, 8)
+            for block in range(BLOCKS):
+                rows = window[tile, pl.ds(block * ROWS + row, 8), :]
+                piece[8 * part : 8 * part + 8, block * BLOCK : (block + 1) * BLOCK] = jnp.where(
+                    inside, rows, 0.0
+                )
 
 
 def serve(window, own, below, above):
@@ -128,8 +152,8 @@
 
 def basis_kernel(
     piece_a, piece_b, piece_c, science, weight, col_high, col_low, row_table, entries,
-    planes_out, gram_out,
-    high_rows, low_rows, planes, sems,
+    planes, gram_out,
+    high_rows, low_rows,
 ):
     remainder = lax.bitwise_and(entries[0, 1] + SHIFT, 7)
     rows = piece_a[...] + piece_b[...] + piece_c[...]
@@ -166,25 +190,14 @@
         first += len(group)
     put_plane(planes, NBASIS - 1, 0, root)
     put_plane(planes, NBASIS, 0, root * science[...])
-    for slot in range(USED, SLOTS):
+    for slot in range(NBASIS + 1, SLOTS):
         put_plane(planes, slot, 0, jnp.zeros((ROWS, COLS), jnp.float32))
-    copies = [
-        pltpu.make_async_copy(
-            planes.at[pl.ds(block * SLOTS * ROWS, USED * ROWS), :],
-            planes_out.at[block],
-            sems.at[block],
-        )
-        for block in range(BLOCKS)
-    ]
-    for copy in copies:
-        copy.start()
-
     def gram_step(chunk, total):
         highs, lows = [], []
         for inner in range(8):
             for block in range(BLOCKS):
-                row = block * SLOTS * ROWS + chunk * 8 + inner
-                high, low = split(planes[pl.ds(row, SLOTS, stride=ROWS), :])
+                row = block * SLOTS * PITCH + chunk * 8 + inner
+                high, low = split(planes[pl.ds(row, SLOTS, stride=PITCH), :])
                 highs.append(high)
                 lows.append(low)
         high = jnp.concatenate(highs, axis=1)
@@ -198,8 +211,6 @@
     gram_out[...] = jnp.concatenate(
         [total, jnp.zeros((SLOTS, BLOCK - 2 * SLOTS), jnp.float32)], axis=1
     )
-    for copy in copies:
-        copy.wait()
 
 
 def basis(pieces, science, weight, entries):
@@ -207,16 +218,14 @@
     return pl.pallas_call(
         basis_kernel,
         out_shape=(
-            jax.ShapeDtypeStruct((BLOCKS, USED * ROWS, BLOCK), jnp.float32),
+            jax.ShapeDtypeStruct((BLOCKS * SLOTS * PITCH, BLOCK), jnp.float32),
             jax.ShapeDtypeStruct((SLOTS, BLOCK), jnp.float32),
         ),
         in_specs=[VMEM] * 8 + [SMEM],
-        out_specs=(ANY, VMEM),
+        out_specs=(VMEM, VMEM),
         scratch_shapes=[
             pltpu.VMEM((NFACTORS, SPAN, COLS), jnp.bfloat16),
             pltpu.VMEM((NFACTORS, SPAN, COLS), jnp.bfloat16),
-            pltpu.VMEM((BLOCKS * SLOTS * ROWS, BLOCK), jnp.float32),
-            pltpu.SemaphoreType.DMA((BLOCKS,)),
         ],
         compiler_params=pltpu.CompilerParams(vmem_limit_bytes=LIMIT),
         name="basis",
@@ -226,9 +235,7 @@
     )
 
 
-def solve_kernel(grams, planes_in, entries, difference, placed, planes, sem):
-    copy = pltpu.make_async_copy(planes_in, planes, sem)
-    copy.start()
+def solve_kernel(grams, planes, entries, difference, placed):
     total = grams[0] + grams[1] + grams[2] + grams[3]
     cross = total[:, SLOTS : 2 * SLOTS]
     normal = total[:, :SLOTS] + cross + cross.T
@@ -244,12 +251,13 @@
         column = jnp.where(row_id[:, :1] == step, 0.0, matrix[:, step : step + 1])
         matrix = jnp.where(row_id == step, scaled, matrix - column * scaled)
     answer = jnp.broadcast_to(matrix[:, NBASIS : NBASIS + 1], (SLOTS, BLOCK))
-    copy.wait()
     for block in range(BLOCKS):
-        total = planes[block, NBASIS * ROWS : USED * ROWS, :]
+        at = (block * SLOTS + NBASIS) * PITCH
+        total = planes[at : at + ROWS, :]
         for plane in range(NBASIS):
             factor = jnp.broadcast_to(answer[plane : plane + 1, :], (ROWS, BLOCK))
-            total = total - factor * planes[block, plane * ROWS : (plane + 1) * ROWS, :]
+            at = (block * SLOTS + plane) * PITCH
+            total = total - factor * planes[at : at + ROWS, :]
         difference[:, block * BLOCK : (block + 1) * BLOCK] = total
     row_move, col_move = entries[0, 1], entries[0, 2]
     moved = pltpu.roll(difference[...], lax.rem(row_move + ROWS, ROWS), axis=0)
@@ -265,12 +273,8 @@
     return pl.pallas_call(
         solve_kernel,
         out_shape=(shape, shape),
-        in_specs=[VMEM, ANY, SMEM],
+        in_specs=[VMEM, VMEM, SMEM],
         out_specs=(VMEM, VMEM),
-        scratch_shapes=[
-            pltpu.VMEM((BLOCKS, USED * ROWS, BLOCK), jnp.float32),
-            pltpu.SemaphoreType.DMA,
-        ],
         compiler_params=pltpu.CompilerParams(vmem_limit_bytes=LIMIT),
         name="solve",
     )(grams, planes, entries)
@@ -285,14 +289,17 @@
         for hit, stamp in zip(hits, (stamp_own, stamp_below, stamp_above)):
             total = total + jnp.where(hit == tile, stamp[...], 0.0)
             count = count + jnp.where(hit == tile, 1.0, 0.0)
-        tiles[tile, :ROWS, :] = total
-        tiles[tile, ROWS:, :] = jnp.full((8, COLS), count, jnp.float32)
+        for block in range(BLOCKS):
+            tiles[tile, block * ROWS : (block + 1) * ROWS, :] = total[
+                :, block * BLOCK : (block + 1) * BLOCK
+            ]
+        tiles[tile, TALL:, :] = jnp.full((8, BLOCK), count, jnp.float32)
 
 
 def gather(stamps, own, below, above):
     return pl.pallas_call(
         gather_kernel,
-        out_shape=jax.ShapeDtypeStruct((PLANE, ROWS + 8, COLS), jnp.float32),
+        out_shape=jax.ShapeDtypeStruct((PLANE, TALL + 8, BLOCK), jnp.float32),
         in_specs=[VMEM] * 3 + [SMEM] * 3,
         out_specs=VMEM,
         compiler_params=pltpu.CompilerParams(vmem_limit_bytes=LIMIT),
@@ -301,11 +308,16 @@
 
 
 def mean_kernel(parts, coadd):
-    total = parts[0]
+    count = parts[0, TALL:, :]
     for index in range(1, PLANE):
-        total = total + parts[index]
-    count = jnp.maximum(total[ROWS : ROWS + 1, :], 1.0)
-    coadd[...] = total[:ROWS] / count
+        count = count + parts[index, TALL:, :]
+    count = jnp.maximum(count[:1], 1.0)
+    for block in range(BLOCKS):
+        rows = slice(block * ROWS, (block + 1) * ROWS)
+        total = parts[0, rows, :]
+        for index in range(1, PLANE):
+            total = total + parts[index, rows, :]
+        coadd[:, block * BLOCK : (block + 1) * BLOCK] = total / count
 
 
 def mean(parts):
@@ -327,11 +339,8 @@
     own = intersections[0]
     below = lax.ppermute(own, "visit", upward)
     above = lax.ppermute(own, "visit", downward)
-    copies = jnp.broadcast_to(template, (PLANE, ROWS, COLS))
-    window = lax.all_to_all(copies, "visit", 0, 0, axis_index_groups=groups)
-    piece_own, piece_up, piece_down = serve(
-        window.reshape(PLANE * ROWS, COLS), own, below, above
-    )
+    window = lax.all_to_all(spread(template[0]), "visit", 0, 0, axis_index_groups=groups)
+    piece_own, piece_up, piece_down = serve(window, own, below, above)
     from_above = lax.ppermute(piece_down, "visit", downward)
     from_below = lax.ppermute(piece_up, "visit", upward)
     planes, gram = basis(

time: 100 us -> 94.7 us (0.947)
  Pallas kernels: 15.6 us -> 12.3 us
  local copies, waits for them, and re-layouts: 2.04 us -> 0.92 us
    pallas_call x3 -> x4, Pallas kernels: 14.1 us -> 10.8 us  [the longest x1 4.84 us: basis(): pl.pallas_call(basis_kernel, out_shape=(jax.ShapeDtypeStruct((BLOCKS * SL...]
    broadcast_in_dim x1 -> x0, local copies, waits for them, and re-layouts: 2.01 us -> none  [shards(): copies = jnp.broadcast_to(template, (PLANE, ROWS, COLS))]
where the time goes in v2:
time: 94.7 us; the launch traced here: 94.3 us
  starting transfers between devices  36.4 us (38%)
  blocking collectives  27.5 us (29%)
  waiting for transfers between devices  16.5 us (17%)
  Pallas kernels  12.3 us (13%)
    all_to_all x1, blocking collectives, shards(): parts = lax.all_to_all(tiles, 'visit', 0, 0, axis_index_groups=groups)  22.2 us
    ppermute x1, starting transfers between devices, shards(): above = lax.ppermute(own, 'visit', downward)  11.4 us
    ppermute x1, starting transfers between devices, shards(): from_above = lax.ppermute(piece_down, 'visit', downward)  9.18 us
    all_to_all x1, starting transfers between devices, shards(): lax.all_to_all(spread(template[0]), 'visit', 0, 0, axis_index_groups=groups)  6.18 us
    ppermute x1, waiting for transfers between devices, shards(): from_below = lax.ppermute(piece_up, 'visit', upward)  5.61 us
    all_gather x1, blocking collectives, shards(): grams = lax.all_gather(gram, 'patch')  5.25 us
    pallas_call x1, Pallas kernels, basis(): pl.pallas_call(basis_kernel, out_shape=(jax.ShapeDtypeStruct((BLOCKS * SL...  4.84 us
    ppermute x1, waiting for transfers between devices, shards(): below = lax.ppermute(own, 'visit', upward)  4.71 us
  transfers between devices with their start and end apart: 7, of which 5 were waited for; matrix products, arithmetic and copies ran while one was open for 0% of the time, Pallas kernels for 0%

profile of v2, /device:TPU:2, one launch (start us, length us, event | category | flops | bytes accessed | tf_op | source)
XLA Modules:
  0.0 94.3 jit_solution(16960419100610425237)
XLA Ops:
  0.6 0.9 copy-done.3
  1.5 1.1 %spread.1 = f32[8,256,128]{2,1,0:T(8,128)} custom-call(f32[64,512]{1,0:T(8,128)S(1)} %bitcast.8), custom_call_target="tpu_custom_call" | custom-call | tf_op jit(solution)/shard_map/spread/pallas_call | solution.py:113
  2.6 0.0 copy-start.5
  2.6 6.2 %all-to-all-start = ((f32[8,256,128]{2,1,0:T(8,128)}), f32[8,256,128]{2,1,0:T(8,128)S(1)}, u32[]{:S(2)}, u32[]{:S(2)}) async-start(f32[8,256,128]{2,1,0:T(8,128)} %spread.1), calls=%async_computation | async-start | bytes 2097152 | tf_op jit(solution)/shard_map/all_to_all | solution.py:342
  8.8 11.4 %collective-permute-start.1 = (s32[1,3]{1,0:T(1,128)S(1)}, s32[1,3]{1,0:T(1,128)S(1)}, u32[]{:S(2)}, u32[]{:S(2)}) collective-permute-start(s32[1,3]{1,0:T(1,128)S(1)} %bitcast.11), channel_id=1, source_target_pairs={{32,0},{36,4},{40,8},{44,12},{48,16},{52,20},{56,24},{60,28},{64,3... | collective-permute-start | bytes 44 | tf_op jit(solution)/shard_map/ppermute | solution.py:341
  20.2 1.9 %collective-permute-start = (s32[1,3]{1,0:T(1,128)S(1)}, s32[1,3]{1,0:T(1,128)S(1)}, u32[]{:S(2)}, u32[]{:S(2)}) collective-permute-start(s32[1,3]{1,0:T(1,128)S(1)} %bitcast.12), channel_id=1, source_target_pairs={{0,32},{4,36},{8,40},{12,44},{16,48},{20,52},{24,56},{28,60},{32,6... | collective-permute-start | bytes 44 | tf_op jit(solution)/shard_map/ppermute | solution.py:340
  22.1 0.0 collective-permute-done.1.above
  22.1 4.7 %collective-permute-done.below = s32[1,3]{1,0:T(1,128)S(1)} collective-permute-done((s32[1,3]{1,0:T(1,128)S(1)}, s32[1,3]{1,0:T(1,128)S(1)}, u32[]{:S(2)}, u32[]{:S(2)}) %collective-permute-start) | collective-permute-done | bytes 44 | tf_op jit(solution)/shard_map/ppermute | solution.py:340
  26.9 0.0 all-to-all-done.window
  26.9 0.8 serve.1
  27.6 9.2 %collective-permute-start.2 = (f32[96,512]{1,0:T(8,128)S(1)}, f32[96,512]{1,0:T(8,128)S(1)}, u32[]{:S(2)}, u32[]{:S(2)}) collective-permute-start(f32[96,512]{1,0:T(8,128)S(1)} %get-tuple-element.10), channel_id=1, source_target_pairs={{32,0},{36,4},{40,8},{44,12},{48,16},{52,20},{56,24},{60,28},{64,3... | collective-permute-start | bytes 589832 | tf_op jit(solution)/shard_map/ppermute | solution.py:344
  36.8 1.9 %collective-permute-start.3 = (f32[96,512]{1,0:T(8,128)S(1)}, f32[96,512]{1,0:T(8,128)S(1)}, u32[]{:S(2)}, u32[]{:S(2)}) collective-permute-start(f32[96,512]{1,0:T(8,128)S(1)} %get-tuple-element.11), channel_id=1, source_target_pairs={{0,32},{4,36},{8,40},{12,44},{16,48},{20,52},{24,56},{28,60},{32,6... | collective-permute-start | bytes 589832 | tf_op jit(solution)/shard_map/ppermute | solution.py:345
  38.7 1.2 %collective-permute-done.2.piece_b = f32[96,512]{1,0:T(8,128)S(1)} collective-permute-done((f32[96,512]{1,0:T(8,128)S(1)}, f32[96,512]{1,0:T(8,128)S(1)}, u32[]{:S(2)}, u32[]{:S(2)}) %collective-permute-start.2) | collective-permute-done | bytes 196640 | tf_op jit(solution)/shard_map/ppermute | solution.py:344
  40.0 5.6 %collective-permute-done.3.piece_c = f32[96,512]{1,0:T(8,128)S(1)} collective-permute-done((f32[96,512]{1,0:T(8,128)S(1)}, f32[96,512]{1,0:T(8,128)S(1)}, u32[]{:S(2)}, u32[]{:S(2)}) %collective-permute-start.3) | collective-permute-done | bytes 196640 | tf_op jit(solution)/shard_map/ppermute | solution.py:345
  45.6 4.8 %basis.1 = (f32[9216,128]{1,0:T(8,128)S(1)}, f32[32,128]{1,0:T(8,128)S(1)}) custom-call(f32[96,512]{1,0:T(8,128)S(1)} %get-tuple-element.9.piece_a, f32[96,512]{1,0:T(8,128)S(1)} %collective-permute-done.2.piece_b, f32[96,512]{1,0:T(8,128)S(1)} %collective-permute-done.3.piece_c, f32[64,512]{1,0:T(8,128)S(1)} %bitcast.9, f32[64,512]{1,0:T(8,128)S(1)} %bitcast.10, ...), custom_call_target="tpu_custom_call" | custom-call | tf_op jit(solution)/shard_map/basis/pallas_call | solution.py:218
  50.5 5.2 %all-gather = f32[128,128]{1,0:T(8,128)S(1)} all-gather(f32[32,128]{1,0:T(8,128)S(1)} %get-tuple-element.12), channel_id=2, replica_groups=mesh['visit'=128,'patch'=4] {'patch'}, dimensions={0}, use_global_device_ids=true | all-gather | bytes 81920 | tf_op jit(solution)/shard_map/all_gather | solution.py:349
  55.7 4.1 %solve.1 = (f32[64,512]{1,0:T(8,128)}, f32[64,512]{1,0:T(8,128)S(1)}) custom-call(f32[4,32,128]{2,1,0:T(8,128)S(1)} %bitcast.7, f32[9216,128]{1,0:T(8,128)S(1)} %get-tuple-element.13.planes, s32[1,3]{1,0:T(1,128)S(1)} %bitcast.15), custom_call_target="tpu_custom_call" | custom-call | tf_op jit(solution)/shard_map/solve/pallas_call | solution.py:273
  59.9 1.9 %collective-permute-start.5 = (f32[64,512]{1,0:T(8,128)S(1)}, f32[64,512]{1,0:T(8,128)S(1)}, u32[]{:S(2)}, u32[]{:S(2)}) collective-permute-start(f32[64,512]{1,0:T(8,128)S(1)} %get-tuple-element.15.stamp_own), channel_id=1, source_target_pairs={{32,0},{36,4},{40,8},{44,12},{48,16},{52,20},{56,24},{60,28},{64,3... | collective-permute-start | bytes 393224 | tf_op jit(solution)/shard_map/ppermute | solution.py:352
  61.8 3.9 %collective-permute-start.4 = (f32[64,512]{1,0:T(8,128)S(1)}, f32[64,512]{1,0:T(8,128)S(1)}, u32[]{:S(2)}, u32[]{:S(2)}) collective-permute-start(f32[64,512]{1,0:T(8,128)S(1)} %get-tuple-element.15.stamp_own), channel_id=1, source_target_pairs={{0,32},{4,36},{8,40},{12,44},{16,48},{20,52},{24,56},{28,60},{32,6... | collective-permute-start | bytes 393224 | tf_op jit(solution)/shard_map/ppermute | solution.py:351
  65.7 1.8 %collective-permute-done.5.stamp_above = f32[64,512]{1,0:T(8,128)S(1)} collective-permute-done((f32[64,512]{1,0:T(8,128)S(1)}, f32[64,512]{1,0:T(8,128)S(1)}, u32[]{:S(2)}, u32[]{:S(2)}) %collective-permute-start.5) | collective-permute-done | bytes 131104 | tf_op jit(solution)/shard_map/ppermute | solution.py:352
  67.5 3.1 %collective-permute-done.4.stamp_below = f32[64,512]{1,0:T(8,128)S(1)} collective-permute-done((f32[64,512]{1,0:T(8,128)S(1)}, f32[64,512]{1,0:T(8,128)S(1)}, u32[]{:S(2)}, u32[]{:S(2)}) %collective-permute-start.4) | collective-permute-done | bytes 131104 | tf_op jit(solution)/shard_map/ppermute | solution.py:351
  70.6 0.8 gather.1
  71.4 22.2 %all_to_all.10.parts = f32[8,264,128]{2,1,0:T(8,128)S(1)} all-to-all(f32[8,264,128]{2,1,0:T(8,128)S(1)} %gather.1), channel_id=1, replica_groups={{0,4,8,12,16,20,24,28},{32,36,40,44,48,52,56,60},{64,68,72,76,80,84,88,..., dimensions={0} | all-to-all | bytes 2162688 | tf_op jit(solution)/shard_map/all_to_all | solution.py:354
  93.6 0.7 mean.1
  (12 shorter events, 0.0 us)
Async XLA Ops:
  0.6 0.9 copy-start.3
  1.5 7.3 %copy-start.6 = (s32[1,1,3]{2,1,0:T(1,128)S(1)}, s32[1,1,3]{2,1,0:T(1,128)}, u32[]{:S(2)}) copy-start(s32[1,1,3]{2,1,0:T(1,128)} %param.10) | copy-start | bytes 40
  2.6 43.0 %copy-start = (bf16[256,1408]{1,0:T(8,128)(2,1)S(1)}, bf16[256,1408]{1,0:T(8,128)(2,1)}, u32[]{:S(2)}) copy-start(bf16[256,1408]{1,0:T(8,128)(2,1)} %constant.7.clone.col_low) | copy-start | bytes 2162692
  2.6 43.0 %copy-start.1 = (bf16[256,1408]{1,0:T(8,128)(2,1)S(1)}, bf16[256,1408]{1,0:T(8,128)(2,1)}, u32[]{:S(2)}) copy-start(bf16[256,1408]{1,0:T(8,128)(2,1)} %constant.6.clone.col_high) | copy-start | bytes 2162692
  2.6 43.0 %copy-start.2 = (bf16[864,192]{1,0:T(8,128)(2,1)S(1)}, bf16[864,192]{1,0:T(8,128)(2,1)}, u32[]{:S(2)}) copy-start(bf16[864,192]{1,0:T(8,128)(2,1)} %constant.8.clone.row_table) | copy-start | bytes 995332
  2.6 43.0 %copy-start.4 = (f32[1,1,64,512]{3,2,1,0:T(8,128)S(1)}, f32[1,1,64,512]{3,2,1,0:T(8,128)}, u32[]{:S(2)}) copy-start(f32[1,1,64,512]{3,2,1,0:T(8,128)} %param.8) | copy-start | bytes 393220
  2.6 43.0 %copy-start.5 = (f32[1,1,64,512]{3,2,1,0:T(8,128)S(1)}, f32[1,1,64,512]{3,2,1,0:T(8,128)}, u32[]{:S(2)}) copy-start(f32[1,1,64,512]{3,2,1,0:T(8,128)} %param.9) | copy-start | bytes 393220
  2.6 24.2 %all-to-all-start = ((f32[8,256,128]{2,1,0:T(8,128)}), f32[8,256,128]{2,1,0:T(8,128)S(1)}, u32[]{:S(2)}, u32[]{:S(2)}) async-start(f32[8,256,128]{2,1,0:T(8,128)} %spread.1), calls=%async_computation | async-start | bytes 2097152 | tf_op jit(solution)/shard_map/all_to_all | solution.py:342
  8.8 13.3 %collective-permute-start.1 = (s32[1,3]{1,0:T(1,128)S(1)}, s32[1,3]{1,0:T(1,128)S(1)}, u32[]{:S(2)}, u32[]{:S(2)}) collective-permute-start(s32[1,3]{1,0:T(1,128)S(1)} %bitcast.11), channel_id=1, source_target_pairs={{32,0},{36,4},{40,8},{44,12},{48,16},{52,20},{56,24},{60,28},{64,3... | collective-permute-start | bytes 44 | tf_op jit(solution)/shard_map/ppermute | solution.py:341
  20.2 6.6 %collective-permute-start = (s32[1,3]{1,0:T(1,128)S(1)}, s32[1,3]{1,0:T(1,128)S(1)}, u32[]{:S(2)}, u32[]{:S(2)}) collective-permute-start(s32[1,3]{1,0:T(1,128)S(1)} %bitcast.12), channel_id=1, source_target_pairs={{0,32},{4,36},{8,40},{12,44},{16,48},{20,52},{24,56},{28,60},{32,6... | collective-permute-start | bytes 44 | tf_op jit(solution)/shard_map/ppermute | solution.py:340
  27.6 12.4 %collective-permute-start.2 = (f32[96,512]{1,0:T(8,128)S(1)}, f32[96,512]{1,0:T(8,128)S(1)}, u32[]{:S(2)}, u32[]{:S(2)}) collective-permute-start(f32[96,512]{1,0:T(8,128)S(1)} %get-tuple-element.10), channel_id=1, source_target_pairs={{32,0},{36,4},{40,8},{44,12},{48,16},{52,20},{56,24},{60,28},{64,3... | collective-permute-start | bytes 589832 | tf_op jit(solution)/shard_map/ppermute | solution.py:344
  36.8 8.8 %collective-permute-start.3 = (f32[96,512]{1,0:T(8,128)S(1)}, f32[96,512]{1,0:T(8,128)S(1)}, u32[]{:S(2)}, u32[]{:S(2)}) collective-permute-start(f32[96,512]{1,0:T(8,128)S(1)} %get-tuple-element.11), channel_id=1, source_target_pairs={{0,32},{4,36},{8,40},{12,44},{16,48},{20,52},{24,56},{28,60},{32,6... | collective-permute-start | bytes 589832 | tf_op jit(solution)/shard_map/ppermute | solution.py:345
  59.9 7.6 %collective-permute-start.5 = (f32[64,512]{1,0:T(8,128)S(1)}, f32[64,512]{1,0:T(8,128)S(1)}, u32[]{:S(2)}, u32[]{:S(2)}) collective-permute-start(f32[64,512]{1,0:T(8,128)S(1)} %get-tuple-element.15.stamp_own), channel_id=1, source_target_pairs={{32,0},{36,4},{40,8},{44,12},{48,16},{52,20},{56,24},{60,28},{64,3... | collective-permute-start | bytes 393224 | tf_op jit(solution)/shard_map/ppermute | solution.py:352
  61.8 8.8 %collective-permute-start.4 = (f32[64,512]{1,0:T(8,128)S(1)}, f32[64,512]{1,0:T(8,128)S(1)}, u32[]{:S(2)}, u32[]{:S(2)}) collective-permute-start(f32[64,512]{1,0:T(8,128)S(1)} %get-tuple-element.15.stamp_own), channel_id=1, source_target_pairs={{0,32},{4,36},{8,40},{12,44},{16,48},{20,52},{24,56},{28,60},{32,6... | collective-permute-start | bytes 393224 | tf_op jit(solution)/shard_map/ppermute | solution.py:351

commit v3 on v2

--- a/solution.py
+++ b/solution.py
@@ -24,6 +24,7 @@
 PITCH = 72
 TALL = BLOCKS * ROWS
 HALF = 32
+CHUNK = 32
 DEPTH = 64
 
 SIGMAS = (1.0, 2.0, 4.0)
@@ -194,9 +195,9 @@
         put_plane(planes, slot, 0, jnp.zeros((ROWS, COLS), jnp.float32))
     def gram_step(chunk, total):
         highs, lows = [], []
-        for inner in range(8):
+        for inner in range(CHUNK):
             for block in range(BLOCKS):
-                row = block * SLOTS * PITCH + chunk * 8 + inner
+                row = block * SLOTS * PITCH + chunk * CHUNK + inner
                 high, low = split(planes[pl.ds(row, SLOTS, stride=PITCH), :])
                 highs.append(high)
                 lows.append(low)
@@ -207,7 +208,7 @@
             high, both, (((1,), (1,)), ((), ())), preferred_element_type=jnp.float32
         )
 
-    total = lax.fori_loop(0, ROWS // 8, gram_step, jnp.zeros((SLOTS, 2 * SLOTS), jnp.float32))
+    total = lax.fori_loop(0, ROWS // CHUNK, gram_step, jnp.zeros((SLOTS, 2 * SLOTS), jnp.float32))
     gram_out[...] = jnp.concatenate(
         [total, jnp.zeros((SLOTS, BLOCK - 2 * SLOTS), jnp.float32)], axis=1
     )
@@ -244,12 +245,17 @@
     diagonal = jnp.logical_and(row_id == col_id, row_id < NBASIS)
     trace = jnp.sum(jnp.where(diagonal, normal, 0.0), keepdims=True)
     matrix = normal + jnp.where(diagonal, RIDGE * trace / NBASIS, 0.0)
-    for step in range(NBASIS):
-        row = matrix[step : step + 1, :]
-        inverse = 1.0 / row[:, step : step + 1]
-        scaled = row * inverse
-        column = jnp.where(row_id[:, :1] == step, 0.0, matrix[:, step : step + 1])
-        matrix = jnp.where(row_id == step, scaled, matrix - column * scaled)
+    for step in range(0, NBASIS, 2):
+        first = jnp.broadcast_to(matrix[:, step : step + 1], (SLOTS, SLOTS))
+        second = jnp.broadcast_to(matrix[:, step + 1 : step + 2], (SLOTS, SLOTS))
+        upper, lower = slice(step, step + 1), slice(step + 1, step + 2)
+        inverse = 1.0 / (first[upper] * second[lower] - second[upper] * first[lower])
+        row_upper = (second[lower] * matrix[upper] - second[upper] * matrix[lower]) * inverse
+        row_lower = (first[upper] * matrix[lower] - first[lower] * matrix[upper]) * inverse
+        others = matrix - first * row_upper - second * row_lower
+        matrix = jnp.where(
+            row_id == step, row_upper, jnp.where(row_id == step + 1, row_lower, others)
+        )
     answer = jnp.broadcast_to(matrix[:, NBASIS : NBASIS + 1], (SLOTS, BLOCK))
     for block in range(BLOCKS):
         at = (block * SLOTS + NBASIS) * PITCH
@@ -281,8 +287,11 @@
 
 
 def gather_kernel(stamp_own, stamp_below, stamp_above, own, below, above, tiles):
-    base = (lax.axis_index("visit") // PLANE) * PLANE
+    visit = lax.axis_index("visit")
+    base = (visit // PLANE) * PLANE
     hits = [entries[0, 0] - base for entries in (own, below, above)]
+    hits[1] = jnp.where(visit >= PLANE, hits[1], -1)
+    hits[2] = jnp.where(visit < lax.axis_size("visit") - PLANE, hits[2], -1)
     for tile in range(PLANE):
         total = jnp.zeros((ROWS, COLS), jnp.float32)
         count = jnp.float32(0.0)
@@ -334,7 +343,7 @@
 def shards(template, science, inverse_variance, intersections):
     visits = lax.axis_size("visit")
     groups = [list(range(first, first + PLANE)) for first in range(0, visits, PLANE)]
-    upward = [(i, (i + PLANE) % visits) for i in range(visits)]
+    upward = [(i, i + PLANE) for i in range(visits - PLANE)]
     downward = [(target, source) for source, target in upward]
     own = intersections[0]
     below = lax.ppermute(own, "visit", upward)

time: 94.7 us -> 86.5 us (0.913)
  the two profiles are of different devices: /device:TPU:2 before, /device:TPU:384 now
where the time goes in v3:
time: 86.5 us; the launch traced here: 86.1 us
  blocking collectives  27.5 us (32%)
  starting transfers between devices  25 us (29%)
  waiting for transfers between devices  21.5 us (25%)
  Pallas kernels  10.4 us (12%)
  local copies, waits for them, and re-layouts  0.92 us (1%)
    all_to_all x1, blocking collectives, shards(): parts = lax.all_to_all(tiles, 'visit', 0, 0, axis_index_groups=groups)  22.2 us
    all_to_all x1, starting transfers between devices, shards(): lax.all_to_all(spread(template[0]), 'visit', 0, 0, axis_index_groups=groups)  7.07 us
    ppermute x1, waiting for transfers between devices, shards(): from_below = lax.ppermute(piece_up, 'visit', upward)  5.34 us
    all_gather x1, blocking collectives, shards(): grams = lax.all_gather(gram, 'patch')  5.25 us
    all_to_all x1, waiting for transfers between devices, shards(): lax.all_to_all(spread(template[0]), 'visit', 0, 0, axis_index_groups=groups)  5.06 us
    ppermute x1, waiting for transfers between devices, shards(): below = lax.ppermute(own, 'visit', upward)  4.71 us
    ppermute x1, starting transfers between devices, shards(): above = lax.ppermute(own, 'visit', downward)  4.13 us
    ppermute x1, starting transfers between devices, shards(): from_above = lax.ppermute(piece_down, 'visit', downward)  4.13 us
  transfers between devices with their start and end apart: 7, of which 6 were waited for; matrix products, arithmetic and copies ran while one was open for 0% of the time, Pallas kernels for 0%

profile of v3, /device:TPU:384, one launch (start us, length us, event | category | flops | bytes accessed | tf_op | source)
XLA Modules:
  0.0 86.1 jit_solution(3120910157691346154)
XLA Ops:
  0.6 0.9 %copy-done.3 = f32[1,64,512]{2,1,0:T(8,128)S(1)} copy-done((f32[1,64,512]{2,1,0:T(8,128)S(1)}, f32[1,64,512]{2,1,0:T(8,128)}, u32[]{:S(2)}) %copy-start.3) | copy-done | bytes 131096
  1.5 1.1 %spread.1 = f32[8,256,128]{2,1,0:T(8,128)} custom-call(f32[64,512]{1,0:T(8,128)S(1)} %bitcast.8), custom_call_target="tpu_custom_call" | custom-call | tf_op jit(solution)/shard_map/spread/pallas_call | solution.py:114
  2.6 0.0 copy-start.5
  2.6 7.1 %all-to-all-start = ((f32[8,256,128]{2,1,0:T(8,128)}), f32[8,256,128]{2,1,0:T(8,128)S(1)}, u32[]{:S(2)}, u32[]{:S(2)}) async-start(f32[8,256,128]{2,1,0:T(8,128)} %spread.1), calls=%async_computation | async-start | bytes 2097152 | tf_op jit(solution)/shard_map/all_to_all | solution.py:351
  9.7 4.1 %collective-permute-start.1 = (s32[1,3]{1,0:T(1,128)S(1)}, s32[1,3]{1,0:T(1,128)S(1)}, u32[]{:S(2)}, u32[]{:S(2)}) collective-permute-start(s32[1,3]{1,0:T(1,128)S(1)} %bitcast.11), channel_id=1, source_target_pairs={{32,0},{36,4},{40,8},{44,12},{48,16},{52,20},{56,24},{60,28},{64,3... | collective-permute-start | bytes 44 | tf_op jit(solution)/shard_map/ppermute | solution.py:350
  13.8 1.9 %collective-permute-start = (s32[1,3]{1,0:T(1,128)S(1)}, s32[1,3]{1,0:T(1,128)S(1)}, u32[]{:S(2)}, u32[]{:S(2)}) collective-permute-start(s32[1,3]{1,0:T(1,128)S(1)} %bitcast.12), channel_id=1, source_target_pairs={{0,32},{4,36},{8,40},{12,44},{16,48},{20,52},{24,56},{28,60},{32,6... | collective-permute-start | bytes 44 | tf_op jit(solution)/shard_map/ppermute | solution.py:349
  15.8 0.0 collective-permute-done.1.above
  15.8 4.7 %collective-permute-done.below = s32[1,3]{1,0:T(1,128)S(1)} collective-permute-done((s32[1,3]{1,0:T(1,128)S(1)}, s32[1,3]{1,0:T(1,128)S(1)}, u32[]{:S(2)}, u32[]{:S(2)}) %collective-permute-start) | collective-permute-done | bytes 44 | tf_op jit(solution)/shard_map/ppermute | solution.py:349
  20.5 5.1 %all-to-all-done.window = f32[8,256,128]{2,1,0:T(8,128)S(1)} async-done(((f32[8,256,128]{2,1,0:T(8,128)}), f32[8,256,128]{2,1,0:T(8,128)S(1)}, u32[]{:S(2)}, u32[]{:S(2)}) %all-to-all-start) | async-done | bytes 1048608 | tf_op jit(solution)/shard_map/all_to_all | solution.py:351
  25.5 0.8 serve.1
  26.3 4.1 %collective-permute-start.2 = (f32[96,512]{1,0:T(8,128)S(1)}, f32[96,512]{1,0:T(8,128)S(1)}, u32[]{:S(2)}, u32[]{:S(2)}) collective-permute-start(f32[96,512]{1,0:T(8,128)S(1)} %get-tuple-element.10), channel_id=1, source_target_pairs={{32,0},{36,4},{40,8},{44,12},{48,16},{52,20},{56,24},{60,28},{64,3... | collective-permute-start | bytes 589832 | tf_op jit(solution)/shard_map/ppermute | solution.py:353
  30.4 1.9 %collective-permute-start.3 = (f32[96,512]{1,0:T(8,128)S(1)}, f32[96,512]{1,0:T(8,128)S(1)}, u32[]{:S(2)}, u32[]{:S(2)}) collective-permute-start(f32[96,512]{1,0:T(8,128)S(1)} %get-tuple-element.11), channel_id=1, source_target_pairs={{0,32},{4,36},{8,40},{12,44},{16,48},{20,52},{24,56},{28,60},{32,6... | collective-permute-start | bytes 589832 | tf_op jit(solution)/shard_map/ppermute | solution.py:354
  32.4 1.5 %collective-permute-done.2.piece_b = f32[96,512]{1,0:T(8,128)S(1)} collective-permute-done((f32[96,512]{1,0:T(8,128)S(1)}, f32[96,512]{1,0:T(8,128)S(1)}, u32[]{:S(2)}, u32[]{:S(2)}) %collective-permute-start.2) | collective-permute-done | bytes 196640 | tf_op jit(solution)/shard_map/ppermute | solution.py:353
  33.9 5.3 %collective-permute-done.3.piece_c = f32[96,512]{1,0:T(8,128)S(1)} collective-permute-done((f32[96,512]{1,0:T(8,128)S(1)}, f32[96,512]{1,0:T(8,128)S(1)}, u32[]{:S(2)}, u32[]{:S(2)}) %collective-permute-start.3) | collective-permute-done | bytes 196640 | tf_op jit(solution)/shard_map/ppermute | solution.py:354
  39.2 4.0 %basis.1 = (f32[9216,128]{1,0:T(8,128)S(1)}, f32[32,128]{1,0:T(8,128)S(1)}) custom-call(f32[96,512]{1,0:T(8,128)S(1)} %get-tuple-element.9.piece_a, f32[96,512]{1,0:T(8,128)S(1)} %collective-permute-done.2.piece_b, f32[96,512]{1,0:T(8,128)S(1)} %collective-permute-done.3.piece_c, f32[64,512]{1,0:T(8,128)S(1)} %bitcast.9, f32[64,512]{1,0:T(8,128)S(1)} %bitcast.10, ...), custom_call_target="tpu_custom_call" | custom-call | tf_op jit(solution)/shard_map/basis/pallas_call | solution.py:219
  43.2 5.2 %all-gather = f32[128,128]{1,0:T(8,128)S(1)} all-gather(f32[32,128]{1,0:T(8,128)S(1)} %get-tuple-element.12), channel_id=2, replica_groups=mesh['visit'=128,'patch'=4] {'patch'}, dimensions={0}, use_global_device_ids=true | all-gather | bytes 81920 | tf_op jit(solution)/shard_map/all_gather | solution.py:358
  48.5 3.2 %solve.1 = (f32[64,512]{1,0:T(8,128)}, f32[64,512]{1,0:T(8,128)S(1)}) custom-call(f32[4,32,128]{2,1,0:T(8,128)S(1)} %bitcast.7, f32[9216,128]{1,0:T(8,128)S(1)} %get-tuple-element.13.planes, s32[1,3]{1,0:T(1,128)S(1)} %bitcast.15), custom_call_target="tpu_custom_call" | custom-call | tf_op jit(solution)/shard_map/solve/pallas_call | solution.py:279
  51.6 1.9 %collective-permute-start.5 = (f32[64,512]{1,0:T(8,128)S(1)}, f32[64,512]{1,0:T(8,128)S(1)}, u32[]{:S(2)}, u32[]{:S(2)}) collective-permute-start(f32[64,512]{1,0:T(8,128)S(1)} %get-tuple-element.15.stamp_own), channel_id=1, source_target_pairs={{32,0},{36,4},{40,8},{44,12},{48,16},{52,20},{56,24},{60,28},{64,3... | collective-permute-start | bytes 393224 | tf_op jit(solution)/shard_map/ppermute | solution.py:361
  53.5 3.9 %collective-permute-start.4 = (f32[64,512]{1,0:T(8,128)S(1)}, f32[64,512]{1,0:T(8,128)S(1)}, u32[]{:S(2)}, u32[]{:S(2)}) collective-permute-start(f32[64,512]{1,0:T(8,128)S(1)} %get-tuple-element.15.stamp_own), channel_id=1, source_target_pairs={{0,32},{4,36},{8,40},{12,44},{16,48},{20,52},{24,56},{28,60},{32,6... | collective-permute-start | bytes 393224 | tf_op jit(solution)/shard_map/ppermute | solution.py:360
  57.5 1.8 %collective-permute-done.5.stamp_above = f32[64,512]{1,0:T(8,128)S(1)} collective-permute-done((f32[64,512]{1,0:T(8,128)S(1)}, f32[64,512]{1,0:T(8,128)S(1)}, u32[]{:S(2)}, u32[]{:S(2)}) %collective-permute-start.5) | collective-permute-done | bytes 131104 | tf_op jit(solution)/shard_map/ppermute | solution.py:361
  59.2 3.1 %collective-permute-done.4.stamp_below = f32[64,512]{1,0:T(8,128)S(1)} collective-permute-done((f32[64,512]{1,0:T(8,128)S(1)}, f32[64,512]{1,0:T(8,128)S(1)}, u32[]{:S(2)}, u32[]{:S(2)}) %collective-permute-start.4) | collective-permute-done | bytes 131104 | tf_op jit(solution)/shard_map/ppermute | solution.py:360
  62.4 0.8 gather.1
  63.2 22.2 %all_to_all.10.parts = f32[8,264,128]{2,1,0:T(8,128)S(1)} all-to-all(f32[8,264,128]{2,1,0:T(8,128)S(1)} %gather.1), channel_id=1, replica_groups={{0,4,8,12,16,20,24,28},{32,36,40,44,48,52,56,60},{64,68,72,76,80,84,88,..., dimensions={0} | all-to-all | bytes 2162688 | tf_op jit(solution)/shard_map/all_to_all | solution.py:363
  85.4 0.7 mean.1
  (12 shorter events, 0.0 us)
Async XLA Ops:
  0.6 0.9 %copy-start.3 = (f32[1,64,512]{2,1,0:T(8,128)S(1)}, f32[1,64,512]{2,1,0:T(8,128)}, u32[]{:S(2)}) copy-start(f32[1,64,512]{2,1,0:T(8,128)} %param.7) | copy-start | bytes 393220
  1.5 8.2 %copy-start.6 = (s32[1,1,3]{2,1,0:T(1,128)S(1)}, s32[1,1,3]{2,1,0:T(1,128)}, u32[]{:S(2)}) copy-start(s32[1,1,3]{2,1,0:T(1,128)} %param.10) | copy-start | bytes 40
  2.6 36.6 %copy-start = (bf16[256,1408]{1,0:T(8,128)(2,1)S(1)}, bf16[256,1408]{1,0:T(8,128)(2,1)}, u32[]{:S(2)}) copy-start(bf16[256,1408]{1,0:T(8,128)(2,1)} %constant.7.clone.col_low) | copy-start | bytes 2162692
  2.6 36.6 %copy-start.1 = (bf16[256,1408]{1,0:T(8,128)(2,1)S(1)}, bf16[256,1408]{1,0:T(8,128)(2,1)}, u32[]{:S(2)}) copy-start(bf16[256,1408]{1,0:T(8,128)(2,1)} %constant.6.clone.col_high) | copy-start | bytes 2162692
  2.6 36.6 %copy-start.2 = (bf16[864,192]{1,0:T(8,128)(2,1)S(1)}, bf16[864,192]{1,0:T(8,128)(2,1)}, u32[]{:S(2)}) copy-start(bf16[864,192]{1,0:T(8,128)(2,1)} %constant.8.clone.row_table) | copy-start | bytes 995332
  2.6 36.6 %copy-start.4 = (f32[1,1,64,512]{3,2,1,0:T(8,128)S(1)}, f32[1,1,64,512]{3,2,1,0:T(8,128)}, u32[]{:S(2)}) copy-start(f32[1,1,64,512]{3,2,1,0:T(8,128)} %param.8) | copy-start | bytes 393220
  2.6 36.6 %copy-start.5 = (f32[1,1,64,512]{3,2,1,0:T(8,128)S(1)}, f32[1,1,64,512]{3,2,1,0:T(8,128)}, u32[]{:S(2)}) copy-start(f32[1,1,64,512]{3,2,1,0:T(8,128)} %param.9) | copy-start | bytes 393220
  2.6 22.9 %all-to-all-start = ((f32[8,256,128]{2,1,0:T(8,128)}), f32[8,256,128]{2,1,0:T(8,128)S(1)}, u32[]{:S(2)}, u32[]{:S(2)}) async-start(f32[8,256,128]{2,1,0:T(8,128)} %spread.1), calls=%async_computation | async-start | bytes 2097152 | tf_op jit(solution)/shard_map/all_to_all | solution.py:351
  9.7 6.1 %collective-permute-start.1 = (s32[1,3]{1,0:T(1,128)S(1)}, s32[1,3]{1,0:T(1,128)S(1)}, u32[]{:S(2)}, u32[]{:S(2)}) collective-permute-start(s32[1,3]{1,0:T(1,128)S(1)} %bitcast.11), channel_id=1, source_target_pairs={{32,0},{36,4},{40,8},{44,12},{48,16},{52,20},{56,24},{60,28},{64,3... | collective-permute-start | bytes 44 | tf_op jit(solution)/shard_map/ppermute | solution.py:350
  13.8 6.6 %collective-permute-start = (s32[1,3]{1,0:T(1,128)S(1)}, s32[1,3]{1,0:T(1,128)S(1)}, u32[]{:S(2)}, u32[]{:S(2)}) collective-permute-start(s32[1,3]{1,0:T(1,128)S(1)} %bitcast.12), channel_id=1, source_target_pairs={{0,32},{4,36},{8,40},{12,44},{16,48},{20,52},{24,56},{28,60},{32,6... | collective-permute-start | bytes 44 | tf_op jit(solution)/shard_map/ppermute | solution.py:349
  26.3 7.6 %collective-permute-start.2 = (f32[96,512]{1,0:T(8,128)S(1)}, f32[96,512]{1,0:T(8,128)S(1)}, u32[]{:S(2)}, u32[]{:S(2)}) collective-permute-start(f32[96,512]{1,0:T(8,128)S(1)} %get-tuple-element.10), channel_id=1, source_target_pairs={{32,0},{36,4},{40,8},{44,12},{48,16},{52,20},{56,24},{60,28},{64,3... | collective-permute-start | bytes 589832 | tf_op jit(solution)/shard_map/ppermute | solution.py:353
  30.4 8.8 %collective-permute-start.3 = (f32[96,512]{1,0:T(8,128)S(1)}, f32[96,512]{1,0:T(8,128)S(1)}, u32[]{:S(2)}, u32[]{:S(2)}) collective-permute-start(f32[96,512]{1,0:T(8,128)S(1)} %get-tuple-element.11), channel_id=1, source_target_pairs={{0,32},{4,36},{8,40},{12,44},{16,48},{20,52},{24,56},{28,60},{32,6... | collective-permute-start | bytes 589832 | tf_op jit(solution)/shard_map/ppermute | solution.py:354
  51.6 7.6 %collective-permute-start.5 = (f32[64,512]{1,0:T(8,128)S(1)}, f32[64,512]{1,0:T(8,128)S(1)}, u32[]{:S(2)}, u32[]{:S(2)}) collective-permute-start(f32[64,512]{1,0:T(8,128)S(1)} %get-tuple-element.15.stamp_own), channel_id=1, source_target_pairs={{32,0},{36,4},{40,8},{44,12},{48,16},{52,20},{56,24},{60,28},{64,3... | collective-permute-start | bytes 393224 | tf_op jit(solution)/shard_map/ppermute | solution.py:361
  53.5 8.8 %collective-permute-start.4 = (f32[64,512]{1,0:T(8,128)S(1)}, f32[64,512]{1,0:T(8,128)S(1)}, u32[]{:S(2)}, u32[]{:S(2)}) collective-permute-start(f32[64,512]{1,0:T(8,128)S(1)} %get-tuple-element.15.stamp_own), channel_id=1, source_target_pairs={{0,32},{4,36},{8,40},{12,44},{16,48},{20,52},{24,56},{28,60},{32,6... | collective-permute-start | bytes 393224 | tf_op jit(solution)/shard_map/ppermute | solution.py:360

commit v4 on v3

--- a/solution.py
+++ b/solution.py
@@ -17,12 +17,14 @@
 ROWS = 64
 COLS = 512
 PLANE = 8
+LINE = 4
 SPAN = 96
 SLOTS = 32
 BLOCK = 128
 BLOCKS = COLS // BLOCK
 PITCH = 72
 TALL = BLOCKS * ROWS
+NOTED = TALL + 8
 HALF = 32
 CHUNK = 32
 DEPTH = 64
@@ -236,7 +238,7 @@
     )
 
 
-def solve_kernel(grams, planes, entries, difference, placed):
+def solve_kernel(grams, planes, entries, difference, stamps):
     total = grams[0] + grams[1] + grams[2] + grams[3]
     cross = total[:, SLOTS : 2 * SLOTS]
     normal = total[:, :SLOTS] + cross + cross.T
@@ -271,14 +273,25 @@
     from_row = lax.broadcasted_iota(jnp.int32, (ROWS, COLS), 0) - row_move
     from_col = lax.broadcasted_iota(jnp.int32, (ROWS, COLS), 1) - col_move
     inside = (from_row >= 0) & (from_row < ROWS) & (from_col >= 0) & (from_col < COLS)
-    placed[...] = jnp.where(inside, moved, 0.0)
+    placed = jnp.where(inside, moved, 0.0)
+    for place in range(LINE):
+        mine = lax.bitwise_and(entries[0, 0], LINE - 1) == place
+        for block in range(BLOCKS):
+            stamps[place, block * ROWS : (block + 1) * ROWS, :] = jnp.where(
+                mine, placed[:, block * BLOCK : (block + 1) * BLOCK], 0.0
+            )
+        stamps[place, TALL:, :] = jnp.full(
+            (NOTED - TALL, BLOCK), entries[0, 0].astype(jnp.float32), jnp.float32
+        )
 
 
 def solve(grams, planes, entries):
-    shape = jax.ShapeDtypeStruct((ROWS, COLS), jnp.float32)
     return pl.pallas_call(
         solve_kernel,
-        out_shape=(shape, shape),
+        out_shape=(
+            jax.ShapeDtypeStruct((ROWS, COLS), jnp.float32),
+            jax.ShapeDtypeStruct((LINE, NOTED, BLOCK), jnp.float32),
+        ),
         in_specs=[VMEM, VMEM, SMEM],
         out_specs=(VMEM, VMEM),
         compiler_params=pltpu.CompilerParams(vmem_limit_bytes=LIMIT),
@@ -286,58 +299,62 @@
     )(grams, planes, entries)
 
 
-def gather_kernel(stamp_own, stamp_below, stamp_above, own, below, above, tiles):
+def gather_kernel(stamps, to_own, to_flip, to_next, to_far):
     visit = lax.axis_index("visit")
-    base = (visit // PLANE) * PLANE
-    hits = [entries[0, 0] - base for entries in (own, below, above)]
-    hits[1] = jnp.where(visit >= PLANE, hits[1], -1)
-    hits[2] = jnp.where(visit < lax.axis_size("visit") - PLANE, hits[2], -1)
-    for tile in range(PLANE):
-        total = jnp.zeros((ROWS, COLS), jnp.float32)
-        count = jnp.float32(0.0)
-        for hit, stamp in zip(hits, (stamp_own, stamp_below, stamp_above)):
-            total = total + jnp.where(hit == tile, stamp[...], 0.0)
-            count = count + jnp.where(hit == tile, 1.0, 0.0)
+    even = lax.rem(visit // LINE, 2) == 0
+    low = lax.rem(visit, LINE) < LINE // 2
+    targets = (
+        visit,
+        jnp.where(even, visit + LINE, visit - LINE),
+        jnp.where(even, visit - LINE, visit + LINE),
+        jnp.where(low, visit + 2 * LINE, visit - 2 * LINE),
+    )
+    for target, out in zip(targets, (to_own, to_flip, to_next, to_far)):
+        number = target.astype(jnp.float32)
+        hits = [stamps[place, TALL:, :] == number for place in range(LINE)]
+        count = jnp.zeros((NOTED - TALL, BLOCK), jnp.float32)
+        for hit in hits:
+            count = count + jnp.where(hit, 1.0, 0.0)
+        out[TALL:, :] = count
         for block in range(BLOCKS):
-            tiles[tile, block * ROWS : (block + 1) * ROWS, :] = total[
-                :, block * BLOCK : (block + 1) * BLOCK
-            ]
-        tiles[tile, TALL:, :] = jnp.full((8, BLOCK), count, jnp.float32)
-
-
-def gather(stamps, own, below, above):
+            rows = slice(block * ROWS, (block + 1) * ROWS)
+            total = jnp.zeros((ROWS, BLOCK), jnp.float32)
+            for place in range(LINE):
+                total = total + jnp.where(hits[place][:1], stamps[place, rows, :], 0.0)
+            out[rows, :] = total
+
+
+def gather(stamps):
+    shape = jax.ShapeDtypeStruct((NOTED, BLOCK), jnp.float32)
     return pl.pallas_call(
         gather_kernel,
-        out_shape=jax.ShapeDtypeStruct((PLANE, TALL + 8, BLOCK), jnp.float32),
-        in_specs=[VMEM] * 3 + [SMEM] * 3,
-        out_specs=VMEM,
+        out_shape=(shape,) * 4,
+        in_specs=[VMEM],
+        out_specs=(VMEM,) * 4,
         compiler_params=pltpu.CompilerParams(vmem_limit_bytes=LIMIT),
         name="gather",
-    )(*stamps, own, below, above)
-
-
-def mean_kernel(parts, coadd):
-    count = parts[0, TALL:, :]
-    for index in range(1, PLANE):
-        count = count + parts[index, TALL:, :]
+    )(stamps)
+
+
+def mean_kernel(part_a, part_b, part_c, part_d, coadd):
+    parts = (part_a, part_b, part_c, part_d)
+    count = sum(part[TALL:, :] for part in parts)
     count = jnp.maximum(count[:1], 1.0)
     for block in range(BLOCKS):
         rows = slice(block * ROWS, (block + 1) * ROWS)
-        total = parts[0, rows, :]
-        for index in range(1, PLANE):
-            total = total + parts[index, rows, :]
+        total = sum(part[rows, :] for part in parts)
         coadd[:, block * BLOCK : (block + 1) * BLOCK] = total / count
 
 
-def mean(parts):
+def mean(*parts):
     return pl.pallas_call(
         mean_kernel,
         out_shape=jax.ShapeDtypeStruct((ROWS, COLS), jnp.float32),
-        in_specs=[VMEM],
+        in_specs=[VMEM] * 4,
         out_specs=VMEM,
         compiler_params=pltpu.CompilerParams(vmem_limit_bytes=LIMIT),
         name="mean",
-    )(parts)
+    )(*parts)
 
 
 def shards(template, science, inverse_variance, intersections):
@@ -356,12 +373,19 @@
         (piece_own, from_above, from_below), science[0, 0], inverse_variance[0, 0], own
     )
     grams = lax.all_gather(gram, "patch")
-    difference, placed = solve(grams, planes, own)
-    stamp_below = lax.ppermute(placed, "visit", upward)
-    stamp_above = lax.ppermute(placed, "visit", downward)
-    tiles = gather((placed, stamp_below, stamp_above), own, below, above)
-    parts = lax.all_to_all(tiles, "visit", 0, 0, axis_index_groups=groups)
-    return (difference[None, None], mean(parts)[None])
+    difference, stamps = solve(grams, planes, own)
+    lines = [list(range(first, first + LINE)) for first in range(0, visits, LINE)]
+    to_own, to_flip, to_next, to_far = gather(
+        lax.all_to_all(stamps, "visit", 0, 0, axis_index_groups=lines)
+    )
+    flip = [(i, i ^ LINE) for i in range(visits)]
+    following = [(i, ((i + LINE) ^ LINE) - LINE) for i in range(LINE, visits - LINE)]
+    far = [(i, i + 2 * LINE if i % LINE < LINE // 2 else i - 2 * LINE) for i in range(visits)]
+    far = [(source, target) for source, target in far if 0 <= target < visits]
+    from_far = lax.ppermute(to_far, "visit", far)
+    from_next = lax.ppermute(to_next, "visit", following)
+    from_flip = lax.ppermute(to_flip, "visit", flip)
+    return (difference[None, None], mean(to_own, from_flip, from_next, from_far)[None])
 
 
 def solution(mesh):

time: 86.5 us -> 85.6 us (0.990)
  blocking collectives: 27.5 us -> 18.7 us
  starting transfers between devices: 25 us -> 29.7 us
  local copies, waits for them, and re-layouts: 0.92 us -> 4.5 us
    all_to_all x1, blocking collectives: 22.2 us -> 13.4 us  [shards(): lax.all_to_all(stamps, 'visit', 0, 0, axis_index_groups=lines)]
    ppermute x2 -> x3, starting transfers between devices: 5.83 us -> 10.7 us  [the longest x1 4.14 us: shards(): from_far = lax.ppermute(to_far, 'visit', far)]
    unnamed x14, local copies, waits for them, and re-layouts: 0.92 us -> 4.5 us
    ppermute x2 -> x3, waiting for transfers between devices: 4.91 us -> 5.07 us  [the longest x1 5.07 us: shards(): from_next = lax.ppermute(to_next, 'visit', following)]
  transfers between devices with their start and end apart: 7 -> 8, of which waited for: 6 -> 5; matrix products, arithmetic and copies ran while one was open for 0% -> 0% of each run, Pallas kernels for 0% -> 0%
where the time goes in v4:
time: 85.6 us; the launch traced here: 85.1 us
  starting transfers between devices  29.7 us (35%)
  waiting for transfers between devices  21.7 us (25%)
  blocking collectives  18.7 us (22%)
  Pallas kernels  9.77 us (11%)
  local copies, waits for them, and re-layouts  4.5 us (5%)
    all_to_all x1, blocking collectives, shards(): lax.all_to_all(stamps, 'visit', 0, 0, axis_index_groups=lines)  13.4 us
    all_to_all x1, starting transfers between devices, shards(): lax.all_to_all(spread(template[0]), 'visit', 0, 0, axis_index_groups=groups)  6.93 us
    ppermute x1, waiting for transfers between devices, shards(): from_below = lax.ppermute(piece_up, 'visit', upward)  5.34 us
    all_gather x1, blocking collectives, shards(): grams = lax.all_gather(gram, 'patch')  5.25 us
    ppermute x1, waiting for transfers between devices, shards(): from_next = lax.ppermute(to_next, 'visit', following)  5.07 us
    all_to_all x1, waiting for transfers between devices, shards(): lax.all_to_all(spread(template[0]), 'visit', 0, 0, axis_index_groups=groups)  4.94 us
    ppermute x1, waiting for transfers between devices, shards(): below = lax.ppermute(own, 'visit', upward)  4.84 us
    unnamed x14, local copies, waits for them, and re-layouts  4.5 us
  transfers between devices with their start and end apart: 8, of which 5 were waited for; matrix products, arithmetic and copies ran while one was open for 0% of the time, Pallas kernels for 0%

profile of v4, /device:TPU:384, one launch (start us, length us, event | category | flops | bytes accessed | tf_op | source)
XLA Modules:
  0.0 85.1 jit_solution(4993158280260496129)
XLA Ops:
  0.7 1.0 %copy-done.3 = f32[1,64,512]{2,1,0:T(8,128)S(1)} copy-done((f32[1,64,512]{2,1,0:T(8,128)S(1)}, f32[1,64,512]{2,1,0:T(8,128)}, u32[]{:S(2)}) %copy-start.3) | copy-done | bytes 131096
  1.7 1.0 %spread.1 = f32[8,256,128]{2,1,0:T(8,128)} custom-call(f32[64,512]{1,0:T(8,128)S(1)} %bitcast.8), custom_call_target="tpu_custom_call" | custom-call | tf_op jit(solution)/shard_map/spread/pallas_call | solution.py:116
  2.7 6.9 %all-to-all-start = ((f32[8,256,128]{2,1,0:T(8,128)}), f32[8,256,128]{2,1,0:T(8,128)S(1)}, u32[]{:S(2)}, u32[]{:S(2)}) async-start(f32[8,256,128]{2,1,0:T(8,128)} %spread.1), calls=%async_computation | async-start | bytes 2097152 | tf_op jit(solution)/shard_map/all_to_all | solution.py:368
  9.6 4.1 %collective-permute-start.1 = (s32[1,3]{1,0:T(1,128)}, s32[1,3]{1,0:T(1,128)S(1)}, u32[]{:S(2)}, u32[]{:S(2)}) collective-permute-start(s32[1,3]{1,0:T(1,128)} %bitcast.11), channel_id=1, source_target_pairs={{32,0},{36,4},{40,8},{44,12},{48,16},{52,20},{56,24},{60,28},{64,3... | collective-permute-start | bytes 44 | tf_op jit(solution)/shard_map/ppermute | solution.py:367
  13.8 1.9 %collective-permute-start = (s32[1,3]{1,0:T(1,128)}, s32[1,3]{1,0:T(1,128)S(1)}, u32[]{:S(2)}, u32[]{:S(2)}) collective-permute-start(s32[1,3]{1,0:T(1,128)} %bitcast.12), channel_id=1, source_target_pairs={{0,32},{4,36},{8,40},{12,44},{16,48},{20,52},{24,56},{28,60},{32,6... | collective-permute-start | bytes 44 | tf_op jit(solution)/shard_map/ppermute | solution.py:366
  15.7 4.8 %collective-permute-done.below = s32[1,3]{1,0:T(1,128)S(1)} collective-permute-done((s32[1,3]{1,0:T(1,128)}, s32[1,3]{1,0:T(1,128)S(1)}, u32[]{:S(2)}, u32[]{:S(2)}) %collective-permute-start) | collective-permute-done | bytes 44 | tf_op jit(solution)/shard_map/ppermute | solution.py:366
  20.6 4.9 %all-to-all-done.window = f32[8,256,128]{2,1,0:T(8,128)S(1)} async-done(((f32[8,256,128]{2,1,0:T(8,128)}), f32[8,256,128]{2,1,0:T(8,128)S(1)}, u32[]{:S(2)}, u32[]{:S(2)}) %all-to-all-start) | async-done | bytes 1048608 | tf_op jit(solution)/shard_map/all_to_all | solution.py:368
  26.1 0.8 serve.1
  26.9 4.1 %collective-permute-start.2 = (f32[96,512]{1,0:T(8,128)S(1)}, f32[96,512]{1,0:T(8,128)S(1)}, u32[]{:S(2)}, u32[]{:S(2)}) collective-permute-start(f32[96,512]{1,0:T(8,128)S(1)} %get-tuple-element.14), channel_id=1, source_target_pairs={{32,0},{36,4},{40,8},{44,12},{48,16},{52,20},{56,24},{60,28},{64,3... | collective-permute-start | bytes 589832 | tf_op jit(solution)/shard_map/ppermute | solution.py:370
  31.0 1.9 %collective-permute-start.3 = (f32[96,512]{1,0:T(8,128)S(1)}, f32[96,512]{1,0:T(8,128)S(1)}, u32[]{:S(2)}, u32[]{:S(2)}) collective-permute-start(f32[96,512]{1,0:T(8,128)S(1)} %get-tuple-element.15), channel_id=1, source_target_pairs={{0,32},{4,36},{8,40},{12,44},{16,48},{20,52},{24,56},{28,60},{32,6... | collective-permute-start | bytes 589832 | tf_op jit(solution)/shard_map/ppermute | solution.py:371
  33.0 1.5 %collective-permute-done.2.piece_b = f32[96,512]{1,0:T(8,128)S(1)} collective-permute-done((f32[96,512]{1,0:T(8,128)S(1)}, f32[96,512]{1,0:T(8,128)S(1)}, u32[]{:S(2)}, u32[]{:S(2)}) %collective-permute-start.2) | collective-permute-done | bytes 196640 | tf_op jit(solution)/shard_map/ppermute | solution.py:370
  34.5 5.3 %collective-permute-done.3.piece_c = f32[96,512]{1,0:T(8,128)S(1)} collective-permute-done((f32[96,512]{1,0:T(8,128)S(1)}, f32[96,512]{1,0:T(8,128)S(1)}, u32[]{:S(2)}, u32[]{:S(2)}) %collective-permute-start.3) | collective-permute-done | bytes 196640 | tf_op jit(solution)/shard_map/ppermute | solution.py:371
  39.8 1.0 %copy-done.2 = bf16[864,192]{1,0:T(8,128)(2,1)S(1)} copy-done((bf16[864,192]{1,0:T(8,128)(2,1)S(1)}, bf16[864,192]{1,0:T(8,128)(2,1)}, u32[]{:S(2)}) %copy-start.2) | copy-done | bytes 331800
  40.8 0.9 %copy-done.4 = f32[1,1,64,512]{3,2,1,0:T(8,128)S(1)} copy-done((f32[1,1,64,512]{3,2,1,0:T(8,128)S(1)}, f32[1,1,64,512]{3,2,1,0:T(8,128)}, u32[]{:S(2)}) %copy-start.4) | copy-done | bytes 131096
  41.7 0.9 %copy-done.5 = f32[1,1,64,512]{3,2,1,0:T(8,128)S(1)} copy-done((f32[1,1,64,512]{3,2,1,0:T(8,128)S(1)}, f32[1,1,64,512]{3,2,1,0:T(8,128)}, u32[]{:S(2)}) %copy-start.5) | copy-done | bytes 131096
  42.7 4.0 %basis.1 = (f32[9216,128]{1,0:T(8,128)S(1)}, f32[32,128]{1,0:T(8,128)S(1)}) custom-call(f32[96,512]{1,0:T(8,128)S(1)} %get-tuple-element.13.piece_a, f32[96,512]{1,0:T(8,128)S(1)} %collective-permute-done.2.piece_b, f32[96,512]{1,0:T(8,128)S(1)} %collective-permute-done.3.piece_c, f32[64,512]{1,0:T(8,128)S(1)} %bitcast.9, f32[64,512]{1,0:T(8,128)S(1)} %bitcast.10, ...), custom_call_target="tpu_custom_call" | custom-call | tf_op jit(solution)/shard_map/basis/pallas_call | solution.py:221
  46.6 5.2 %all-gather = f32[128,128]{1,0:T(8,128)S(1)} all-gather(f32[32,128]{1,0:T(8,128)S(1)} %get-tuple-element.16), channel_id=2, replica_groups=mesh['visit'=128,'patch'=4] {'patch'}, dimensions={0}, use_global_device_ids=true | all-gather | bytes 81920 | tf_op jit(solution)/shard_map/all_gather | solution.py:375
  51.9 3.2 %solve.1 = (f32[64,512]{1,0:T(8,128)}, f32[4,264,128]{2,1,0:T(8,128)S(1)}) custom-call(f32[4,32,128]{2,1,0:T(8,128)S(1)} %bitcast.7, f32[9216,128]{1,0:T(8,128)S(1)} %get-tuple-element.17.planes, s32[1,3]{1,0:T(1,128)S(1)} %bitcast.15), custom_call_target="tpu_custom_call" | custom-call | tf_op jit(solution)/shard_map/solve/pallas_call | solution.py:289
  55.0 13.4 %all_to_all.10.stamps = f32[4,264,128]{2,1,0:T(8,128)S(1)} all-to-all(f32[4,264,128]{2,1,0:T(8,128)S(1)} %get-tuple-element.19), channel_id=1, replica_groups={{0,4,8,12},{16,20,24,28},{32,36,40,44},{48,52,56,60},{64,68,72,76},{80,..., dimensions={0} | all-to-all | bytes 1081344 | tf_op jit(solution)/shard_map/all_to_all | solution.py:379
  68.6 3.9 %collective-permute-start.4 = (f32[264,128]{1,0:T(8,128)S(1)}, f32[264,128]{1,0:T(8,128)S(1)}, u32[]{:S(2)}, u32[]{:S(2)}) collective-permute-start(f32[264,128]{1,0:T(8,128)S(1)} %get-tuple-element.21), channel_id=1, source_target_pairs={{0,16},{4,20},{8,24},{12,28},{16,0},{20,4},{24,8},{28,12},{32,48},... | collective-permute-start | bytes 405512 | tf_op jit(solution)/shard_map/ppermute | solution.py:387
  72.6 2.6 %collective-permute-start.5 = (f32[264,128]{1,0:T(8,128)S(1)}, f32[264,128]{1,0:T(8,128)S(1)}, u32[]{:S(2)}, u32[]{:S(2)}) collective-permute-start(f32[264,128]{1,0:T(8,128)S(1)} %get-tuple-element.22), channel_id=1, source_target_pairs={{16,32},{20,36},{24,40},{28,44},{32,16},{36,20},{40,24},{44,28},{4... | collective-permute-start | bytes 405512 | tf_op jit(solution)/shard_map/ppermute | solution.py:386
  75.2 4.1 %collective-permute-start.6 = (f32[264,128]{1,0:T(8,128)S(1)}, f32[264,128]{1,0:T(8,128)S(1)}, u32[]{:S(2)}, u32[]{:S(2)}) collective-permute-start(f32[264,128]{1,0:T(8,128)S(1)} %get-tuple-element.23), channel_id=1, source_target_pairs={{0,32},{4,36},{16,48},{20,52},{32,64},{36,68},{40,8},{44,12},{48,8... | collective-permute-start | bytes 405512 | tf_op jit(solution)/shard_map/ppermute | solution.py:385
  79.4 5.1 %collective-permute-done.5.part_c = f32[264,128]{1,0:T(8,128)S(1)} collective-permute-done((f32[264,128]{1,0:T(8,128)S(1)}, f32[264,128]{1,0:T(8,128)S(1)}, u32[]{:S(2)}, u32[]{:S(2)}) %collective-permute-start.5) | collective-permute-done | bytes 135200 | tf_op jit(solution)/shard_map/ppermute | solution.py:386
  84.4 0.7 mean.1
  (14 shorter events, 0.8 us)
Async XLA Ops:
  0.6 39.2 %copy-start = (bf16[256,1408]{1,0:T(8,128)(2,1)S(1)}, bf16[256,1408]{1,0:T(8,128)(2,1)}, u32[]{:S(2)}) copy-start(bf16[256,1408]{1,0:T(8,128)(2,1)} %constant.7.clone.col_low) | copy-start | bytes 2162692
  0.6 39.2 %copy-start.1 = (bf16[256,1408]{1,0:T(8,128)(2,1)S(1)}, bf16[256,1408]{1,0:T(8,128)(2,1)}, u32[]{:S(2)}) copy-start(bf16[256,1408]{1,0:T(8,128)(2,1)} %constant.6.clone.col_high) | copy-start | bytes 2162692
  0.7 1.0 %copy-start.3 = (f32[1,64,512]{2,1,0:T(8,128)S(1)}, f32[1,64,512]{2,1,0:T(8,128)}, u32[]{:S(2)}) copy-start(f32[1,64,512]{2,1,0:T(8,128)} %param.7) | copy-start | bytes 393220
  2.7 22.8 %all-to-all-start = ((f32[8,256,128]{2,1,0:T(8,128)}), f32[8,256,128]{2,1,0:T(8,128)S(1)}, u32[]{:S(2)}, u32[]{:S(2)}) async-start(f32[8,256,128]{2,1,0:T(8,128)} %spread.1), calls=%async_computation | async-start | bytes 2097152 | tf_op jit(solution)/shard_map/all_to_all | solution.py:368
  9.6 6.1 %collective-permute-start.1 = (s32[1,3]{1,0:T(1,128)}, s32[1,3]{1,0:T(1,128)S(1)}, u32[]{:S(2)}, u32[]{:S(2)}) collective-permute-start(s32[1,3]{1,0:T(1,128)} %bitcast.11), channel_id=1, source_target_pairs={{32,0},{36,4},{40,8},{44,12},{48,16},{52,20},{56,24},{60,28},{64,3... | collective-permute-start | bytes 44 | tf_op jit(solution)/shard_map/ppermute | solution.py:367
  13.8 6.8 %collective-permute-start = (s32[1,3]{1,0:T(1,128)}, s32[1,3]{1,0:T(1,128)S(1)}, u32[]{:S(2)}, u32[]{:S(2)}) collective-permute-start(s32[1,3]{1,0:T(1,128)} %bitcast.12), channel_id=1, source_target_pairs={{0,32},{4,36},{8,40},{12,44},{16,48},{20,52},{24,56},{28,60},{32,6... | collective-permute-start | bytes 44 | tf_op jit(solution)/shard_map/ppermute | solution.py:366
  25.5 0.7 copy-start.6
  26.9 7.6 %collective-permute-start.2 = (f32[96,512]{1,0:T(8,128)S(1)}, f32[96,512]{1,0:T(8,128)S(1)}, u32[]{:S(2)}, u32[]{:S(2)}) collective-permute-start(f32[96,512]{1,0:T(8,128)S(1)} %get-tuple-element.14), channel_id=1, source_target_pairs={{32,0},{36,4},{40,8},{44,12},{48,16},{52,20},{56,24},{60,28},{64,3... | collective-permute-start | bytes 589832 | tf_op jit(solution)/shard_map/ppermute | solution.py:370
  31.0 8.8 %collective-permute-start.3 = (f32[96,512]{1,0:T(8,128)S(1)}, f32[96,512]{1,0:T(8,128)S(1)}, u32[]{:S(2)}, u32[]{:S(2)}) collective-permute-start(f32[96,512]{1,0:T(8,128)S(1)} %get-tuple-element.15), channel_id=1, source_target_pairs={{0,32},{4,36},{8,40},{12,44},{16,48},{20,52},{24,56},{28,60},{32,6... | collective-permute-start | bytes 589832 | tf_op jit(solution)/shard_map/ppermute | solution.py:371
  39.8 1.0 %copy-start.2 = (bf16[864,192]{1,0:T(8,128)(2,1)S(1)}, bf16[864,192]{1,0:T(8,128)(2,1)}, u32[]{:S(2)}) copy-start(bf16[864,192]{1,0:T(8,128)(2,1)} %constant.8.clone.row_table) | copy-start | bytes 995332
  40.8 0.9 %copy-start.4 = (f32[1,1,64,512]{3,2,1,0:T(8,128)S(1)}, f32[1,1,64,512]{3,2,1,0:T(8,128)}, u32[]{:S(2)}) copy-start(f32[1,1,64,512]{3,2,1,0:T(8,128)} %param.8) | copy-start | bytes 393220
  41.7 0.9 %copy-start.5 = (f32[1,1,64,512]{3,2,1,0:T(8,128)S(1)}, f32[1,1,64,512]{3,2,1,0:T(8,128)}, u32[]{:S(2)}) copy-start(f32[1,1,64,512]{3,2,1,0:T(8,128)} %param.9) | copy-start | bytes 393220
  68.6 10.7 %collective-permute-start.4 = (f32[264,128]{1,0:T(8,128)S(1)}, f32[264,128]{1,0:T(8,128)S(1)}, u32[]{:S(2)}, u32[]{:S(2)}) collective-permute-start(f32[264,128]{1,0:T(8,128)S(1)} %get-tuple-element.21), channel_id=1, source_target_pairs={{0,16},{4,20},{8,24},{12,28},{16,0},{20,4},{24,8},{28,12},{32,48},... | collective-permute-start | bytes 405512 | tf_op jit(solution)/shard_map/ppermute | solution.py:387
  72.6 11.9 %collective-permute-start.5 = (f32[264,128]{1,0:T(8,128)S(1)}, f32[264,128]{1,0:T(8,128)S(1)}, u32[]{:S(2)}, u32[]{:S(2)}) collective-permute-start(f32[264,128]{1,0:T(8,128)S(1)} %get-tuple-element.22), channel_id=1, source_target_pairs={{16,32},{20,36},{24,40},{28,44},{32,16},{36,20},{40,24},{44,28},{4... | collective-permute-start | bytes 405512 | tf_op jit(solution)/shard_map/ppermute | solution.py:386
  75.2 9.2 %collective-permute-start.6 = (f32[264,128]{1,0:T(8,128)S(1)}, f32[264,128]{1,0:T(8,128)S(1)}, u32[]{:S(2)}, u32[]{:S(2)}) collective-permute-start(f32[264,128]{1,0:T(8,128)S(1)} %get-tuple-element.23), channel_id=1, source_target_pairs={{0,32},{4,36},{16,48},{20,52},{32,64},{36,68},{40,8},{44,12},{48,8... | collective-permute-start | bytes 405512 | tf_op jit(solution)/shard_map/ppermute | solution.py:385

commit v5 on v4

--- a/solution.py
+++ b/solution.py
@@ -33,9 +33,11 @@
 DEGREES = (4, 2, 2)
 RIDGE = 0.01
 LIMIT = 32 * 1024 * 1024
-
-SMEM = pl.BlockSpec(memory_space=pltpu.SMEM)
+BESIDE = 5
+BESIDE_ROWS = -(-(NBASIS - 1) // BESIDE) * HALF
+
 VMEM = pl.BlockSpec(memory_space=pltpu.VMEM)
+HBM = pl.BlockSpec(memory_space=pltpu.HBM)
 
 
 def factor_table():
@@ -72,24 +74,28 @@
     return high, low
 
 
-def column_tables():
+def tables():
     table = factor_table()
     distance = np.arange(2 * BLOCK)[:, None] - np.arange(BLOCK)[None, :]
     bands = np.zeros((2 * BLOCK, NFACTORS, BLOCK), np.float32)
     for offset in range(2 * KHALF + 1):
         bands += table[None, :, offset, None] * (distance == offset)[:, None, :]
-    return split_constant(bands.reshape(2 * BLOCK, NFACTORS * BLOCK))
-
-
-def row_tables():
-    table = factor_table()
+    columns = split_constant(bands.reshape(2 * BLOCK, NFACTORS * BLOCK))
     distance = np.arange(DEPTH)[None, :] - np.arange(HALF)[:, None]
-    planes = [index for group in GROUPS for index in group]
-    bands = np.zeros((len(planes), HALF, DEPTH), np.float32)
+    chosen = [index for group in GROUPS for index in group]
+    bands = np.zeros((len(chosen), HALF, DEPTH), np.float32)
     for offset in range(2 * KHALF + 1):
-        bands += table[planes, offset][:, None, None] * (distance == offset)[None]
-    high, low = split_constant(bands.reshape(len(planes) * HALF, DEPTH))
-    return np.concatenate([high, high, low], axis=1)
+        bands += table[chosen, offset][:, None, None] * (distance == offset)[None]
+    high, low = split_constant(bands)
+    rows = np.zeros((BESIDE_ROWS, NFACTORS * BLOCK), ml_dtypes.bfloat16)
+    for plane, band in enumerate(np.concatenate([high, high, low], axis=2)):
+        row, lane = row_band_place(plane)
+        rows[row : row + HALF, lane : lane + 3 * DEPTH] = band
+    return np.concatenate([*columns, rows])
+
+
+def row_band_place(plane):
+    return plane // BESIDE * HALF, plane % BESIDE * 2 * BLOCK
 
 
 def split(values):
@@ -123,17 +129,46 @@
     )(tile)
 
 
-def serve_kernel(window, own, below, above, piece_own, piece_up, piece_down):
+def prepare_kernel(
+    own, below, above, science, weight, table,
+    requests, root, scaled_science, table_out,
+):
+    for index, entries in enumerate((own, below, above)):
+        requests[index : index + 1, :] = entries[...]
+    values = jnp.sqrt(weight[...])
+    root[...] = values
+    scaled_science[...] = values * science[...]
+    table_out[...] = table[...]
+
+
+def prepare(entries, science, weight, table):
+    shape = jax.ShapeDtypeStruct((ROWS, COLS), jnp.float32)
+    return pl.pallas_call(
+        prepare_kernel,
+        out_shape=(
+            jax.ShapeDtypeStruct((3, 3), jnp.int32),
+            shape,
+            shape,
+            jax.ShapeDtypeStruct(table.shape, table.dtype),
+        ),
+        in_specs=[VMEM] * 6,
+        out_specs=(VMEM,) * 4,
+        compiler_params=pltpu.CompilerParams(vmem_limit_bytes=LIMIT),
+        name="prepare",
+    )(*entries, science, weight, table)
+
+
+def serve_kernel(window, requests, piece_own, piece_up, piece_down):
     base = (lax.axis_index("visit") // PLANE) * PLANE
-    for entries, piece in ((own, piece_own), (below, piece_down), (above, piece_up)):
-        start = (entries[0, 0] - base) * ROWS + entries[0, 1] - KHALF
+    for index, piece in enumerate((piece_own, piece_down, piece_up)):
+        start = (requests[...][index, 0] - base) * ROWS + requests[...][index, 1] - KHALF
         first = lax.shift_right_arithmetic(start, 3)
         for part in range(SPAN // 8):
-            index = first + part
-            inside = jnp.logical_and(index >= 0, index < PLANE * ROWS // 8)
-            index = jnp.clip(index, 0, PLANE * ROWS // 8 - 1)
-            tile = lax.shift_right_logical(index, 3)
-            row = pl.multiple_of(lax.bitwise_and(index, 7) * 8, 8)
+            strip = first + part
+            inside = jnp.logical_and(strip >= 0, strip < PLANE * ROWS // 8)
+            strip = jnp.clip(strip, 0, PLANE * ROWS // 8 - 1)
+            tile = lax.shift_right_logical(strip, 3)
+            row = pl.multiple_of(lax.bitwise_and(strip, 7) * 8, 8)
             for block in range(BLOCKS):
                 rows = window[tile, pl.ds(block * ROWS + row, 8), :]
                 piece[8 * part : 8 * part + 8, block * BLOCK : (block + 1) * BLOCK] = jnp.where(
@@ -141,34 +176,35 @@
                 )
 
 
-def serve(window, own, below, above):
+def serve(window, requests):
     shape = jax.ShapeDtypeStruct((SPAN, COLS), jnp.float32)
     return pl.pallas_call(
         serve_kernel,
         out_shape=(shape, shape, shape),
-        in_specs=[VMEM, SMEM, SMEM, SMEM],
+        in_specs=[VMEM, VMEM],
         out_specs=(VMEM, VMEM, VMEM),
         compiler_params=pltpu.CompilerParams(vmem_limit_bytes=LIMIT),
         name="serve",
-    )(window, own, below, above)
+    )(window, requests)
 
 
 def basis_kernel(
-    piece_a, piece_b, piece_c, science, weight, col_high, col_low, row_table, entries,
+    piece_a, piece_b, piece_c, root, scaled_science, table, entries,
     planes, gram_out,
     high_rows, low_rows,
 ):
-    remainder = lax.bitwise_and(entries[0, 1] + SHIFT, 7)
+    remainder = lax.bitwise_and(entries[...][0, 1] + SHIFT, 7)
     rows = piece_a[...] + piece_b[...] + piece_c[...]
     rows = pltpu.roll(rows, lax.rem(SPAN - remainder, SPAN), axis=0)
     padded = jnp.concatenate([rows, jnp.zeros((SPAN, BLOCK), jnp.float32)], axis=1)
-    cutout = pltpu.roll(padded, KHALF - entries[0, 2], axis=1)
+    cutout = pltpu.roll(padded, KHALF - entries[...][0, 2], axis=1)
     cut_high, cut_low = split(cutout)
+    col_high, col_low = table[: 2 * BLOCK, :], table[2 * BLOCK : 4 * BLOCK, :]
     for block in range(COLS // BLOCK):
         cols = slice(block * BLOCK, (block + 2) * BLOCK)
         both = jnp.concatenate([cut_high[:, cols], cut_low[:, cols]], axis=0)
-        main = jnp.dot(both, col_high[...], preferred_element_type=jnp.float32)
-        rest = jnp.dot(cut_high[:, cols], col_low[...], preferred_element_type=jnp.float32)
+        main = jnp.dot(both, col_high, preferred_element_type=jnp.float32)
+        rest = jnp.dot(cut_high[:, cols], col_low, preferred_element_type=jnp.float32)
         across = main[:SPAN] + main[SPAN:] + rest
         across_high, across_low = split(across)
         for factor in range(NFACTORS):
@@ -176,23 +212,28 @@
             put = slice(block * BLOCK, (block + 1) * BLOCK)
             high_rows[factor, :, put] = across_high[:, take]
             low_rows[factor, :, put] = across_low[:, take]
-    root = jnp.sqrt(weight[...])
     first = 0
     for factor, group in enumerate(GROUPS):
-        table = row_table[first * HALF : (first + len(group)) * HALF, :]
+        bands = []
+        for member in range(len(group)):
+            row, lane = row_band_place(first + member)
+            row += 4 * BLOCK
+            bands.append(table[row : row + HALF, lane : lane + 3 * DEPTH])
+        bands = jnp.concatenate(bands, axis=0)
         for half in range(ROWS // HALF):
             take = slice(half * HALF, half * HALF + DEPTH)
             high = high_rows[factor, take, :]
             stacked = jnp.concatenate([high, low_rows[factor, take, :], high], axis=0)
-            out = jnp.dot(table, stacked, preferred_element_type=jnp.float32)
+            out = jnp.dot(bands, stacked, preferred_element_type=jnp.float32)
             for member in range(len(group)):
                 scaled = (
-                    out[member * HALF : (member + 1) * HALF] * root[half * HALF : (half + 1) * HALF]
+                    out[member * HALF : (member + 1) * HALF]
+                    * root[half * HALF : (half + 1) * HALF, :]
                 )
                 put_plane(planes, first + member, half * HALF, scaled)
         first += len(group)
-    put_plane(planes, NBASIS - 1, 0, root)
-    put_plane(planes, NBASIS, 0, root * science[...])
+    put_plane(planes, NBASIS - 1, 0, root[...])
+    put_plane(planes, NBASIS, 0, scaled_science[...])
     for slot in range(NBASIS + 1, SLOTS):
         put_plane(planes, slot, 0, jnp.zeros((ROWS, COLS), jnp.float32))
     def gram_step(chunk, total):
@@ -216,15 +257,14 @@
     )
 
 
-def basis(pieces, science, weight, entries):
-    col_high, col_low = column_tables()
+def basis(pieces, *operands):
     return pl.pallas_call(
         basis_kernel,
         out_shape=(
             jax.ShapeDtypeStruct((BLOCKS * SLOTS * PITCH, BLOCK), jnp.float32),
             jax.ShapeDtypeStruct((SLOTS, BLOCK), jnp.float32),
         ),
-        in_specs=[VMEM] * 8 + [SMEM],
+        in_specs=[VMEM] * 7,
         out_specs=(VMEM, VMEM),
         scratch_shapes=[
             pltpu.VMEM((NFACTORS, SPAN, COLS), jnp.bfloat16),
@@ -232,13 +272,10 @@
         ],
         compiler_params=pltpu.CompilerParams(vmem_limit_bytes=LIMIT),
         name="basis",
-    )(
-        *pieces, science, weight, jnp.asarray(col_high), jnp.asarray(col_low),
-        jnp.asarray(row_tables()), entries,
-    )
-
-
-def solve_kernel(grams, planes, entries, difference, stamps):
+    )(*pieces, *operands)
+
+
+def solve_kernel(grams, planes, entries, difference_out, stamps, difference, sem):
     total = grams[0] + grams[1] + grams[2] + grams[3]
     cross = total[:, SLOTS : 2 * SLOTS]
     normal = total[:, :SLOTS] + cross + cross.T
@@ -267,7 +304,9 @@
             at = (block * SLOTS + plane) * PITCH
             total = total - factor * planes[at : at + ROWS, :]
         difference[:, block * BLOCK : (block + 1) * BLOCK] = total
-    row_move, col_move = entries[0, 1], entries[0, 2]
+    copy = pltpu.make_async_copy(difference, difference_out, sem)
+    copy.start()
+    row_move, col_move = entries[...][0, 1], entries[...][0, 2]
     moved = pltpu.roll(difference[...], lax.rem(row_move + ROWS, ROWS), axis=0)
     moved = pltpu.roll(moved, lax.rem(col_move + COLS, COLS), axis=1)
     from_row = lax.broadcasted_iota(jnp.int32, (ROWS, COLS), 0) - row_move
@@ -275,14 +314,15 @@
     inside = (from_row >= 0) & (from_row < ROWS) & (from_col >= 0) & (from_col < COLS)
     placed = jnp.where(inside, moved, 0.0)
     for place in range(LINE):
-        mine = lax.bitwise_and(entries[0, 0], LINE - 1) == place
+        mine = lax.bitwise_and(entries[...][0, 0], LINE - 1) == place
         for block in range(BLOCKS):
             stamps[place, block * ROWS : (block + 1) * ROWS, :] = jnp.where(
                 mine, placed[:, block * BLOCK : (block + 1) * BLOCK], 0.0
             )
         stamps[place, TALL:, :] = jnp.full(
-            (NOTED - TALL, BLOCK), entries[0, 0].astype(jnp.float32), jnp.float32
+            (NOTED - TALL, BLOCK), entries[...][0, 0].astype(jnp.float32), jnp.float32
         )
+    copy.wait()
 
 
 def solve(grams, planes, entries):
@@ -292,8 +332,9 @@
             jax.ShapeDtypeStruct((ROWS, COLS), jnp.float32),
             jax.ShapeDtypeStruct((LINE, NOTED, BLOCK), jnp.float32),
         ),
-        in_specs=[VMEM, VMEM, SMEM],
-        out_specs=(VMEM, VMEM),
+        in_specs=[VMEM, VMEM, VMEM],
+        out_specs=(HBM, VMEM),
+        scratch_shapes=[pltpu.VMEM((ROWS, COLS), jnp.float32), pltpu.SemaphoreType.DMA],
         compiler_params=pltpu.CompilerParams(vmem_limit_bytes=LIMIT),
         name="solve",
     )(grams, planes, entries)
@@ -365,15 +406,16 @@
     own = intersections[0]
     below = lax.ppermute(own, "visit", upward)
     above = lax.ppermute(own, "visit", downward)
+    requests, *prepared = prepare(
+        (own, below, above), science[0, 0], inverse_variance[0, 0], jnp.asarray(tables())
+    )
     window = lax.all_to_all(spread(template[0]), "visit", 0, 0, axis_index_groups=groups)
-    piece_own, piece_up, piece_down = serve(window, own, below, above)
+    piece_own, piece_up, piece_down = serve(window, requests)
     from_above = lax.ppermute(piece_down, "visit", downward)
     from_below = lax.ppermute(piece_up, "visit", upward)
-    planes, gram = basis(
-        (piece_own, from_above, from_below), science[0, 0], inverse_variance[0, 0], own
-    )
+    planes, gram = basis((piece_own, from_above, from_below), *prepared, requests)
     grams = lax.all_gather(gram, "patch")
-    difference, stamps = solve(grams, planes, own)
+    difference, stamps = solve(grams, planes, requests)
     lines = [list(range(first, first + LINE)) for first in range(0, visits, LINE)]
     to_own, to_flip, to_next, to_far = gather(
         lax.all_to_all(stamps, "visit", 0, 0, axis_index_groups=lines)

time: 85.6 us -> 81.2 us (0.949)
  waiting for transfers between devices: 21.7 us -> 18.7 us
  Pallas kernels: 9.77 us -> 8.48 us
    all_to_all x1, waiting for transfers between devices: 4.94 us -> 2.09 us  [shards(): lax.all_to_all(spread(template[0]), 'visit', 0, 0, axis_index_groups=groups)]
    unnamed x14 -> x16, local copies, waits for them, and re-layouts: 4.5 us -> 4.38 us
where the time goes in v5:
time: 81.2 us; the launch traced here: 80.8 us
  starting transfers between devices  29.7 us (37%)
  waiting for transfers between devices  18.7 us (23%)
  blocking collectives  18.7 us (23%)
  Pallas kernels  8.48 us (10%)
  local copies, waits for them, and re-layouts  4.38 us (5%)
    all_to_all x1, blocking collectives, shards(): lax.all_to_all(stamps, 'visit', 0, 0, axis_index_groups=lines)  13.4 us
    all_to_all x1, starting transfers between devices, shards(): lax.all_to_all(spread(template[0]), 'visit', 0, 0, axis_index_groups=groups)  6.93 us
    ppermute x1, waiting for transfers between devices, shards(): from_below = lax.ppermute(piece_up, 'visit', upward)  5.34 us
    all_gather x1, blocking collectives, shards(): grams = lax.all_gather(gram, 'patch')  5.25 us
    ppermute x1, waiting for transfers between devices, shards(): from_next = lax.ppermute(to_next, 'visit', following)  5.06 us
    ppermute x1, waiting for transfers between devices, shards(): below = lax.ppermute(own, 'visit', upward)  4.71 us
    unnamed x16, local copies, waits for them, and re-layouts  4.38 us
    ppermute x1, starting transfers between devices, shards(): from_far = lax.ppermute(to_far, 'visit', far)  4.14 us
  transfers between devices with their start and end apart: 8, of which 5 were waited for; matrix products, arithmetic and copies ran while one was open for 0% of the time, Pallas kernels for 0%

profile of v5, /device:TPU:384, one launch (start us, length us, event | category | flops | bytes accessed | tf_op | source)
XLA Modules:
  0.0 80.8 jit_solution(12697714418519911317)
XLA Ops:
  0.7 0.9 %copy-done.1 = f32[1,64,512]{2,1,0:T(8,128)S(1)} copy-done((f32[1,64,512]{2,1,0:T(8,128)S(1)}, f32[1,64,512]{2,1,0:T(8,128)}, u32[]{:S(2)}) %copy-start.1) | copy-done | bytes 131096
  1.6 1.1 %spread.1 = f32[8,256,128]{2,1,0:T(8,128)} custom-call(f32[64,512]{1,0:T(8,128)S(1)} %bitcast.8), custom_call_target="tpu_custom_call" | custom-call | tf_op jit(solution)/shard_map/spread/pallas_call | solution.py:122
  2.6 6.9 %all-to-all-start = ((f32[8,256,128]{2,1,0:T(8,128)}), f32[8,256,128]{2,1,0:T(8,128)S(1)}, u32[]{:S(2)}, u32[]{:S(2)}) async-start(f32[8,256,128]{2,1,0:T(8,128)} %spread.1), calls=%async_computation | async-start | bytes 2097152 | tf_op jit(solution)/shard_map/all_to_all | solution.py:412
  9.5 4.1 %collective-permute-start.1 = (s32[1,3]{1,0:T(1,128)S(1)}, s32[1,3]{1,0:T(1,128)S(1)}, u32[]{:S(2)}, u32[]{:S(2)}) collective-permute-start(s32[1,3]{1,0:T(1,128)S(1)} %bitcast.11), channel_id=1, source_target_pairs={{32,0},{36,4},{40,8},{44,12},{48,16},{52,20},{56,24},{60,28},{64,3... | collective-permute-start | bytes 44 | tf_op jit(solution)/shard_map/ppermute | solution.py:408
  13.7 1.9 %collective-permute-start = (s32[1,3]{1,0:T(1,128)S(1)}, s32[1,3]{1,0:T(1,128)S(1)}, u32[]{:S(2)}, u32[]{:S(2)}) collective-permute-start(s32[1,3]{1,0:T(1,128)S(1)} %bitcast.12), channel_id=1, source_target_pairs={{0,32},{4,36},{8,40},{12,44},{16,48},{20,52},{24,56},{28,60},{32,6... | collective-permute-start | bytes 44 | tf_op jit(solution)/shard_map/ppermute | solution.py:407
  15.6 4.7 %collective-permute-done.below = s32[1,3]{1,0:T(1,128)S(1)} collective-permute-done((s32[1,3]{1,0:T(1,128)S(1)}, s32[1,3]{1,0:T(1,128)S(1)}, u32[]{:S(2)}, u32[]{:S(2)}) %collective-permute-start) | collective-permute-done | bytes 44 | tf_op jit(solution)/shard_map/ppermute | solution.py:407
  20.3 1.6 %copy-done = bf16[704,1408]{1,0:T(8,128)(2,1)S(1)} copy-done((bf16[704,1408]{1,0:T(8,128)(2,1)S(1)}, bf16[704,1408]{1,0:T(8,128)(2,1)}, u32[]{:S(2)}) %copy-start) | copy-done | bytes 1982488
  21.9 0.7 copy-done.7
  22.7 0.6 copy-done.4
  23.3 2.1 %all-to-all-done.window = f32[8,256,128]{2,1,0:T(8,128)S(1)} async-done(((f32[8,256,128]{2,1,0:T(8,128)}), f32[8,256,128]{2,1,0:T(8,128)S(1)}, u32[]{:S(2)}, u32[]{:S(2)}) %all-to-all-start) | async-done | bytes 1048608 | tf_op jit(solution)/shard_map/all_to_all | solution.py:412
  25.4 0.7 copy-done.5
  26.4 4.1 %collective-permute-start.2 = (f32[96,512]{1,0:T(8,128)S(1)}, f32[96,512]{1,0:T(8,128)S(1)}, u32[]{:S(2)}, u32[]{:S(2)}) collective-permute-start(f32[96,512]{1,0:T(8,128)S(1)} %get-tuple-element.19), channel_id=1, source_target_pairs={{32,0},{36,4},{40,8},{44,12},{48,16},{52,20},{56,24},{60,28},{64,3... | collective-permute-start | bytes 589832 | tf_op jit(solution)/shard_map/ppermute | solution.py:414
  30.5 1.9 %collective-permute-start.3 = (f32[96,512]{1,0:T(8,128)S(1)}, f32[96,512]{1,0:T(8,128)S(1)}, u32[]{:S(2)}, u32[]{:S(2)}) collective-permute-start(f32[96,512]{1,0:T(8,128)S(1)} %get-tuple-element.20), channel_id=1, source_target_pairs={{0,32},{4,36},{8,40},{12,44},{16,48},{20,52},{24,56},{28,60},{32,6... | collective-permute-start | bytes 589832 | tf_op jit(solution)/shard_map/ppermute | solution.py:415
  32.4 1.5 %collective-permute-done.2.piece_b = f32[96,512]{1,0:T(8,128)S(1)} collective-permute-done((f32[96,512]{1,0:T(8,128)S(1)}, f32[96,512]{1,0:T(8,128)S(1)}, u32[]{:S(2)}, u32[]{:S(2)}) %collective-permute-start.2) | collective-permute-done | bytes 196640 | tf_op jit(solution)/shard_map/ppermute | solution.py:414
  33.9 5.3 %collective-permute-done.3.piece_c = f32[96,512]{1,0:T(8,128)S(1)} collective-permute-done((f32[96,512]{1,0:T(8,128)S(1)}, f32[96,512]{1,0:T(8,128)S(1)}, u32[]{:S(2)}, u32[]{:S(2)}) %collective-permute-start.3) | collective-permute-done | bytes 196640 | tf_op jit(solution)/shard_map/ppermute | solution.py:415
  39.3 3.5 %basis.1 = (f32[9216,128]{1,0:T(8,128)S(1)}, f32[32,128]{1,0:T(8,128)S(1)}) custom-call(f32[96,512]{1,0:T(8,128)S(1)} %get-tuple-element.18.piece_a, f32[96,512]{1,0:T(8,128)S(1)} %collective-permute-done.2.piece_b, f32[96,512]{1,0:T(8,128)S(1)} %collective-permute-done.3.piece_c, f32[64,512]{1,0:T(8,128)S(1)} %get-tuple-element.21.root, ...), custom_call_target="tpu_custom_call" | custom-call | tf_op jit(solution)/shard_map/basis/pallas_call | solution.py:261
  42.8 5.2 %all-gather = f32[128,128]{1,0:T(8,128)S(1)} all-gather(f32[32,128]{1,0:T(8,128)S(1)} %get-tuple-element.24), channel_id=2, replica_groups=mesh['visit'=128,'patch'=4] {'patch'}, dimensions={0}, use_global_device_ids=true | all-gather | bytes 81920 | tf_op jit(solution)/shard_map/all_gather | solution.py:417
  48.0 2.6 %solve.1 = (f32[64,512]{1,0:T(8,128)}, f32[4,264,128]{2,1,0:T(8,128)S(1)}) custom-call(f32[4,32,128]{2,1,0:T(8,128)S(1)} %bitcast.7, f32[9216,128]{1,0:T(8,128)S(1)} %get-tuple-element.25.planes, s32[3,3]{1,0:T(4,128)S(1)} %copy-done.5), custom_call_target="tpu_custom_call" | custom-call | tf_op jit(solution)/shard_map/solve/pallas_call | solution.py:329
  50.6 13.4 %all_to_all.10.stamps = f32[4,264,128]{2,1,0:T(8,128)S(1)} all-to-all(f32[4,264,128]{2,1,0:T(8,128)S(1)} %get-tuple-element.27), channel_id=1, replica_groups={{0,4,8,12},{16,20,24,28},{32,36,40,44},{48,52,56,60},{64,68,72,76},{80,..., dimensions={0} | all-to-all | bytes 1081344 | tf_op jit(solution)/shard_map/all_to_all | solution.py:421
  64.2 3.9 %collective-permute-start.4 = (f32[264,128]{1,0:T(8,128)S(1)}, f32[264,128]{1,0:T(8,128)S(1)}, u32[]{:S(2)}, u32[]{:S(2)}) collective-permute-start(f32[264,128]{1,0:T(8,128)S(1)} %get-tuple-element.29), channel_id=1, source_target_pairs={{0,16},{4,20},{8,24},{12,28},{16,0},{20,4},{24,8},{28,12},{32,48},... | collective-permute-start | bytes 405512 | tf_op jit(solution)/shard_map/ppermute | solution.py:429
  68.2 2.6 %collective-permute-start.5 = (f32[264,128]{1,0:T(8,128)S(1)}, f32[264,128]{1,0:T(8,128)S(1)}, u32[]{:S(2)}, u32[]{:S(2)}) collective-permute-start(f32[264,128]{1,0:T(8,128)S(1)} %get-tuple-element.30), channel_id=1, source_target_pairs={{16,32},{20,36},{24,40},{28,44},{32,16},{36,20},{40,24},{44,28},{4... | collective-permute-start | bytes 405512 | tf_op jit(solution)/shard_map/ppermute | solution.py:428
  70.8 4.1 %collective-permute-start.6 = (f32[264,128]{1,0:T(8,128)S(1)}, f32[264,128]{1,0:T(8,128)S(1)}, u32[]{:S(2)}, u32[]{:S(2)}) collective-permute-start(f32[264,128]{1,0:T(8,128)S(1)} %get-tuple-element.31), channel_id=1, source_target_pairs={{0,32},{4,36},{16,48},{20,52},{32,64},{36,68},{40,8},{44,12},{48,8... | collective-permute-start | bytes 405512 | tf_op jit(solution)/shard_map/ppermute | solution.py:427
  75.0 5.1 %collective-permute-done.5.part_c = f32[264,128]{1,0:T(8,128)S(1)} collective-permute-done((f32[264,128]{1,0:T(8,128)S(1)}, f32[264,128]{1,0:T(8,128)S(1)}, u32[]{:S(2)}, u32[]{:S(2)}) %collective-permute-start.5) | collective-permute-done | bytes 135200 | tf_op jit(solution)/shard_map/ppermute | solution.py:428
  80.1 0.7 mean.1
  (17 shorter events, 0.6 us)
Async XLA Ops:
  0.6 8.9 %copy-start.6 = (s32[1,1,3]{2,1,0:T(1,128)S(1)}, s32[1,1,3]{2,1,0:T(1,128)}, u32[]{:S(2)}) copy-start(s32[1,1,3]{2,1,0:T(1,128)} %param.8) | copy-start | bytes 40
  0.6 0.9 %copy-start.1 = (f32[1,64,512]{2,1,0:T(8,128)S(1)}, f32[1,64,512]{2,1,0:T(8,128)}, u32[]{:S(2)}) copy-start(f32[1,64,512]{2,1,0:T(8,128)} %param.5) | copy-start | bytes 393220
  1.6 18.8 %copy-start.2 = (f32[1,1,64,512]{3,2,1,0:T(8,128)S(1)}, f32[1,1,64,512]{3,2,1,0:T(8,128)}, u32[]{:S(2)}) copy-start(f32[1,1,64,512]{3,2,1,0:T(8,128)} %param.6) | copy-start | bytes 393220
  1.6 18.8 %copy-start.3 = (f32[1,1,64,512]{3,2,1,0:T(8,128)S(1)}, f32[1,1,64,512]{3,2,1,0:T(8,128)}, u32[]{:S(2)}) copy-start(f32[1,1,64,512]{3,2,1,0:T(8,128)} %param.7) | copy-start | bytes 393220
  2.6 22.8 %all-to-all-start = ((f32[8,256,128]{2,1,0:T(8,128)}), f32[8,256,128]{2,1,0:T(8,128)S(1)}, u32[]{:S(2)}, u32[]{:S(2)}) async-start(f32[8,256,128]{2,1,0:T(8,128)} %spread.1), calls=%async_computation | async-start | bytes 2097152 | tf_op jit(solution)/shard_map/all_to_all | solution.py:412
  9.5 6.1 %collective-permute-start.1 = (s32[1,3]{1,0:T(1,128)S(1)}, s32[1,3]{1,0:T(1,128)S(1)}, u32[]{:S(2)}, u32[]{:S(2)}) collective-permute-start(s32[1,3]{1,0:T(1,128)S(1)} %bitcast.11), channel_id=1, source_target_pairs={{32,0},{36,4},{40,8},{44,12},{48,16},{52,20},{56,24},{60,28},{64,3... | collective-permute-start | bytes 44 | tf_op jit(solution)/shard_map/ppermute | solution.py:408
  13.7 6.6 %collective-permute-start = (s32[1,3]{1,0:T(1,128)S(1)}, s32[1,3]{1,0:T(1,128)S(1)}, u32[]{:S(2)}, u32[]{:S(2)}) collective-permute-start(s32[1,3]{1,0:T(1,128)S(1)} %bitcast.12), channel_id=1, source_target_pairs={{0,32},{4,36},{8,40},{12,44},{16,48},{20,52},{24,56},{28,60},{32,6... | collective-permute-start | bytes 44 | tf_op jit(solution)/shard_map/ppermute | solution.py:407
  20.3 1.6 %copy-start = (bf16[704,1408]{1,0:T(8,128)(2,1)S(1)}, bf16[704,1408]{1,0:T(8,128)(2,1)}, u32[]{:S(2)}) copy-start(bf16[704,1408]{1,0:T(8,128)(2,1)} %constant.2.clone.table) | copy-start | bytes 5947396
  21.9 0.7 copy-start.7
  22.7 0.6 copy-start.4
  25.4 0.7 copy-start.5
  26.4 7.6 %collective-permute-start.2 = (f32[96,512]{1,0:T(8,128)S(1)}, f32[96,512]{1,0:T(8,128)S(1)}, u32[]{:S(2)}, u32[]{:S(2)}) collective-permute-start(f32[96,512]{1,0:T(8,128)S(1)} %get-tuple-element.19), channel_id=1, source_target_pairs={{32,0},{36,4},{40,8},{44,12},{48,16},{52,20},{56,24},{60,28},{64,3... | collective-permute-start | bytes 589832 | tf_op jit(solution)/shard_map/ppermute | solution.py:414
  30.5 8.8 %collective-permute-start.3 = (f32[96,512]{1,0:T(8,128)S(1)}, f32[96,512]{1,0:T(8,128)S(1)}, u32[]{:S(2)}, u32[]{:S(2)}) collective-permute-start(f32[96,512]{1,0:T(8,128)S(1)} %get-tuple-element.20), channel_id=1, source_target_pairs={{0,32},{4,36},{8,40},{12,44},{16,48},{20,52},{24,56},{28,60},{32,6... | collective-permute-start | bytes 589832 | tf_op jit(solution)/shard_map/ppermute | solution.py:415
  64.2 10.7 %collective-permute-start.4 = (f32[264,128]{1,0:T(8,128)S(1)}, f32[264,128]{1,0:T(8,128)S(1)}, u32[]{:S(2)}, u32[]{:S(2)}) collective-permute-start(f32[264,128]{1,0:T(8,128)S(1)} %get-tuple-element.29), channel_id=1, source_target_pairs={{0,16},{4,20},{8,24},{12,28},{16,0},{20,4},{24,8},{28,12},{32,48},... | collective-permute-start | bytes 405512 | tf_op jit(solution)/shard_map/ppermute | solution.py:429
  68.2 11.9 %collective-permute-start.5 = (f32[264,128]{1,0:T(8,128)S(1)}, f32[264,128]{1,0:T(8,128)S(1)}, u32[]{:S(2)}, u32[]{:S(2)}) collective-permute-start(f32[264,128]{1,0:T(8,128)S(1)} %get-tuple-element.30), channel_id=1, source_target_pairs={{16,32},{20,36},{24,40},{28,44},{32,16},{36,20},{40,24},{44,28},{4... | collective-permute-start | bytes 405512 | tf_op jit(solution)/shard_map/ppermute | solution.py:428
  70.8 9.2 %collective-permute-start.6 = (f32[264,128]{1,0:T(8,128)S(1)}, f32[264,128]{1,0:T(8,128)S(1)}, u32[]{:S(2)}, u32[]{:S(2)}) collective-permute-start(f32[264,128]{1,0:T(8,128)S(1)} %get-tuple-element.31), channel_id=1, source_target_pairs={{0,32},{4,36},{16,48},{20,52},{32,64},{36,68},{40,8},{44,12},{48,8... | collective-permute-start | bytes 405512 | tf_op jit(solution)/shard_map/ppermute | solution.py:427

commit v6 on v5

--- a/solution.py
+++ b/solution.py
@@ -129,39 +129,46 @@
     )(tile)
 
 
+def noted_number(sheet, index, part):
+    return sheet[2 * ROWS : 2 * ROWS + 1, :BLOCK][0, 3 * index + part].astype(jnp.int32)
+
+
 def prepare_kernel(
     own, below, above, science, weight, table,
-    requests, root, scaled_science, table_out,
+    sheet, table_out,
 ):
+    lane = lax.broadcasted_iota(jnp.int32, (8, COLS), 1)
+    noted = jnp.zeros((8, COLS), jnp.float32)
     for index, entries in enumerate((own, below, above)):
-        requests[index : index + 1, :] = entries[...]
+        for part in range(3):
+            number = entries[...][0, part].astype(jnp.float32)
+            noted = jnp.where(lane == 3 * index + part, number, noted)
+    sheet[2 * ROWS :, :] = noted
     values = jnp.sqrt(weight[...])
-    root[...] = values
-    scaled_science[...] = values * science[...]
+    sheet[:ROWS, :] = values
+    sheet[ROWS : 2 * ROWS, :] = values * science[...]
     table_out[...] = table[...]
 
 
 def prepare(entries, science, weight, table):
-    shape = jax.ShapeDtypeStruct((ROWS, COLS), jnp.float32)
     return pl.pallas_call(
         prepare_kernel,
         out_shape=(
-            jax.ShapeDtypeStruct((3, 3), jnp.int32),
-            shape,
-            shape,
+            jax.ShapeDtypeStruct((2 * ROWS + 8, COLS), jnp.float32),
             jax.ShapeDtypeStruct(table.shape, table.dtype),
         ),
         in_specs=[VMEM] * 6,
-        out_specs=(VMEM,) * 4,
+        out_specs=(VMEM,) * 2,
         compiler_params=pltpu.CompilerParams(vmem_limit_bytes=LIMIT),
         name="prepare",
     )(*entries, science, weight, table)
 
 
-def serve_kernel(window, requests, piece_own, piece_up, piece_down):
+def serve_kernel(window, sheet, piece_own, piece_up, piece_down):
     base = (lax.axis_index("visit") // PLANE) * PLANE
     for index, piece in enumerate((piece_own, piece_down, piece_up)):
-        start = (requests[...][index, 0] - base) * ROWS + requests[...][index, 1] - KHALF
+        tile_asked, row_move = noted_number(sheet, index, 0), noted_number(sheet, index, 1)
+        start = (tile_asked - base) * ROWS + row_move - KHALF
         first = lax.shift_right_arithmetic(start, 3)
         for part in range(SPAN // 8):
             strip = first + part
@@ -176,7 +183,7 @@
                 )
 
 
-def serve(window, requests):
+def serve(window, sheet):
     shape = jax.ShapeDtypeStruct((SPAN, COLS), jnp.float32)
     return pl.pallas_call(
         serve_kernel,
@@ -185,19 +192,19 @@
         out_specs=(VMEM, VMEM, VMEM),
         compiler_params=pltpu.CompilerParams(vmem_limit_bytes=LIMIT),
         name="serve",
-    )(window, requests)
+    )(window, sheet)
 
 
 def basis_kernel(
-    piece_a, piece_b, piece_c, root, scaled_science, table, entries,
+    piece_a, piece_b, piece_c, sheet, table,
     planes, gram_out,
     high_rows, low_rows,
 ):
-    remainder = lax.bitwise_and(entries[...][0, 1] + SHIFT, 7)
+    remainder = lax.bitwise_and(noted_number(sheet, 0, 1) + SHIFT, 7)
     rows = piece_a[...] + piece_b[...] + piece_c[...]
     rows = pltpu.roll(rows, lax.rem(SPAN - remainder, SPAN), axis=0)
     padded = jnp.concatenate([rows, jnp.zeros((SPAN, BLOCK), jnp.float32)], axis=1)
-    cutout = pltpu.roll(padded, KHALF - entries[...][0, 2], axis=1)
+    cutout = pltpu.roll(padded, KHALF - noted_number(sheet, 0, 2), axis=1)
     cut_high, cut_low = split(cutout)
     col_high, col_low = table[: 2 * BLOCK, :], table[2 * BLOCK : 4 * BLOCK, :]
     for block in range(COLS // BLOCK):
@@ -228,12 +235,12 @@
             for member in range(len(group)):
                 scaled = (
                     out[member * HALF : (member + 1) * HALF]
-                    * root[half * HALF : (half + 1) * HALF, :]
+                    * sheet[half * HALF : (half + 1) * HALF, :]
                 )
                 put_plane(planes, first + member, half * HALF, scaled)
         first += len(group)
-    put_plane(planes, NBASIS - 1, 0, root[...])
-    put_plane(planes, NBASIS, 0, scaled_science[...])
+    put_plane(planes, NBASIS - 1, 0, sheet[:ROWS, :])
+    put_plane(planes, NBASIS, 0, sheet[ROWS : 2 * ROWS, :])
     for slot in range(NBASIS + 1, SLOTS):
         put_plane(planes, slot, 0, jnp.zeros((ROWS, COLS), jnp.float32))
     def gram_step(chunk, total):
@@ -264,7 +271,7 @@
             jax.ShapeDtypeStruct((BLOCKS * SLOTS * PITCH, BLOCK), jnp.float32),
             jax.ShapeDtypeStruct((SLOTS, BLOCK), jnp.float32),
         ),
-        in_specs=[VMEM] * 7,
+        in_specs=[VMEM] * 5,
         out_specs=(VMEM, VMEM),
         scratch_shapes=[
             pltpu.VMEM((NFACTORS, SPAN, COLS), jnp.bfloat16),
@@ -275,7 +282,7 @@
     )(*pieces, *operands)
 
 
-def solve_kernel(grams, planes, entries, difference_out, stamps, difference, sem):
+def solve_kernel(grams, planes, sheet, difference_out, stamps, difference, sem):
     total = grams[0] + grams[1] + grams[2] + grams[3]
     cross = total[:, SLOTS : 2 * SLOTS]
     normal = total[:, :SLOTS] + cross + cross.T
@@ -306,7 +313,7 @@
         difference[:, block * BLOCK : (block + 1) * BLOCK] = total
     copy = pltpu.make_async_copy(difference, difference_out, sem)
     copy.start()
-    row_move, col_move = entries[...][0, 1], entries[...][0, 2]
+    tile, row_move, col_move = (noted_number(sheet, 0, part) for part in range(3))
     moved = pltpu.roll(difference[...], lax.rem(row_move + ROWS, ROWS), axis=0)
     moved = pltpu.roll(moved, lax.rem(col_move + COLS, COLS), axis=1)
     from_row = lax.broadcasted_iota(jnp.int32, (ROWS, COLS), 0) - row_move
@@ -314,18 +321,18 @@
     inside = (from_row >= 0) & (from_row < ROWS) & (from_col >= 0) & (from_col < COLS)
     placed = jnp.where(inside, moved, 0.0)
     for place in range(LINE):
-        mine = lax.bitwise_and(entries[...][0, 0], LINE - 1) == place
+        mine = lax.bitwise_and(tile, LINE - 1) == place
         for block in range(BLOCKS):
             stamps[place, block * ROWS : (block + 1) * ROWS, :] = jnp.where(
                 mine, placed[:, block * BLOCK : (block + 1) * BLOCK], 0.0
             )
         stamps[place, TALL:, :] = jnp.full(
-            (NOTED - TALL, BLOCK), entries[...][0, 0].astype(jnp.float32), jnp.float32
+            (NOTED - TALL, BLOCK), tile.astype(jnp.float32), jnp.float32
         )
     copy.wait()
 
 
-def solve(grams, planes, entries):
+def solve(grams, planes, sheet):
     return pl.pallas_call(
         solve_kernel,
         out_shape=(
@@ -337,7 +344,7 @@
         scratch_shapes=[pltpu.VMEM((ROWS, COLS), jnp.float32), pltpu.SemaphoreType.DMA],
         compiler_params=pltpu.CompilerParams(vmem_limit_bytes=LIMIT),
         name="solve",
-    )(grams, planes, entries)
+    )(grams, planes, sheet)
 
 
 def gather_kernel(stamps, to_own, to_flip, to_next, to_far):
@@ -406,16 +413,16 @@
     own = intersections[0]
     below = lax.ppermute(own, "visit", upward)
     above = lax.ppermute(own, "visit", downward)
-    requests, *prepared = prepare(
+    sheet, table = prepare(
         (own, below, above), science[0, 0], inverse_variance[0, 0], jnp.asarray(tables())
     )
     window = lax.all_to_all(spread(template[0]), "visit", 0, 0, axis_index_groups=groups)
-    piece_own, piece_up, piece_down = serve(window, requests)
+    piece_own, piece_up, piece_down = serve(window, sheet)
     from_above = lax.ppermute(piece_down, "visit", downward)
     from_below = lax.ppermute(piece_up, "visit", upward)
-    planes, gram = basis((piece_own, from_above, from_below), *prepared, requests)
+    planes, gram = basis((piece_own, from_above, from_below), sheet, table)
     grams = lax.all_gather(gram, "patch")
-    difference, stamps = solve(grams, planes, requests)
+    difference, stamps = solve(grams, planes, sheet)
     lines = [list(range(first, first + LINE)) for first in range(0, visits, LINE)]
     to_own, to_flip, to_next, to_far = gather(
         lax.all_to_all(stamps, "visit", 0, 0, axis_index_groups=lines)

time: 81.2 us -> 80.5 us (level)
  local copies, waits for them, and re-layouts: 4.38 us -> 3.37 us
    unnamed x16 -> x10, local copies, waits for them, and re-layouts: 4.38 us -> 3.37 us
where the time goes in v6:
time: 80.5 us; the launch traced here: 80.1 us
  starting transfers between devices  29.7 us (37%)
  waiting for transfers between devices  19 us (24%)
  blocking collectives  18.7 us (23%)
  Pallas kernels  8.5 us (11%)
  local copies, waits for them, and re-layouts  3.37 us (4%)
    all_to_all x1, blocking collectives, shards(): lax.all_to_all(stamps, 'visit', 0, 0, axis_index_groups=lines)  13.4 us
    all_to_all x1, starting transfers between devices, shards(): lax.all_to_all(spread(template[0]), 'visit', 0, 0, axis_index_groups=groups)  6.93 us
    ppermute x1, waiting for transfers between devices, shards(): from_below = lax.ppermute(piece_up, 'visit', upward)  5.34 us
    all_gather x1, blocking collectives, shards(): grams = lax.all_gather(gram, 'patch')  5.25 us
    ppermute x1, waiting for transfers between devices, shards(): from_next = lax.ppermute(to_next, 'visit', following)  5.07 us
    ppermute x1, waiting for transfers between devices, shards(): below = lax.ppermute(own, 'visit', upward)  4.71 us
    ppermute x1, starting transfers between devices, shards(): from_far = lax.ppermute(to_far, 'visit', far)  4.15 us
    ppermute x1, starting transfers between devices, shards(): above = lax.ppermute(own, 'visit', downward)  4.13 us
  transfers between devices with their start and end apart: 8, of which 5 were waited for; matrix products, arithmetic and copies ran while one was open for 0% of the time, Pallas kernels for 0%

profile of v6, /device:TPU:384, one launch (start us, length us, event | category | flops | bytes accessed | tf_op | source)
XLA Modules:
  0.0 80.1 jit_solution(17153119661951723438)
XLA Ops:
  0.6 0.9 %copy-done.1 = f32[1,64,512]{2,1,0:T(8,128)S(1)} copy-done((f32[1,64,512]{2,1,0:T(8,128)S(1)}, f32[1,64,512]{2,1,0:T(8,128)}, u32[]{:S(2)}) %copy-start.1) | copy-done | bytes 131096
  1.6 1.0 %spread.1 = f32[8,256,128]{2,1,0:T(8,128)} custom-call(f32[64,512]{1,0:T(8,128)S(1)} %bitcast.8), custom_call_target="tpu_custom_call" | custom-call | tf_op jit(solution)/shard_map/spread/pallas_call | solution.py:122
  2.6 6.9 %all-to-all-start = ((f32[8,256,128]{2,1,0:T(8,128)}), f32[8,256,128]{2,1,0:T(8,128)S(1)}, u32[]{:S(2)}, u32[]{:S(2)}) async-start(f32[8,256,128]{2,1,0:T(8,128)} %spread.1), calls=%async_computation | async-start | bytes 2097152 | tf_op jit(solution)/shard_map/all_to_all | solution.py:419
  9.5 4.1 %collective-permute-start.1 = (s32[1,3]{1,0:T(1,128)S(1)}, s32[1,3]{1,0:T(1,128)S(1)}, u32[]{:S(2)}, u32[]{:S(2)}) collective-permute-start(s32[1,3]{1,0:T(1,128)S(1)} %bitcast.11), channel_id=1, source_target_pairs={{32,0},{36,4},{40,8},{44,12},{48,16},{52,20},{56,24},{60,28},{64,3... | collective-permute-start | bytes 44 | tf_op jit(solution)/shard_map/ppermute | solution.py:415
  13.7 1.9 %collective-permute-start = (s32[1,3]{1,0:T(1,128)S(1)}, s32[1,3]{1,0:T(1,128)S(1)}, u32[]{:S(2)}, u32[]{:S(2)}) collective-permute-start(s32[1,3]{1,0:T(1,128)S(1)} %bitcast.12), channel_id=1, source_target_pairs={{0,32},{4,36},{8,40},{12,44},{16,48},{20,52},{24,56},{28,60},{32,6... | collective-permute-start | bytes 44 | tf_op jit(solution)/shard_map/ppermute | solution.py:414
  15.6 4.7 %collective-permute-done.below = s32[1,3]{1,0:T(1,128)S(1)} collective-permute-done((s32[1,3]{1,0:T(1,128)S(1)}, s32[1,3]{1,0:T(1,128)S(1)}, u32[]{:S(2)}, u32[]{:S(2)}) %collective-permute-start) | collective-permute-done | bytes 44 | tf_op jit(solution)/shard_map/ppermute | solution.py:414
  20.3 1.6 %copy-done = bf16[704,1408]{1,0:T(8,128)(2,1)S(1)} copy-done((bf16[704,1408]{1,0:T(8,128)(2,1)S(1)}, bf16[704,1408]{1,0:T(8,128)(2,1)}, u32[]{:S(2)}) %copy-start) | copy-done | bytes 1982488
  21.9 0.9 %copy-done.3 = f32[1,1,64,512]{3,2,1,0:T(8,128)S(1)} copy-done((f32[1,1,64,512]{3,2,1,0:T(8,128)S(1)}, f32[1,1,64,512]{3,2,1,0:T(8,128)}, u32[]{:S(2)}) %copy-start.3) | copy-done | bytes 131096
  22.8 0.2 prepare.1
  23.0 2.4 %all-to-all-done.window = f32[8,256,128]{2,1,0:T(8,128)S(1)} async-done(((f32[8,256,128]{2,1,0:T(8,128)}), f32[8,256,128]{2,1,0:T(8,128)S(1)}, u32[]{:S(2)}, u32[]{:S(2)}) %all-to-all-start) | async-done | bytes 1048608 | tf_op jit(solution)/shard_map/all_to_all | solution.py:419
  25.4 0.3 serve.1
  25.7 4.1 %collective-permute-start.2 = (f32[96,512]{1,0:T(8,128)S(1)}, f32[96,512]{1,0:T(8,128)S(1)}, u32[]{:S(2)}, u32[]{:S(2)}) collective-permute-start(f32[96,512]{1,0:T(8,128)S(1)} %get-tuple-element.17), channel_id=1, source_target_pairs={{32,0},{36,4},{40,8},{44,12},{48,16},{52,20},{56,24},{60,28},{64,3... | collective-permute-start | bytes 589832 | tf_op jit(solution)/shard_map/ppermute | solution.py:421
  29.8 1.9 %collective-permute-start.3 = (f32[96,512]{1,0:T(8,128)S(1)}, f32[96,512]{1,0:T(8,128)S(1)}, u32[]{:S(2)}, u32[]{:S(2)}) collective-permute-start(f32[96,512]{1,0:T(8,128)S(1)} %get-tuple-element.18), channel_id=1, source_target_pairs={{0,32},{4,36},{8,40},{12,44},{16,48},{20,52},{24,56},{28,60},{32,6... | collective-permute-start | bytes 589832 | tf_op jit(solution)/shard_map/ppermute | solution.py:422
  31.7 1.5 %collective-permute-done.2.piece_b = f32[96,512]{1,0:T(8,128)S(1)} collective-permute-done((f32[96,512]{1,0:T(8,128)S(1)}, f32[96,512]{1,0:T(8,128)S(1)}, u32[]{:S(2)}, u32[]{:S(2)}) %collective-permute-start.2) | collective-permute-done | bytes 196640 | tf_op jit(solution)/shard_map/ppermute | solution.py:421
  33.2 5.3 %collective-permute-done.3.piece_c = f32[96,512]{1,0:T(8,128)S(1)} collective-permute-done((f32[96,512]{1,0:T(8,128)S(1)}, f32[96,512]{1,0:T(8,128)S(1)}, u32[]{:S(2)}, u32[]{:S(2)}) %collective-permute-start.3) | collective-permute-done | bytes 196640 | tf_op jit(solution)/shard_map/ppermute | solution.py:422
  38.6 3.5 %basis.1 = (f32[9216,128]{1,0:T(8,128)S(1)}, f32[32,128]{1,0:T(8,128)S(1)}) custom-call(f32[96,512]{1,0:T(8,128)S(1)} %get-tuple-element.16.piece_a, f32[96,512]{1,0:T(8,128)S(1)} %collective-permute-done.2.piece_b, f32[96,512]{1,0:T(8,128)S(1)} %collective-permute-done.3.piece_c, f32[136,512]{1,0:T(8,128)S(1)} %get-tuple-element.15.sheet, ...), custom_call_target="tpu_custom_call" | custom-call | tf_op jit(solution)/shard_map/basis/pallas_call | solution.py:268
  42.1 5.2 %all-gather = f32[128,128]{1,0:T(8,128)S(1)} all-gather(f32[32,128]{1,0:T(8,128)S(1)} %get-tuple-element.20), channel_id=2, replica_groups=mesh['visit'=128,'patch'=4] {'patch'}, dimensions={0}, use_global_device_ids=true | all-gather | bytes 81920 | tf_op jit(solution)/shard_map/all_gather | solution.py:424
  47.3 2.6 %solve.1 = (f32[64,512]{1,0:T(8,128)}, f32[4,264,128]{2,1,0:T(8,128)S(1)}) custom-call(f32[4,32,128]{2,1,0:T(8,128)S(1)} %bitcast.7, f32[9216,128]{1,0:T(8,128)S(1)} %get-tuple-element.21.planes, f32[136,512]{1,0:T(8,128)S(1)} %get-tuple-element.15.sheet), custom_call_target="tpu_custom_call" | custom-call | tf_op jit(solution)/shard_map/solve/pallas_call | solution.py:336
  50.0 13.4 %all_to_all.10.stamps = f32[4,264,128]{2,1,0:T(8,128)S(1)} all-to-all(f32[4,264,128]{2,1,0:T(8,128)S(1)} %get-tuple-element.23), channel_id=1, replica_groups={{0,4,8,12},{16,20,24,28},{32,36,40,44},{48,52,56,60},{64,68,72,76},{80,..., dimensions={0} | all-to-all | bytes 1081344 | tf_op jit(solution)/shard_map/all_to_all | solution.py:428
  63.6 4.0 %collective-permute-start.4 = (f32[264,128]{1,0:T(8,128)S(1)}, f32[264,128]{1,0:T(8,128)S(1)}, u32[]{:S(2)}, u32[]{:S(2)}) collective-permute-start(f32[264,128]{1,0:T(8,128)S(1)} %get-tuple-element.25), channel_id=1, source_target_pairs={{0,16},{4,20},{8,24},{12,28},{16,0},{20,4},{24,8},{28,12},{32,48},... | collective-permute-start | bytes 405512 | tf_op jit(solution)/shard_map/ppermute | solution.py:436
  67.5 2.6 %collective-permute-start.5 = (f32[264,128]{1,0:T(8,128)S(1)}, f32[264,128]{1,0:T(8,128)S(1)}, u32[]{:S(2)}, u32[]{:S(2)}) collective-permute-start(f32[264,128]{1,0:T(8,128)S(1)} %get-tuple-element.26), channel_id=1, source_target_pairs={{16,32},{20,36},{24,40},{28,44},{32,16},{36,20},{40,24},{44,28},{4... | collective-permute-start | bytes 405512 | tf_op jit(solution)/shard_map/ppermute | solution.py:435
  70.2 4.1 %collective-permute-start.6 = (f32[264,128]{1,0:T(8,128)S(1)}, f32[264,128]{1,0:T(8,128)S(1)}, u32[]{:S(2)}, u32[]{:S(2)}) collective-permute-start(f32[264,128]{1,0:T(8,128)S(1)} %get-tuple-element.27), channel_id=1, source_target_pairs={{0,32},{4,36},{16,48},{20,52},{32,64},{36,68},{40,8},{44,12},{48,8... | collective-permute-start | bytes 405512 | tf_op jit(solution)/shard_map/ppermute | solution.py:434
  74.3 5.1 %collective-permute-done.5.part_c = f32[264,128]{1,0:T(8,128)S(1)} collective-permute-done((f32[264,128]{1,0:T(8,128)S(1)}, f32[264,128]{1,0:T(8,128)S(1)}, u32[]{:S(2)}, u32[]{:S(2)}) %collective-permute-start.5) | collective-permute-done | bytes 135200 | tf_op jit(solution)/shard_map/ppermute | solution.py:435
  79.4 0.7 mean.1
  (11 shorter events, 0.2 us)
Async XLA Ops:
  0.6 8.9 %copy-start.4 = (s32[1,1,3]{2,1,0:T(1,128)S(1)}, s32[1,1,3]{2,1,0:T(1,128)}, u32[]{:S(2)}) copy-start(s32[1,1,3]{2,1,0:T(1,128)} %param.8) | copy-start | bytes 40
  0.6 0.9 %copy-start.1 = (f32[1,64,512]{2,1,0:T(8,128)S(1)}, f32[1,64,512]{2,1,0:T(8,128)}, u32[]{:S(2)}) copy-start(f32[1,64,512]{2,1,0:T(8,128)} %param.5) | copy-start | bytes 393220
  1.6 18.8 %copy-start.2 = (f32[1,1,64,512]{3,2,1,0:T(8,128)S(1)}, f32[1,1,64,512]{3,2,1,0:T(8,128)}, u32[]{:S(2)}) copy-start(f32[1,1,64,512]{3,2,1,0:T(8,128)} %param.6) | copy-start | bytes 393220
  2.6 22.8 %all-to-all-start = ((f32[8,256,128]{2,1,0:T(8,128)}), f32[8,256,128]{2,1,0:T(8,128)S(1)}, u32[]{:S(2)}, u32[]{:S(2)}) async-start(f32[8,256,128]{2,1,0:T(8,128)} %spread.1), calls=%async_computation | async-start | bytes 2097152 | tf_op jit(solution)/shard_map/all_to_all | solution.py:419
  9.5 6.1 %collective-permute-start.1 = (s32[1,3]{1,0:T(1,128)S(1)}, s32[1,3]{1,0:T(1,128)S(1)}, u32[]{:S(2)}, u32[]{:S(2)}) collective-permute-start(s32[1,3]{1,0:T(1,128)S(1)} %bitcast.11), channel_id=1, source_target_pairs={{32,0},{36,4},{40,8},{44,12},{48,16},{52,20},{56,24},{60,28},{64,3... | collective-permute-start | bytes 44 | tf_op jit(solution)/shard_map/ppermute | solution.py:415
  13.7 6.6 %collective-permute-start = (s32[1,3]{1,0:T(1,128)S(1)}, s32[1,3]{1,0:T(1,128)S(1)}, u32[]{:S(2)}, u32[]{:S(2)}) collective-permute-start(s32[1,3]{1,0:T(1,128)S(1)} %bitcast.12), channel_id=1, source_target_pairs={{0,32},{4,36},{8,40},{12,44},{16,48},{20,52},{24,56},{28,60},{32,6... | collective-permute-start | bytes 44 | tf_op jit(solution)/shard_map/ppermute | solution.py:414
  20.3 1.6 %copy-start = (bf16[704,1408]{1,0:T(8,128)(2,1)S(1)}, bf16[704,1408]{1,0:T(8,128)(2,1)}, u32[]{:S(2)}) copy-start(bf16[704,1408]{1,0:T(8,128)(2,1)} %constant.2.clone.table) | copy-start | bytes 5947396
  21.9 0.9 %copy-start.3 = (f32[1,1,64,512]{3,2,1,0:T(8,128)S(1)}, f32[1,1,64,512]{3,2,1,0:T(8,128)}, u32[]{:S(2)}) copy-start(f32[1,1,64,512]{3,2,1,0:T(8,128)} %param.7) | copy-start | bytes 393220
  25.7 7.6 %collective-permute-start.2 = (f32[96,512]{1,0:T(8,128)S(1)}, f32[96,512]{1,0:T(8,128)S(1)}, u32[]{:S(2)}, u32[]{:S(2)}) collective-permute-start(f32[96,512]{1,0:T(8,128)S(1)} %get-tuple-element.17), channel_id=1, source_target_pairs={{32,0},{36,4},{40,8},{44,12},{48,16},{52,20},{56,24},{60,28},{64,3... | collective-permute-start | bytes 589832 | tf_op jit(solution)/shard_map/ppermute | solution.py:421
  29.8 8.8 %collective-permute-start.3 = (f32[96,512]{1,0:T(8,128)S(1)}, f32[96,512]{1,0:T(8,128)S(1)}, u32[]{:S(2)}, u32[]{:S(2)}) collective-permute-start(f32[96,512]{1,0:T(8,128)S(1)} %get-tuple-element.18), channel_id=1, source_target_pairs={{0,32},{4,36},{8,40},{12,44},{16,48},{20,52},{24,56},{28,60},{32,6... | collective-permute-start | bytes 589832 | tf_op jit(solution)/shard_map/ppermute | solution.py:422
  63.6 10.7 %collective-permute-start.4 = (f32[264,128]{1,0:T(8,128)S(1)}, f32[264,128]{1,0:T(8,128)S(1)}, u32[]{:S(2)}, u32[]{:S(2)}) collective-permute-start(f32[264,128]{1,0:T(8,128)S(1)} %get-tuple-element.25), channel_id=1, source_target_pairs={{0,16},{4,20},{8,24},{12,28},{16,0},{20,4},{24,8},{28,12},{32,48},... | collective-permute-start | bytes 405512 | tf_op jit(solution)/shard_map/ppermute | solution.py:436
  67.5 11.9 %collective-permute-start.5 = (f32[264,128]{1,0:T(8,128)S(1)}, f32[264,128]{1,0:T(8,128)S(1)}, u32[]{:S(2)}, u32[]{:S(2)}) collective-permute-start(f32[264,128]{1,0:T(8,128)S(1)} %get-tuple-element.26), channel_id=1, source_target_pairs={{16,32},{20,36},{24,40},{28,44},{32,16},{36,20},{40,24},{44,28},{4... | collective-permute-start | bytes 405512 | tf_op jit(solution)/shard_map/ppermute | solution.py:435
  70.2 9.2 %collective-permute-start.6 = (f32[264,128]{1,0:T(8,128)S(1)}, f32[264,128]{1,0:T(8,128)S(1)}, u32[]{:S(2)}, u32[]{:S(2)}) collective-permute-start(f32[264,128]{1,0:T(8,128)S(1)} %get-tuple-element.27), channel_id=1, source_target_pairs={{0,32},{4,36},{16,48},{20,52},{32,64},{36,68},{40,8},{44,12},{48,8... | collective-permute-start | bytes 405512 | tf_op jit(solution)/shard_map/ppermute | solution.py:434

commit v7 on v6

--- a/solution.py
+++ b/solution.py
@@ -129,20 +129,18 @@
     )(tile)
 
 
-def noted_number(sheet, index, part):
-    return sheet[2 * ROWS : 2 * ROWS + 1, :BLOCK][0, 3 * index + part].astype(jnp.int32)
+def noted_number(sheet, part):
+    return sheet[2 * ROWS : 2 * ROWS + 1, :BLOCK][0, part].astype(jnp.int32)
 
 
 def prepare_kernel(
-    own, below, above, science, weight, table,
+    entries, science, weight, table,
     sheet, table_out,
 ):
     lane = lax.broadcasted_iota(jnp.int32, (8, COLS), 1)
     noted = jnp.zeros((8, COLS), jnp.float32)
-    for index, entries in enumerate((own, below, above)):
-        for part in range(3):
-            number = entries[...][0, part].astype(jnp.float32)
-            noted = jnp.where(lane == 3 * index + part, number, noted)
+    for part in range(3):
+        noted = jnp.where(lane == part, entries[...][0, part].astype(jnp.float32), noted)
     sheet[2 * ROWS :, :] = noted
     values = jnp.sqrt(weight[...])
     sheet[:ROWS, :] = values
@@ -157,18 +155,19 @@
             jax.ShapeDtypeStruct((2 * ROWS + 8, COLS), jnp.float32),
             jax.ShapeDtypeStruct(table.shape, table.dtype),
         ),
-        in_specs=[VMEM] * 6,
+        in_specs=[VMEM] * 4,
         out_specs=(VMEM,) * 2,
         compiler_params=pltpu.CompilerParams(vmem_limit_bytes=LIMIT),
         name="prepare",
-    )(*entries, science, weight, table)
-
-
-def serve_kernel(window, sheet, piece_own, piece_up, piece_down):
+    )(entries, science, weight, table)
+
+
+def serve_kernel(window, sheet, below, above, piece_own, piece_up, piece_down):
     base = (lax.axis_index("visit") // PLANE) * PLANE
-    for index, piece in enumerate((piece_own, piece_down, piece_up)):
-        tile_asked, row_move = noted_number(sheet, index, 0), noted_number(sheet, index, 1)
-        start = (tile_asked - base) * ROWS + row_move - KHALF
+    own = (noted_number(sheet, 0), noted_number(sheet, 1))
+    others = [(entries[...][0, 0], entries[...][0, 1]) for entries in (below, above)]
+    for (asked, row_move), piece in zip((own, *others), (piece_own, piece_down, piece_up)):
+        start = (asked - base) * ROWS + row_move - KHALF
         first = lax.shift_right_arithmetic(start, 3)
         for part in range(SPAN // 8):
             strip = first + part
@@ -183,16 +182,16 @@
                 )
 
 
-def serve(window, sheet):
+def serve(window, sheet, below, above):
     shape = jax.ShapeDtypeStruct((SPAN, COLS), jnp.float32)
     return pl.pallas_call(
         serve_kernel,
         out_shape=(shape, shape, shape),
-        in_specs=[VMEM, VMEM],
+        in_specs=[VMEM] * 4,
         out_specs=(VMEM, VMEM, VMEM),
         compiler_params=pltpu.CompilerParams(vmem_limit_bytes=LIMIT),
         name="serve",
-    )(window, sheet)
+    )(window, sheet, below, above)
 
 
 def basis_kernel(
@@ -200,11 +199,11 @@
     planes, gram_out,
     high_rows, low_rows,
 ):
-    remainder = lax.bitwise_and(noted_number(sheet, 0, 1) + SHIFT, 7)
+    remainder = lax.bitwise_and(noted_number(sheet, 1) + SHIFT, 7)
     rows = piece_a[...] + piece_b[...] + piece_c[...]
     rows = pltpu.roll(rows, lax.rem(SPAN - remainder, SPAN), axis=0)
     padded = jnp.concatenate([rows, jnp.zeros((SPAN, BLOCK), jnp.float32)], axis=1)
-    cutout = pltpu.roll(padded, KHALF - noted_number(sheet, 0, 2), axis=1)
+    cutout = pltpu.roll(padded, KHALF - noted_number(sheet, 2), axis=1)
     cut_high, cut_low = split(cutout)
     col_high, col_low = table[: 2 * BLOCK, :], table[2 * BLOCK : 4 * BLOCK, :]
     for block in range(COLS // BLOCK):
@@ -282,7 +281,34 @@
     )(*pieces, *operands)
 
 
-def solve_kernel(grams, planes, sheet, difference_out, stamps, difference, sem):
+def solve_pair(corner, heads):
+    (a, b), (c, d) = corner
+    inverse = 1.0 / (a * d - b * c)
+    return (d * heads[0] - b * heads[1]) * inverse, (a * heads[1] - c * heads[0]) * inverse
+
+
+def solve_corner(corner, heads):
+    first = [row[:2] for row in corner[:2]]
+    right = [solve_pair(first, [corner[0][col], corner[1][col]]) for col in (2, 3)]
+    upper = solve_pair(first, heads[:2])
+    rest = [
+        [
+            corner[row][col] - corner[row][0] * right[col - 2][0] - corner[row][1] * right[col - 2][1]
+            for col in (2, 3)
+        ]
+        for row in (2, 3)
+    ]
+    lower = solve_pair(
+        rest,
+        [heads[row] - corner[row][0] * upper[0] - corner[row][1] * upper[1] for row in (2, 3)],
+    )
+    return (
+        *(upper[row] - right[0][row] * lower[0] - right[1][row] * lower[1] for row in range(2)),
+        *lower,
+    )
+
+
+def solve_kernel(grams, planes, sheet, model_out, stamps):
     total = grams[0] + grams[1] + grams[2] + grams[3]
     cross = total[:, SLOTS : 2 * SLOTS]
     normal = total[:, :SLOTS] + cross + cross.T
@@ -291,30 +317,31 @@
     diagonal = jnp.logical_and(row_id == col_id, row_id < NBASIS)
     trace = jnp.sum(jnp.where(diagonal, normal, 0.0), keepdims=True)
     matrix = normal + jnp.where(diagonal, RIDGE * trace / NBASIS, 0.0)
-    for step in range(0, NBASIS, 2):
-        first = jnp.broadcast_to(matrix[:, step : step + 1], (SLOTS, SLOTS))
-        second = jnp.broadcast_to(matrix[:, step + 1 : step + 2], (SLOTS, SLOTS))
-        upper, lower = slice(step, step + 1), slice(step + 1, step + 2)
-        inverse = 1.0 / (first[upper] * second[lower] - second[upper] * first[lower])
-        row_upper = (second[lower] * matrix[upper] - second[upper] * matrix[lower]) * inverse
-        row_lower = (first[upper] * matrix[lower] - first[lower] * matrix[upper]) * inverse
-        others = matrix - first * row_upper - second * row_lower
-        matrix = jnp.where(
-            row_id == step, row_upper, jnp.where(row_id == step + 1, row_lower, others)
-        )
+    for step in range(0, NBASIS, 4):
+        columns = [
+            jnp.broadcast_to(matrix[:, step + part : step + part + 1], (SLOTS, SLOTS))
+            for part in range(4)
+        ]
+        heads = [matrix[step + part : step + part + 1] for part in range(4)]
+        corner = [[columns[col][step + row : step + row + 1] for col in range(4)] for row in range(4)]
+        solved = solve_corner(corner, heads)
+        others = matrix
+        for part in range(4):
+            others = others - columns[part] * solved[part]
+        matrix = others
+        for part in range(4):
+            matrix = jnp.where(row_id == step + part, solved[part], matrix)
     answer = jnp.broadcast_to(matrix[:, NBASIS : NBASIS + 1], (SLOTS, BLOCK))
     for block in range(BLOCKS):
-        at = (block * SLOTS + NBASIS) * PITCH
-        total = planes[at : at + ROWS, :]
+        model = jnp.zeros((ROWS, BLOCK), jnp.float32)
         for plane in range(NBASIS):
             factor = jnp.broadcast_to(answer[plane : plane + 1, :], (ROWS, BLOCK))
             at = (block * SLOTS + plane) * PITCH
-            total = total - factor * planes[at : at + ROWS, :]
-        difference[:, block * BLOCK : (block + 1) * BLOCK] = total
-    copy = pltpu.make_async_copy(difference, difference_out, sem)
-    copy.start()
-    tile, row_move, col_move = (noted_number(sheet, 0, part) for part in range(3))
-    moved = pltpu.roll(difference[...], lax.rem(row_move + ROWS, ROWS), axis=0)
+            model = model + factor * planes[at : at + ROWS, :]
+        model_out[:, block * BLOCK : (block + 1) * BLOCK] = model
+    difference = sheet[ROWS : 2 * ROWS, :] - model_out[...]
+    tile, row_move, col_move = (noted_number(sheet, part) for part in range(3))
+    moved = pltpu.roll(difference, lax.rem(row_move + ROWS, ROWS), axis=0)
     moved = pltpu.roll(moved, lax.rem(col_move + COLS, COLS), axis=1)
     from_row = lax.broadcasted_iota(jnp.int32, (ROWS, COLS), 0) - row_move
     from_col = lax.broadcasted_iota(jnp.int32, (ROWS, COLS), 1) - col_move
@@ -329,7 +356,6 @@
         stamps[place, TALL:, :] = jnp.full(
             (NOTED - TALL, BLOCK), tile.astype(jnp.float32), jnp.float32
         )
-    copy.wait()
 
 
 def solve(grams, planes, sheet):
@@ -340,8 +366,7 @@
             jax.ShapeDtypeStruct((LINE, NOTED, BLOCK), jnp.float32),
         ),
         in_specs=[VMEM, VMEM, VMEM],
-        out_specs=(HBM, VMEM),
-        scratch_shapes=[pltpu.VMEM((ROWS, COLS), jnp.float32), pltpu.SemaphoreType.DMA],
+        out_specs=(VMEM, VMEM),
         compiler_params=pltpu.CompilerParams(vmem_limit_bytes=LIMIT),
         name="solve",
     )(grams, planes, sheet)
@@ -414,15 +439,15 @@
     below = lax.ppermute(own, "visit", upward)
     above = lax.ppermute(own, "visit", downward)
     sheet, table = prepare(
-        (own, below, above), science[0, 0], inverse_variance[0, 0], jnp.asarray(tables())
+        own, science[0, 0], inverse_variance[0, 0], jnp.asarray(tables())
     )
     window = lax.all_to_all(spread(template[0]), "visit", 0, 0, axis_index_groups=groups)
-    piece_own, piece_up, piece_down = serve(window, sheet)
+    piece_own, piece_up, piece_down = serve(window, sheet, below, above)
     from_above = lax.ppermute(piece_down, "visit", downward)
     from_below = lax.ppermute(piece_up, "visit", upward)
     planes, gram = basis((piece_own, from_above, from_below), sheet, table)
     grams = lax.all_gather(gram, "patch")
-    difference, stamps = solve(grams, planes, sheet)
+    model, stamps = solve(grams, planes, sheet)
     lines = [list(range(first, first + LINE)) for first in range(0, visits, LINE)]
     to_own, to_flip, to_next, to_far = gather(
         lax.all_to_all(stamps, "visit", 0, 0, axis_index_groups=lines)
@@ -434,6 +459,7 @@
     from_far = lax.ppermute(to_far, "visit", far)
     from_next = lax.ppermute(to_next, "visit", following)
     from_flip = lax.ppermute(to_flip, "visit", flip)
+    difference = sheet[ROWS : 2 * ROWS] - model
     return (difference[None, None], mean(to_own, from_flip, from_next, from_far)[None])
 
 

time: 80.5 us -> 79.5 us (0.988)
  Pallas kernels: 8.5 us -> 7.49 us
    ppermute x1, waiting for transfers between devices: 4.71 us -> 2.04 us  [shards(): below = lax.ppermute(own, 'visit', upward)]
    all_to_all x1, waiting for transfers between devices: 2.4 us -> 5.06 us  [shards(): lax.all_to_all(spread(template[0]), 'visit', 0, 0, axis_index_groups=groups)]
    pallas_call x1, Pallas kernels: 2.62 us -> 1.62 us  [solve(): pl.pallas_call(solve_kernel, out_shape=(jax.ShapeDtypeStruct((ROWS, COLS)...]
  transfers between devices with their start and end apart: 8 -> 8, of which waited for: 5 -> 5; matrix products, arithmetic and copies ran while one was open for 0% -> 1% of each run, Pallas kernels for 0% -> 0%
where the time goes in v7:
time: 79.5 us; the launch traced here: 79.1 us
  starting transfers between devices  29.7 us (37%)
  blocking collectives  18.7 us (24%)
  waiting for transfers between devices  18.4 us (23%)
  Pallas kernels  7.49 us (9%)
  local copies, waits for them, and re-layouts  3.36 us (4%)
    all_to_all x1, blocking collectives, shards(): lax.all_to_all(stamps, 'visit', 0, 0, axis_index_groups=lines)  13.4 us
    all_to_all x1, starting transfers between devices, shards(): lax.all_to_all(spread(template[0]), 'visit', 0, 0, axis_index_groups=groups)  6.93 us
    ppermute x1, waiting for transfers between devices, shards(): from_below = lax.ppermute(piece_up, 'visit', upward)  5.34 us
    all_gather x1, blocking collectives, shards(): grams = lax.all_gather(gram, 'patch')  5.25 us
    all_to_all x1, waiting for transfers between devices, shards(): lax.all_to_all(spread(template[0]), 'visit', 0, 0, axis_index_groups=groups)  5.06 us
    ppermute x1, waiting for transfers between devices, shards(): from_next = lax.ppermute(to_next, 'visit', following)  4.4 us
    ppermute x1, starting transfers between devices, shards(): from_far = lax.ppermute(to_far, 'visit', far)  4.13 us
    ppermute x1, starting transfers between devices, shards(): above = lax.ppermute(own, 'visit', downward)  4.13 us
  transfers between devices with their start and end apart: 8, of which 5 were waited for; matrix products, arithmetic and copies ran while one was open for 1% of the time, Pallas kernels for 0%

profile of v7, /device:TPU:384, one launch (start us, length us, event | category | flops | bytes accessed | tf_op | source)
XLA Modules:
  0.0 79.1 jit_solution(2521644182897177986)
XLA Ops:
  0.6 0.9 %copy-done.1 = f32[1,64,512]{2,1,0:T(8,128)S(1)} copy-done((f32[1,64,512]{2,1,0:T(8,128)S(1)}, f32[1,64,512]{2,1,0:T(8,128)}, u32[]{:S(2)}) %copy-start.1) | copy-done | bytes 131096
  1.6 1.0 %spread.1 = f32[8,256,128]{2,1,0:T(8,128)} custom-call(f32[64,512]{1,0:T(8,128)S(1)} %bitcast.9), custom_call_target="tpu_custom_call" | custom-call | tf_op jit(solution)/shard_map/spread/pallas_call | solution.py:122
  2.6 6.9 %all-to-all-start = ((f32[8,256,128]{2,1,0:T(8,128)}), f32[8,256,128]{2,1,0:T(8,128)S(1)}, u32[]{:S(2)}, u32[]{:S(2)}) async-start(f32[8,256,128]{2,1,0:T(8,128)} %spread.1), calls=%async_computation | async-start | bytes 2097152 | tf_op jit(solution)/shard_map/all_to_all | solution.py:444
  9.5 4.1 %collective-permute-start.1 = (s32[1,3]{1,0:T(1,128)S(1)}, s32[1,3]{1,0:T(1,128)S(1)}, u32[]{:S(2)}, u32[]{:S(2)}) collective-permute-start(s32[1,3]{1,0:T(1,128)S(1)} %bitcast.12), channel_id=1, source_target_pairs={{32,0},{36,4},{40,8},{44,12},{48,16},{52,20},{56,24},{60,28},{64,3... | collective-permute-start | bytes 44 | tf_op jit(solution)/shard_map/ppermute | solution.py:440
  13.7 1.9 %collective-permute-start = (s32[1,3]{1,0:T(1,128)S(1)}, s32[1,3]{1,0:T(1,128)S(1)}, u32[]{:S(2)}, u32[]{:S(2)}) collective-permute-start(s32[1,3]{1,0:T(1,128)S(1)} %bitcast.13), channel_id=1, source_target_pairs={{0,32},{4,36},{8,40},{12,44},{16,48},{20,52},{24,56},{28,60},{32,6... | collective-permute-start | bytes 44 | tf_op jit(solution)/shard_map/ppermute | solution.py:439
  15.6 1.5 %copy-done = bf16[704,1408]{1,0:T(8,128)(2,1)S(1)} copy-done((bf16[704,1408]{1,0:T(8,128)(2,1)S(1)}, bf16[704,1408]{1,0:T(8,128)(2,1)}, u32[]{:S(2)}) %copy-start) | copy-done | bytes 1982488
  17.2 0.9 %copy-done.3 = f32[1,1,64,512]{3,2,1,0:T(8,128)S(1)} copy-done((f32[1,1,64,512]{3,2,1,0:T(8,128)S(1)}, f32[1,1,64,512]{3,2,1,0:T(8,128)}, u32[]{:S(2)}) %copy-start.3) | copy-done | bytes 131096
  18.3 2.0 %collective-permute-done.below = s32[1,3]{1,0:T(1,128)S(1)} collective-permute-done((s32[1,3]{1,0:T(1,128)S(1)}, s32[1,3]{1,0:T(1,128)S(1)}, u32[]{:S(2)}, u32[]{:S(2)}) %collective-permute-start) | collective-permute-done | bytes 44 | tf_op jit(solution)/shard_map/ppermute | solution.py:439
  20.3 5.1 %all-to-all-done.window = f32[8,256,128]{2,1,0:T(8,128)S(1)} async-done(((f32[8,256,128]{2,1,0:T(8,128)}), f32[8,256,128]{2,1,0:T(8,128)S(1)}, u32[]{:S(2)}, u32[]{:S(2)}) %all-to-all-start) | async-done | bytes 1048608 | tf_op jit(solution)/shard_map/all_to_all | solution.py:444
  25.4 0.3 serve.1
  25.7 4.1 %collective-permute-start.2 = (f32[96,512]{1,0:T(8,128)S(1)}, f32[96,512]{1,0:T(8,128)S(1)}, u32[]{:S(2)}, u32[]{:S(2)}) collective-permute-start(f32[96,512]{1,0:T(8,128)S(1)} %get-tuple-element.17), channel_id=1, source_target_pairs={{32,0},{36,4},{40,8},{44,12},{48,16},{52,20},{56,24},{60,28},{64,3... | collective-permute-start | bytes 589832 | tf_op jit(solution)/shard_map/ppermute | solution.py:446
  29.8 1.9 %collective-permute-start.3 = (f32[96,512]{1,0:T(8,128)S(1)}, f32[96,512]{1,0:T(8,128)S(1)}, u32[]{:S(2)}, u32[]{:S(2)}) collective-permute-start(f32[96,512]{1,0:T(8,128)S(1)} %get-tuple-element.18), channel_id=1, source_target_pairs={{0,32},{4,36},{8,40},{12,44},{16,48},{20,52},{24,56},{28,60},{32,6... | collective-permute-start | bytes 589832 | tf_op jit(solution)/shard_map/ppermute | solution.py:447
  31.7 1.5 %collective-permute-done.2.piece_b = f32[96,512]{1,0:T(8,128)S(1)} collective-permute-done((f32[96,512]{1,0:T(8,128)S(1)}, f32[96,512]{1,0:T(8,128)S(1)}, u32[]{:S(2)}, u32[]{:S(2)}) %collective-permute-start.2) | collective-permute-done | bytes 196640 | tf_op jit(solution)/shard_map/ppermute | solution.py:446
  33.2 5.3 %collective-permute-done.3.piece_c = f32[96,512]{1,0:T(8,128)S(1)} collective-permute-done((f32[96,512]{1,0:T(8,128)S(1)}, f32[96,512]{1,0:T(8,128)S(1)}, u32[]{:S(2)}, u32[]{:S(2)}) %collective-permute-start.3) | collective-permute-done | bytes 196640 | tf_op jit(solution)/shard_map/ppermute | solution.py:447
  38.6 3.5 %basis.1 = (f32[9216,128]{1,0:T(8,128)S(1)}, f32[32,128]{1,0:T(8,128)S(1)}) custom-call(f32[96,512]{1,0:T(8,128)S(1)} %get-tuple-element.16.piece_a, f32[96,512]{1,0:T(8,128)S(1)} %collective-permute-done.2.piece_b, f32[96,512]{1,0:T(8,128)S(1)} %collective-permute-done.3.piece_c, f32[136,512]{1,0:T(8,128)S(1)} %get-tuple-element.15.sheet, ...), custom_call_target="tpu_custom_call" | custom-call | tf_op jit(solution)/shard_map/basis/pallas_call | solution.py:267
  42.1 5.2 %all-gather = f32[128,128]{1,0:T(8,128)S(1)} all-gather(f32[32,128]{1,0:T(8,128)S(1)} %get-tuple-element.20), channel_id=2, replica_groups=mesh['visit'=128,'patch'=4] {'patch'}, dimensions={0}, use_global_device_ids=true | all-gather | bytes 81920 | tf_op jit(solution)/shard_map/all_gather | solution.py:449
  47.3 1.6 %solve.1 = (f32[64,512]{1,0:T(8,128)S(1)}, f32[4,264,128]{2,1,0:T(8,128)S(1)}) custom-call(f32[4,32,128]{2,1,0:T(8,128)S(1)} %bitcast.8, f32[9216,128]{1,0:T(8,128)S(1)} %get-tuple-element.21.planes, f32[136,512]{1,0:T(8,128)S(1)} %get-tuple-element.15.sheet), custom_call_target="tpu_custom_call" | custom-call | tf_op jit(solution)/shard_map/solve/pallas_call | solution.py:362
  49.0 13.4 %all_to_all.10.stamps = f32[4,264,128]{2,1,0:T(8,128)S(1)} all-to-all(f32[4,264,128]{2,1,0:T(8,128)S(1)} %get-tuple-element.23), channel_id=1, replica_groups={{0,4,8,12},{16,20,24,28},{32,36,40,44},{48,52,56,60},{64,68,72,76},{80,..., dimensions={0} | all-to-all | bytes 1081344 | tf_op jit(solution)/shard_map/all_to_all | solution.py:453
  62.6 4.0 %collective-permute-start.4 = (f32[264,128]{1,0:T(8,128)S(1)}, f32[264,128]{1,0:T(8,128)S(1)}, u32[]{:S(2)}, u32[]{:S(2)}) collective-permute-start(f32[264,128]{1,0:T(8,128)S(1)} %get-tuple-element.25), channel_id=1, source_target_pairs={{0,16},{4,20},{8,24},{12,28},{16,0},{20,4},{24,8},{28,12},{32,48},... | collective-permute-start | bytes 405512 | tf_op jit(solution)/shard_map/ppermute | solution.py:461
  66.5 2.6 %collective-permute-start.5 = (f32[264,128]{1,0:T(8,128)S(1)}, f32[264,128]{1,0:T(8,128)S(1)}, u32[]{:S(2)}, u32[]{:S(2)}) collective-permute-start(f32[264,128]{1,0:T(8,128)S(1)} %get-tuple-element.26), channel_id=1, source_target_pairs={{16,32},{20,36},{24,40},{28,44},{32,16},{36,20},{40,24},{44,28},{4... | collective-permute-start | bytes 405512 | tf_op jit(solution)/shard_map/ppermute | solution.py:460
  69.2 4.1 %collective-permute-start.6 = (f32[264,128]{1,0:T(8,128)S(1)}, f32[264,128]{1,0:T(8,128)S(1)}, u32[]{:S(2)}, u32[]{:S(2)}) collective-permute-start(f32[264,128]{1,0:T(8,128)S(1)} %get-tuple-element.27), channel_id=1, source_target_pairs={{0,32},{4,36},{16,48},{20,52},{32,64},{36,68},{40,8},{44,12},{48,8... | collective-permute-start | bytes 405512 | tf_op jit(solution)/shard_map/ppermute | solution.py:459
  73.3 0.7 subtract_bitcast_fusion
  74.0 4.4 %collective-permute-done.5.part_c = f32[264,128]{1,0:T(8,128)S(1)} collective-permute-done((f32[264,128]{1,0:T(8,128)S(1)}, f32[264,128]{1,0:T(8,128)S(1)}, u32[]{:S(2)}, u32[]{:S(2)}) %collective-permute-start.5) | collective-permute-done | bytes 135200 | tf_op jit(solution)/shard_map/ppermute | solution.py:460
  78.4 0.7 mean.1
  (12 shorter events, 0.4 us)
Async XLA Ops:
  0.6 8.9 %copy-start.4 = (s32[1,1,3]{2,1,0:T(1,128)S(1)}, s32[1,1,3]{2,1,0:T(1,128)}, u32[]{:S(2)}) copy-start(s32[1,1,3]{2,1,0:T(1,128)} %param.8) | copy-start | bytes 40
  0.6 0.9 %copy-start.1 = (f32[1,64,512]{2,1,0:T(8,128)S(1)}, f32[1,64,512]{2,1,0:T(8,128)}, u32[]{:S(2)}) copy-start(f32[1,64,512]{2,1,0:T(8,128)} %param.5) | copy-start | bytes 393220
  1.6 14.1 %copy-start.2 = (f32[1,1,64,512]{3,2,1,0:T(8,128)S(1)}, f32[1,1,64,512]{3,2,1,0:T(8,128)}, u32[]{:S(2)}) copy-start(f32[1,1,64,512]{3,2,1,0:T(8,128)} %param.6) | copy-start | bytes 393220
  2.6 22.8 %all-to-all-start = ((f32[8,256,128]{2,1,0:T(8,128)}), f32[8,256,128]{2,1,0:T(8,128)S(1)}, u32[]{:S(2)}, u32[]{:S(2)}) async-start(f32[8,256,128]{2,1,0:T(8,128)} %spread.1), calls=%async_computation | async-start | bytes 2097152 | tf_op jit(solution)/shard_map/all_to_all | solution.py:444
  9.5 8.7 %collective-permute-start.1 = (s32[1,3]{1,0:T(1,128)S(1)}, s32[1,3]{1,0:T(1,128)S(1)}, u32[]{:S(2)}, u32[]{:S(2)}) collective-permute-start(s32[1,3]{1,0:T(1,128)S(1)} %bitcast.12), channel_id=1, source_target_pairs={{32,0},{36,4},{40,8},{44,12},{48,16},{52,20},{56,24},{60,28},{64,3... | collective-permute-start | bytes 44 | tf_op jit(solution)/shard_map/ppermute | solution.py:440
  13.7 6.6 %collective-permute-start = (s32[1,3]{1,0:T(1,128)S(1)}, s32[1,3]{1,0:T(1,128)S(1)}, u32[]{:S(2)}, u32[]{:S(2)}) collective-permute-start(s32[1,3]{1,0:T(1,128)S(1)} %bitcast.13), channel_id=1, source_target_pairs={{0,32},{4,36},{8,40},{12,44},{16,48},{20,52},{24,56},{28,60},{32,6... | collective-permute-start | bytes 44 | tf_op jit(solution)/shard_map/ppermute | solution.py:439
  15.6 1.6 %copy-start = (bf16[704,1408]{1,0:T(8,128)(2,1)S(1)}, bf16[704,1408]{1,0:T(8,128)(2,1)}, u32[]{:S(2)}) copy-start(bf16[704,1408]{1,0:T(8,128)(2,1)} %constant.2.clone.table) | copy-start | bytes 5947396
  17.2 0.9 %copy-start.3 = (f32[1,1,64,512]{3,2,1,0:T(8,128)S(1)}, f32[1,1,64,512]{3,2,1,0:T(8,128)}, u32[]{:S(2)}) copy-start(f32[1,1,64,512]{3,2,1,0:T(8,128)} %param.7) | copy-start | bytes 393220
  25.7 7.6 %collective-permute-start.2 = (f32[96,512]{1,0:T(8,128)S(1)}, f32[96,512]{1,0:T(8,128)S(1)}, u32[]{:S(2)}, u32[]{:S(2)}) collective-permute-start(f32[96,512]{1,0:T(8,128)S(1)} %get-tuple-element.17), channel_id=1, source_target_pairs={{32,0},{36,4},{40,8},{44,12},{48,16},{52,20},{56,24},{60,28},{64,3... | collective-permute-start | bytes 589832 | tf_op jit(solution)/shard_map/ppermute | solution.py:446
  29.8 8.8 %collective-permute-start.3 = (f32[96,512]{1,0:T(8,128)S(1)}, f32[96,512]{1,0:T(8,128)S(1)}, u32[]{:S(2)}, u32[]{:S(2)}) collective-permute-start(f32[96,512]{1,0:T(8,128)S(1)} %get-tuple-element.18), channel_id=1, source_target_pairs={{0,32},{4,36},{8,40},{12,44},{16,48},{20,52},{24,56},{28,60},{32,6... | collective-permute-start | bytes 589832 | tf_op jit(solution)/shard_map/ppermute | solution.py:447
  62.6 11.4 %collective-permute-start.4 = (f32[264,128]{1,0:T(8,128)S(1)}, f32[264,128]{1,0:T(8,128)S(1)}, u32[]{:S(2)}, u32[]{:S(2)}) collective-permute-start(f32[264,128]{1,0:T(8,128)S(1)} %get-tuple-element.25), channel_id=1, source_target_pairs={{0,16},{4,20},{8,24},{12,28},{16,0},{20,4},{24,8},{28,12},{32,48},... | collective-permute-start | bytes 405512 | tf_op jit(solution)/shard_map/ppermute | solution.py:461
  66.5 11.9 %collective-permute-start.5 = (f32[264,128]{1,0:T(8,128)S(1)}, f32[264,128]{1,0:T(8,128)S(1)}, u32[]{:S(2)}, u32[]{:S(2)}) collective-permute-start(f32[264,128]{1,0:T(8,128)S(1)} %get-tuple-element.26), channel_id=1, source_target_pairs={{16,32},{20,36},{24,40},{28,44},{32,16},{36,20},{40,24},{44,28},{4... | collective-permute-start | bytes 405512 | tf_op jit(solution)/shard_map/ppermute | solution.py:460
  69.2 9.2 %collective-permute-start.6 = (f32[264,128]{1,0:T(8,128)S(1)}, f32[264,128]{1,0:T(8,128)S(1)}, u32[]{:S(2)}, u32[]{:S(2)}) collective-permute-start(f32[264,128]{1,0:T(8,128)S(1)} %get-tuple-element.27), channel_id=1, source_target_pairs={{0,32},{4,36},{16,48},{20,52},{32,64},{36,68},{40,8},{44,12},{48,8... | collective-permute-start | bytes 405512 | tf_op jit(solution)/shard_map/ppermute | solution.py:459

commit v8 on v7

--- a/solution.py
+++ b/solution.py
@@ -457,10 +457,10 @@
     far = [(i, i + 2 * LINE if i % LINE < LINE // 2 else i - 2 * LINE) for i in range(visits)]
     far = [(source, target) for source, target in far if 0 <= target < visits]
     from_far = lax.ppermute(to_far, "visit", far)
+    from_flip = lax.ppermute(to_flip, "visit", flip)
     from_next = lax.ppermute(to_next, "visit", following)
-    from_flip = lax.ppermute(to_flip, "visit", flip)
     difference = sheet[ROWS : 2 * ROWS] - model
-    return (difference[None, None], mean(to_own, from_flip, from_next, from_far)[None])
+    return (difference[None, None], mean(to_own, from_next, from_flip, from_far)[None])
 
 
 def solution(mesh):

time: 79.5 us -> 78.6 us (0.989)
  starting transfers between devices: 29.7 us -> 28.3 us
    ppermute x1, waiting for transfers between devices: 4.4 us -> 0.58 us  [shards(): from_next = lax.ppermute(to_next, 'visit', following)]
    ppermute x1, waiting for transfers between devices: 0.01 us -> 2.59 us  [shards(): from_flip = lax.ppermute(to_flip, 'visit', flip)]
    ppermute x1, waiting for transfers between devices: 0.01 us -> 1.82 us  [shards(): from_far = lax.ppermute(to_far, 'visit', far)]
    ppermute x1, starting transfers between devices: 3.95 us -> 2.68 us  [shards(): from_flip = lax.ppermute(to_flip, 'visit', flip)]
  transfers between devices with their start and end apart: 8 -> 8, of which waited for: 5 -> 7; matrix products, arithmetic and copies ran while one was open for 1% -> 1% of each run, Pallas kernels for 0% -> 0%
where the time goes in v8:
time: 78.6 us; the launch traced here: 78.2 us
  starting transfers between devices  28.3 us (36%)
  waiting for transfers between devices  18.9 us (24%)
  blocking collectives  18.7 us (24%)
  Pallas kernels  7.49 us (10%)
  local copies, waits for them, and re-layouts  3.36 us (4%)
    all_to_all x1, blocking collectives, shards(): lax.all_to_all(stamps, 'visit', 0, 0, axis_index_groups=lines)  13.4 us
    all_to_all x1, starting transfers between devices, shards(): lax.all_to_all(spread(template[0]), 'visit', 0, 0, axis_index_groups=groups)  6.93 us
    ppermute x1, waiting for transfers between devices, shards(): from_below = lax.ppermute(piece_up, 'visit', upward)  5.34 us
    all_gather x1, blocking collectives, shards(): grams = lax.all_gather(gram, 'patch')  5.25 us
    all_to_all x1, waiting for transfers between devices, shards(): lax.all_to_all(spread(template[0]), 'visit', 0, 0, axis_index_groups=groups)  5.06 us
    ppermute x1, starting transfers between devices, shards(): above = lax.ppermute(own, 'visit', downward)  4.13 us
    ppermute x1, starting transfers between devices, shards(): from_above = lax.ppermute(piece_down, 'visit', downward)  4.13 us
    pallas_call x1, Pallas kernels, basis(): pl.pallas_call(basis_kernel, out_shape=(jax.ShapeDtypeStruct((BLOCKS * SL...  3.48 us
  transfers between devices with their start and end apart: 8, of which 7 were waited for; matrix products, arithmetic and copies ran while one was open for 1% of the time, Pallas kernels for 0%

profile of v8, /device:TPU:384, one launch (start us, length us, event | category | flops | bytes accessed | tf_op | source)
XLA Modules:
  0.0 78.2 jit_solution(10280530219804968224)
XLA Ops:
  0.6 0.9 %copy-done.1 = f32[1,64,512]{2,1,0:T(8,128)S(1)} copy-done((f32[1,64,512]{2,1,0:T(8,128)S(1)}, f32[1,64,512]{2,1,0:T(8,128)}, u32[]{:S(2)}) %copy-start.1) | copy-done | bytes 131096
  1.6 1.0 %spread.1 = f32[8,256,128]{2,1,0:T(8,128)} custom-call(f32[64,512]{1,0:T(8,128)S(1)} %bitcast.9), custom_call_target="tpu_custom_call" | custom-call | tf_op jit(solution)/shard_map/spread/pallas_call | solution.py:122
  2.6 6.9 %all-to-all-start = ((f32[8,256,128]{2,1,0:T(8,128)}), f32[8,256,128]{2,1,0:T(8,128)S(1)}, u32[]{:S(2)}, u32[]{:S(2)}) async-start(f32[8,256,128]{2,1,0:T(8,128)} %spread.1), calls=%async_computation | async-start | bytes 2097152 | tf_op jit(solution)/shard_map/all_to_all | solution.py:444
  9.5 4.1 %collective-permute-start.1 = (s32[1,3]{1,0:T(1,128)S(1)}, s32[1,3]{1,0:T(1,128)S(1)}, u32[]{:S(2)}, u32[]{:S(2)}) collective-permute-start(s32[1,3]{1,0:T(1,128)S(1)} %bitcast.12), channel_id=1, source_target_pairs={{32,0},{36,4},{40,8},{44,12},{48,16},{52,20},{56,24},{60,28},{64,3... | collective-permute-start | bytes 44 | tf_op jit(solution)/shard_map/ppermute | solution.py:440
  13.7 1.9 %collective-permute-start = (s32[1,3]{1,0:T(1,128)S(1)}, s32[1,3]{1,0:T(1,128)S(1)}, u32[]{:S(2)}, u32[]{:S(2)}) collective-permute-start(s32[1,3]{1,0:T(1,128)S(1)} %bitcast.13), channel_id=1, source_target_pairs={{0,32},{4,36},{8,40},{12,44},{16,48},{20,52},{24,56},{28,60},{32,6... | collective-permute-start | bytes 44 | tf_op jit(solution)/shard_map/ppermute | solution.py:439
  15.6 1.5 %copy-done = bf16[704,1408]{1,0:T(8,128)(2,1)S(1)} copy-done((bf16[704,1408]{1,0:T(8,128)(2,1)S(1)}, bf16[704,1408]{1,0:T(8,128)(2,1)}, u32[]{:S(2)}) %copy-start) | copy-done | bytes 1982488
  17.2 0.9 %copy-done.3 = f32[1,1,64,512]{3,2,1,0:T(8,128)S(1)} copy-done((f32[1,1,64,512]{3,2,1,0:T(8,128)S(1)}, f32[1,1,64,512]{3,2,1,0:T(8,128)}, u32[]{:S(2)}) %copy-start.3) | copy-done | bytes 131096
  18.3 2.0 %collective-permute-done.below = s32[1,3]{1,0:T(1,128)S(1)} collective-permute-done((s32[1,3]{1,0:T(1,128)S(1)}, s32[1,3]{1,0:T(1,128)S(1)}, u32[]{:S(2)}, u32[]{:S(2)}) %collective-permute-start) | collective-permute-done | bytes 44 | tf_op jit(solution)/shard_map/ppermute | solution.py:439
  20.3 5.1 %all-to-all-done.window = f32[8,256,128]{2,1,0:T(8,128)S(1)} async-done(((f32[8,256,128]{2,1,0:T(8,128)}), f32[8,256,128]{2,1,0:T(8,128)S(1)}, u32[]{:S(2)}, u32[]{:S(2)}) %all-to-all-start) | async-done | bytes 1048608 | tf_op jit(solution)/shard_map/all_to_all | solution.py:444
  25.7 4.1 %collective-permute-start.2 = (f32[96,512]{1,0:T(8,128)S(1)}, f32[96,512]{1,0:T(8,128)S(1)}, u32[]{:S(2)}, u32[]{:S(2)}) collective-permute-start(f32[96,512]{1,0:T(8,128)S(1)} %get-tuple-element.17), channel_id=1, source_target_pairs={{32,0},{36,4},{40,8},{44,12},{48,16},{52,20},{56,24},{60,28},{64,3... | collective-permute-start | bytes 589832 | tf_op jit(solution)/shard_map/ppermute | solution.py:446
  29.8 1.9 %collective-permute-start.3 = (f32[96,512]{1,0:T(8,128)S(1)}, f32[96,512]{1,0:T(8,128)S(1)}, u32[]{:S(2)}, u32[]{:S(2)}) collective-permute-start(f32[96,512]{1,0:T(8,128)S(1)} %get-tuple-element.18), channel_id=1, source_target_pairs={{0,32},{4,36},{8,40},{12,44},{16,48},{20,52},{24,56},{28,60},{32,6... | collective-permute-start | bytes 589832 | tf_op jit(solution)/shard_map/ppermute | solution.py:447
  31.7 1.5 %collective-permute-done.2.piece_b = f32[96,512]{1,0:T(8,128)S(1)} collective-permute-done((f32[96,512]{1,0:T(8,128)S(1)}, f32[96,512]{1,0:T(8,128)S(1)}, u32[]{:S(2)}, u32[]{:S(2)}) %collective-permute-start.2) | collective-permute-done | bytes 196640 | tf_op jit(solution)/shard_map/ppermute | solution.py:446
  33.2 5.3 %collective-permute-done.3.piece_c = f32[96,512]{1,0:T(8,128)S(1)} collective-permute-done((f32[96,512]{1,0:T(8,128)S(1)}, f32[96,512]{1,0:T(8,128)S(1)}, u32[]{:S(2)}, u32[]{:S(2)}) %collective-permute-start.3) | collective-permute-done | bytes 196640 | tf_op jit(solution)/shard_map/ppermute | solution.py:447
  38.6 3.5 %basis.1 = (f32[9216,128]{1,0:T(8,128)S(1)}, f32[32,128]{1,0:T(8,128)S(1)}) custom-call(f32[96,512]{1,0:T(8,128)S(1)} %get-tuple-element.16.piece_a, f32[96,512]{1,0:T(8,128)S(1)} %collective-permute-done.2.piece_b, f32[96,512]{1,0:T(8,128)S(1)} %collective-permute-done.3.piece_c, f32[136,512]{1,0:T(8,128)S(1)} %get-tuple-element.15.sheet, ...), custom_call_target="tpu_custom_call" | custom-call | tf_op jit(solution)/shard_map/basis/pallas_call | solution.py:267
  42.1 5.2 %all-gather = f32[128,128]{1,0:T(8,128)S(1)} all-gather(f32[32,128]{1,0:T(8,128)S(1)} %get-tuple-element.20), channel_id=2, replica_groups=mesh['visit'=128,'patch'=4] {'patch'}, dimensions={0}, use_global_device_ids=true | all-gather | bytes 81920 | tf_op jit(solution)/shard_map/all_gather | solution.py:449
  47.3 1.6 %solve.1 = (f32[64,512]{1,0:T(8,128)S(1)}, f32[4,264,128]{2,1,0:T(8,128)S(1)}) custom-call(f32[4,32,128]{2,1,0:T(8,128)S(1)} %bitcast.8, f32[9216,128]{1,0:T(8,128)S(1)} %get-tuple-element.21.planes, f32[136,512]{1,0:T(8,128)S(1)} %get-tuple-element.15.sheet), custom_call_target="tpu_custom_call" | custom-call | tf_op jit(solution)/shard_map/solve/pallas_call | solution.py:362
  49.0 13.4 %all_to_all.10.stamps = f32[4,264,128]{2,1,0:T(8,128)S(1)} all-to-all(f32[4,264,128]{2,1,0:T(8,128)S(1)} %get-tuple-element.23), channel_id=1, replica_groups={{0,4,8,12},{16,20,24,28},{32,36,40,44},{48,52,56,60},{64,68,72,76},{80,..., dimensions={0} | all-to-all | bytes 1081344 | tf_op jit(solution)/shard_map/all_to_all | solution.py:453
  62.6 3.2 %collective-permute-start.4 = (f32[264,128]{1,0:T(8,128)S(1)}, f32[264,128]{1,0:T(8,128)S(1)}, u32[]{:S(2)}, u32[]{:S(2)}) collective-permute-start(f32[264,128]{1,0:T(8,128)S(1)} %get-tuple-element.25), channel_id=1, source_target_pairs={{16,32},{20,36},{24,40},{28,44},{32,16},{36,20},{40,24},{44,28},{4... | collective-permute-start | bytes 405512 | tf_op jit(solution)/shard_map/ppermute | solution.py:461
  65.7 2.7 %collective-permute-start.5 = (f32[264,128]{1,0:T(8,128)S(1)}, f32[264,128]{1,0:T(8,128)S(1)}, u32[]{:S(2)}, u32[]{:S(2)}) collective-permute-start(f32[264,128]{1,0:T(8,128)S(1)} %get-tuple-element.26), channel_id=1, source_target_pairs={{0,16},{4,20},{8,24},{12,28},{16,0},{20,4},{24,8},{28,12},{32,48},... | collective-permute-start | bytes 405512 | tf_op jit(solution)/shard_map/ppermute | solution.py:460
  68.4 3.4 %collective-permute-start.6 = (f32[264,128]{1,0:T(8,128)S(1)}, f32[264,128]{1,0:T(8,128)S(1)}, u32[]{:S(2)}, u32[]{:S(2)}) collective-permute-start(f32[264,128]{1,0:T(8,128)S(1)} %get-tuple-element.27), channel_id=1, source_target_pairs={{0,32},{4,36},{16,48},{20,52},{32,64},{36,68},{40,8},{44,12},{48,8... | collective-permute-start | bytes 405512 | tf_op jit(solution)/shard_map/ppermute | solution.py:459
  71.8 0.7 subtract_bitcast_fusion
  73.1 2.6 %collective-permute-done.5.part_c = f32[264,128]{1,0:T(8,128)S(1)} collective-permute-done((f32[264,128]{1,0:T(8,128)S(1)}, f32[264,128]{1,0:T(8,128)S(1)}, u32[]{:S(2)}, u32[]{:S(2)}) %collective-permute-start.5) | collective-permute-done | bytes 135200 | tf_op jit(solution)/shard_map/ppermute | solution.py:460
  75.7 1.8 %collective-permute-done.6.part_d = f32[264,128]{1,0:T(8,128)S(1)} collective-permute-done((f32[264,128]{1,0:T(8,128)S(1)}, f32[264,128]{1,0:T(8,128)S(1)}, u32[]{:S(2)}, u32[]{:S(2)}) %collective-permute-start.6) | collective-permute-done | bytes 135200 | tf_op jit(solution)/shard_map/ppermute | solution.py:459
  77.5 0.7 mean.1
  (12 shorter events, 1.2 us)
Async XLA Ops:
  0.6 8.9 %copy-start.4 = (s32[1,1,3]{2,1,0:T(1,128)S(1)}, s32[1,1,3]{2,1,0:T(1,128)}, u32[]{:S(2)}) copy-start(s32[1,1,3]{2,1,0:T(1,128)} %param.8) | copy-start | bytes 40
  0.6 0.9 %copy-start.1 = (f32[1,64,512]{2,1,0:T(8,128)S(1)}, f32[1,64,512]{2,1,0:T(8,128)}, u32[]{:S(2)}) copy-start(f32[1,64,512]{2,1,0:T(8,128)} %param.5) | copy-start | bytes 393220
  1.6 14.1 %copy-start.2 = (f32[1,1,64,512]{3,2,1,0:T(8,128)S(1)}, f32[1,1,64,512]{3,2,1,0:T(8,128)}, u32[]{:S(2)}) copy-start(f32[1,1,64,512]{3,2,1,0:T(8,128)} %param.6) | copy-start | bytes 393220
  2.6 22.8 %all-to-all-start = ((f32[8,256,128]{2,1,0:T(8,128)}), f32[8,256,128]{2,1,0:T(8,128)S(1)}, u32[]{:S(2)}, u32[]{:S(2)}) async-start(f32[8,256,128]{2,1,0:T(8,128)} %spread.1), calls=%async_computation | async-start | bytes 2097152 | tf_op jit(solution)/shard_map/all_to_all | solution.py:444
  9.5 8.7 %collective-permute-start.1 = (s32[1,3]{1,0:T(1,128)S(1)}, s32[1,3]{1,0:T(1,128)S(1)}, u32[]{:S(2)}, u32[]{:S(2)}) collective-permute-start(s32[1,3]{1,0:T(1,128)S(1)} %bitcast.12), channel_id=1, source_target_pairs={{32,0},{36,4},{40,8},{44,12},{48,16},{52,20},{56,24},{60,28},{64,3... | collective-permute-start | bytes 44 | tf_op jit(solution)/shard_map/ppermute | solution.py:440
  13.7 6.6 %collective-permute-start = (s32[1,3]{1,0:T(1,128)S(1)}, s32[1,3]{1,0:T(1,128)S(1)}, u32[]{:S(2)}, u32[]{:S(2)}) collective-permute-start(s32[1,3]{1,0:T(1,128)S(1)} %bitcast.13), channel_id=1, source_target_pairs={{0,32},{4,36},{8,40},{12,44},{16,48},{20,52},{24,56},{28,60},{32,6... | collective-permute-start | bytes 44 | tf_op jit(solution)/shard_map/ppermute | solution.py:439
  15.6 1.6 %copy-start = (bf16[704,1408]{1,0:T(8,128)(2,1)S(1)}, bf16[704,1408]{1,0:T(8,128)(2,1)}, u32[]{:S(2)}) copy-start(bf16[704,1408]{1,0:T(8,128)(2,1)} %constant.2.clone.table) | copy-start | bytes 5947396
  17.2 0.9 %copy-start.3 = (f32[1,1,64,512]{3,2,1,0:T(8,128)S(1)}, f32[1,1,64,512]{3,2,1,0:T(8,128)}, u32[]{:S(2)}) copy-start(f32[1,1,64,512]{3,2,1,0:T(8,128)} %param.7) | copy-start | bytes 393220
  25.7 7.6 %collective-permute-start.2 = (f32[96,512]{1,0:T(8,128)S(1)}, f32[96,512]{1,0:T(8,128)S(1)}, u32[]{:S(2)}, u32[]{:S(2)}) collective-permute-start(f32[96,512]{1,0:T(8,128)S(1)} %get-tuple-element.17), channel_id=1, source_target_pairs={{32,0},{36,4},{40,8},{44,12},{48,16},{52,20},{56,24},{60,28},{64,3... | collective-permute-start | bytes 589832 | tf_op jit(solution)/shard_map/ppermute | solution.py:446
  29.8 8.8 %collective-permute-start.3 = (f32[96,512]{1,0:T(8,128)S(1)}, f32[96,512]{1,0:T(8,128)S(1)}, u32[]{:S(2)}, u32[]{:S(2)}) collective-permute-start(f32[96,512]{1,0:T(8,128)S(1)} %get-tuple-element.18), channel_id=1, source_target_pairs={{0,32},{4,36},{8,40},{12,44},{16,48},{20,52},{24,56},{28,60},{32,6... | collective-permute-start | bytes 589832 | tf_op jit(solution)/shard_map/ppermute | solution.py:447
  62.6 10.5 %collective-permute-start.4 = (f32[264,128]{1,0:T(8,128)S(1)}, f32[264,128]{1,0:T(8,128)S(1)}, u32[]{:S(2)}, u32[]{:S(2)}) collective-permute-start(f32[264,128]{1,0:T(8,128)S(1)} %get-tuple-element.25), channel_id=1, source_target_pairs={{16,32},{20,36},{24,40},{28,44},{32,16},{36,20},{40,24},{44,28},{4... | collective-permute-start | bytes 405512 | tf_op jit(solution)/shard_map/ppermute | solution.py:461
  65.7 9.9 %collective-permute-start.5 = (f32[264,128]{1,0:T(8,128)S(1)}, f32[264,128]{1,0:T(8,128)S(1)}, u32[]{:S(2)}, u32[]{:S(2)}) collective-permute-start(f32[264,128]{1,0:T(8,128)S(1)} %get-tuple-element.26), channel_id=1, source_target_pairs={{0,16},{4,20},{8,24},{12,28},{16,0},{20,4},{24,8},{28,12},{32,48},... | collective-permute-start | bytes 405512 | tf_op jit(solution)/shard_map/ppermute | solution.py:460
  68.4 9.0 %collective-permute-start.6 = (f32[264,128]{1,0:T(8,128)S(1)}, f32[264,128]{1,0:T(8,128)S(1)}, u32[]{:S(2)}, u32[]{:S(2)}) collective-permute-start(f32[264,128]{1,0:T(8,128)S(1)} %get-tuple-element.27), channel_id=1, source_target_pairs={{0,32},{4,36},{16,48},{20,52},{32,64},{36,68},{40,8},{44,12},{48,8... | collective-permute-start | bytes 405512 | tf_op jit(solution)/shard_map/ppermute | solution.py:459

commit v9 on v8

--- a/solution.py
+++ b/solution.py
@@ -19,6 +19,7 @@
 PLANE = 8
 LINE = 4
 SPAN = 96
+SENT = 88
 SLOTS = 32
 BLOCK = 128
 BLOCKS = COLS // BLOCK
@@ -162,7 +163,7 @@
     )(entries, science, weight, table)
 
 
-def serve_kernel(window, sheet, below, above, piece_own, piece_up, piece_down):
+def serve_kernel(window, sheet, below, above, piece_own, piece_up, piece_down, strips):
     base = (lax.axis_index("visit") // PLANE) * PLANE
     own = (noted_number(sheet, 0), noted_number(sheet, 1))
     others = [(entries[...][0, 0], entries[...][0, 1]) for entries in (below, above)]
@@ -177,18 +178,21 @@
             row = pl.multiple_of(lax.bitwise_and(strip, 7) * 8, 8)
             for block in range(BLOCKS):
                 rows = window[tile, pl.ds(block * ROWS + row, 8), :]
-                piece[8 * part : 8 * part + 8, block * BLOCK : (block + 1) * BLOCK] = jnp.where(
+                strips[8 * part : 8 * part + 8, block * BLOCK : (block + 1) * BLOCK] = jnp.where(
                     inside, rows, 0.0
                 )
+        shift = lax.rem(SPAN - lax.bitwise_and(start, 7), SPAN)
+        piece[...] = pltpu.roll(strips[...], shift, axis=0)[:SENT]
 
 
 def serve(window, sheet, below, above):
-    shape = jax.ShapeDtypeStruct((SPAN, COLS), jnp.float32)
+    shape = jax.ShapeDtypeStruct((SENT, COLS), jnp.float32)
     return pl.pallas_call(
         serve_kernel,
         out_shape=(shape, shape, shape),
         in_specs=[VMEM] * 4,
         out_specs=(VMEM, VMEM, VMEM),
+        scratch_shapes=[pltpu.VMEM((SPAN, COLS), jnp.float32)],
         compiler_params=pltpu.CompilerParams(vmem_limit_bytes=LIMIT),
         name="serve",
     )(window, sheet, below, above)
@@ -199,9 +203,8 @@
     planes, gram_out,
     high_rows, low_rows,
 ):
-    remainder = lax.bitwise_and(noted_number(sheet, 1) + SHIFT, 7)
     rows = piece_a[...] + piece_b[...] + piece_c[...]
-    rows = pltpu.roll(rows, lax.rem(SPAN - remainder, SPAN), axis=0)
+    rows = jnp.concatenate([rows, jnp.zeros((SPAN - SENT, COLS), jnp.float32)], axis=0)
     padded = jnp.concatenate([rows, jnp.zeros((SPAN, BLOCK), jnp.float32)], axis=1)
     cutout = pltpu.roll(padded, KHALF - noted_number(sheet, 2), axis=1)
     cut_high, cut_low = split(cutout)

time: 78.6 us -> 78.5 us (level)
  no operation moved by 1% of the time
where the time goes in v9:
time: 78.5 us; the launch traced here: 78 us
  starting transfers between devices  28.1 us (36%)
  waiting for transfers between devices  18.9 us (24%)
  blocking collectives  18.7 us (24%)
  Pallas kernels  7.53 us (10%)
  local copies, waits for them, and re-layouts  3.36 us (4%)
    all_to_all x1, blocking collectives, shards(): lax.all_to_all(stamps, 'visit', 0, 0, axis_index_groups=lines)  13.4 us
    all_to_all x1, starting transfers between devices, shards(): lax.all_to_all(spread(template[0]), 'visit', 0, 0, axis_index_groups=groups)  6.93 us
    ppermute x1, waiting for transfers between devices, shards(): from_below = lax.ppermute(piece_up, 'visit', upward)  5.34 us
    all_gather x1, blocking collectives, shards(): grams = lax.all_gather(gram, 'patch')  5.25 us
    all_to_all x1, waiting for transfers between devices, shards(): lax.all_to_all(spread(template[0]), 'visit', 0, 0, axis_index_groups=groups)  5.06 us
    ppermute x1, starting transfers between devices, shards(): above = lax.ppermute(own, 'visit', downward)  4.13 us
    ppermute x1, starting transfers between devices, shards(): from_above = lax.ppermute(piece_down, 'visit', downward)  4.13 us
    pallas_call x1, Pallas kernels, basis(): pl.pallas_call(basis_kernel, out_shape=(jax.ShapeDtypeStruct((BLOCKS * SL...  3.44 us
  transfers between devices with their start and end apart: 8, of which 7 were waited for; matrix products, arithmetic and copies ran while one was open for 1% of the time, Pallas kernels for 0%

profile of v9, /device:TPU:384, one launch (start us, length us, event | category | flops | bytes accessed | tf_op | source)
XLA Modules:
  0.0 78.0 jit_solution(6062414118383481904)
XLA Ops:
  0.6 0.9 %copy-done.1 = f32[1,64,512]{2,1,0:T(8,128)S(1)} copy-done((f32[1,64,512]{2,1,0:T(8,128)S(1)}, f32[1,64,512]{2,1,0:T(8,128)}, u32[]{:S(2)}) %copy-start.1) | copy-done | bytes 131096
  1.6 1.0 %spread.1 = f32[8,256,128]{2,1,0:T(8,128)} custom-call(f32[64,512]{1,0:T(8,128)S(1)} %bitcast.9), custom_call_target="tpu_custom_call" | custom-call | tf_op jit(solution)/shard_map/spread/pallas_call | solution.py:123
  2.6 6.9 %all-to-all-start = ((f32[8,256,128]{2,1,0:T(8,128)}), f32[8,256,128]{2,1,0:T(8,128)S(1)}, u32[]{:S(2)}, u32[]{:S(2)}) async-start(f32[8,256,128]{2,1,0:T(8,128)} %spread.1), calls=%async_computation | async-start | bytes 2097152 | tf_op jit(solution)/shard_map/all_to_all | solution.py:447
  9.5 4.1 %collective-permute-start.1 = (s32[1,3]{1,0:T(1,128)S(1)}, s32[1,3]{1,0:T(1,128)S(1)}, u32[]{:S(2)}, u32[]{:S(2)}) collective-permute-start(s32[1,3]{1,0:T(1,128)S(1)} %bitcast.12), channel_id=1, source_target_pairs={{32,0},{36,4},{40,8},{44,12},{48,16},{52,20},{56,24},{60,28},{64,3... | collective-permute-start | bytes 44 | tf_op jit(solution)/shard_map/ppermute | solution.py:443
  13.7 1.9 %collective-permute-start = (s32[1,3]{1,0:T(1,128)S(1)}, s32[1,3]{1,0:T(1,128)S(1)}, u32[]{:S(2)}, u32[]{:S(2)}) collective-permute-start(s32[1,3]{1,0:T(1,128)S(1)} %bitcast.13), channel_id=1, source_target_pairs={{0,32},{4,36},{8,40},{12,44},{16,48},{20,52},{24,56},{28,60},{32,6... | collective-permute-start | bytes 44 | tf_op jit(solution)/shard_map/ppermute | solution.py:442
  15.6 1.5 %copy-done = bf16[704,1408]{1,0:T(8,128)(2,1)S(1)} copy-done((bf16[704,1408]{1,0:T(8,128)(2,1)S(1)}, bf16[704,1408]{1,0:T(8,128)(2,1)}, u32[]{:S(2)}) %copy-start) | copy-done | bytes 1982488
  17.2 0.9 %copy-done.3 = f32[1,1,64,512]{3,2,1,0:T(8,128)S(1)} copy-done((f32[1,1,64,512]{3,2,1,0:T(8,128)S(1)}, f32[1,1,64,512]{3,2,1,0:T(8,128)}, u32[]{:S(2)}) %copy-start.3) | copy-done | bytes 131096
  18.3 2.0 %collective-permute-done.below = s32[1,3]{1,0:T(1,128)S(1)} collective-permute-done((s32[1,3]{1,0:T(1,128)S(1)}, s32[1,3]{1,0:T(1,128)S(1)}, u32[]{:S(2)}, u32[]{:S(2)}) %collective-permute-start) | collective-permute-done | bytes 44 | tf_op jit(solution)/shard_map/ppermute | solution.py:442
  20.3 5.1 %all-to-all-done.window = f32[8,256,128]{2,1,0:T(8,128)S(1)} async-done(((f32[8,256,128]{2,1,0:T(8,128)}), f32[8,256,128]{2,1,0:T(8,128)S(1)}, u32[]{:S(2)}, u32[]{:S(2)}) %all-to-all-start) | async-done | bytes 1048608 | tf_op jit(solution)/shard_map/all_to_all | solution.py:447
  25.8 4.1 %collective-permute-start.2 = (f32[88,512]{1,0:T(8,128)S(1)}, f32[88,512]{1,0:T(8,128)S(1)}, u32[]{:S(2)}, u32[]{:S(2)}) collective-permute-start(f32[88,512]{1,0:T(8,128)S(1)} %get-tuple-element.17), channel_id=1, source_target_pairs={{32,0},{36,4},{40,8},{44,12},{48,16},{52,20},{56,24},{60,28},{64,3... | collective-permute-start | bytes 540680 | tf_op jit(solution)/shard_map/ppermute | solution.py:449
  29.9 1.9 %collective-permute-start.3 = (f32[88,512]{1,0:T(8,128)S(1)}, f32[88,512]{1,0:T(8,128)S(1)}, u32[]{:S(2)}, u32[]{:S(2)}) collective-permute-start(f32[88,512]{1,0:T(8,128)S(1)} %get-tuple-element.18), channel_id=1, source_target_pairs={{0,32},{4,36},{8,40},{12,44},{16,48},{20,52},{24,56},{28,60},{32,6... | collective-permute-start | bytes 540680 | tf_op jit(solution)/shard_map/ppermute | solution.py:450
  31.8 1.3 %collective-permute-done.2.piece_b = f32[88,512]{1,0:T(8,128)S(1)} collective-permute-done((f32[88,512]{1,0:T(8,128)S(1)}, f32[88,512]{1,0:T(8,128)S(1)}, u32[]{:S(2)}, u32[]{:S(2)}) %collective-permute-start.2) | collective-permute-done | bytes 180256 | tf_op jit(solution)/shard_map/ppermute | solution.py:449
  33.1 5.3 %collective-permute-done.3.piece_c = f32[88,512]{1,0:T(8,128)S(1)} collective-permute-done((f32[88,512]{1,0:T(8,128)S(1)}, f32[88,512]{1,0:T(8,128)S(1)}, u32[]{:S(2)}, u32[]{:S(2)}) %collective-permute-start.3) | collective-permute-done | bytes 180256 | tf_op jit(solution)/shard_map/ppermute | solution.py:450
  38.5 3.4 %basis.1 = (f32[9216,128]{1,0:T(8,128)S(1)}, f32[32,128]{1,0:T(8,128)S(1)}) custom-call(f32[88,512]{1,0:T(8,128)S(1)} %get-tuple-element.16.piece_a, f32[88,512]{1,0:T(8,128)S(1)} %collective-permute-done.2.piece_b, f32[88,512]{1,0:T(8,128)S(1)} %collective-permute-done.3.piece_c, f32[136,512]{1,0:T(8,128)S(1)} %get-tuple-element.15.sheet, ...), custom_call_target="tpu_custom_call" | custom-call | tf_op jit(solution)/shard_map/basis/pallas_call | solution.py:270
  41.9 5.2 %all-gather = f32[128,128]{1,0:T(8,128)S(1)} all-gather(f32[32,128]{1,0:T(8,128)S(1)} %get-tuple-element.20), channel_id=2, replica_groups=mesh['visit'=128,'patch'=4] {'patch'}, dimensions={0}, use_global_device_ids=true | all-gather | bytes 81920 | tf_op jit(solution)/shard_map/all_gather | solution.py:452
  47.2 1.6 %solve.1 = (f32[64,512]{1,0:T(8,128)S(1)}, f32[4,264,128]{2,1,0:T(8,128)S(1)}) custom-call(f32[4,32,128]{2,1,0:T(8,128)S(1)} %bitcast.8, f32[9216,128]{1,0:T(8,128)S(1)} %get-tuple-element.21.planes, f32[136,512]{1,0:T(8,128)S(1)} %get-tuple-element.15.sheet), custom_call_target="tpu_custom_call" | custom-call | tf_op jit(solution)/shard_map/solve/pallas_call | solution.py:365
  48.8 13.4 %all_to_all.10.stamps = f32[4,264,128]{2,1,0:T(8,128)S(1)} all-to-all(f32[4,264,128]{2,1,0:T(8,128)S(1)} %get-tuple-element.23), channel_id=1, replica_groups={{0,4,8,12},{16,20,24,28},{32,36,40,44},{48,52,56,60},{64,68,72,76},{80,..., dimensions={0} | all-to-all | bytes 1081344 | tf_op jit(solution)/shard_map/all_to_all | solution.py:456
  62.4 3.0 %collective-permute-start.4 = (f32[264,128]{1,0:T(8,128)S(1)}, f32[264,128]{1,0:T(8,128)S(1)}, u32[]{:S(2)}, u32[]{:S(2)}) collective-permute-start(f32[264,128]{1,0:T(8,128)S(1)} %get-tuple-element.25), channel_id=1, source_target_pairs={{16,32},{20,36},{24,40},{28,44},{32,16},{36,20},{40,24},{44,28},{4... | collective-permute-start | bytes 405512 | tf_op jit(solution)/shard_map/ppermute | solution.py:464
  65.4 2.7 %collective-permute-start.5 = (f32[264,128]{1,0:T(8,128)S(1)}, f32[264,128]{1,0:T(8,128)S(1)}, u32[]{:S(2)}, u32[]{:S(2)}) collective-permute-start(f32[264,128]{1,0:T(8,128)S(1)} %get-tuple-element.26), channel_id=1, source_target_pairs={{0,16},{4,20},{8,24},{12,28},{16,0},{20,4},{24,8},{28,12},{32,48},... | collective-permute-start | bytes 405512 | tf_op jit(solution)/shard_map/ppermute | solution.py:463
  68.1 3.4 %collective-permute-start.6 = (f32[264,128]{1,0:T(8,128)S(1)}, f32[264,128]{1,0:T(8,128)S(1)}, u32[]{:S(2)}, u32[]{:S(2)}) collective-permute-start(f32[264,128]{1,0:T(8,128)S(1)} %get-tuple-element.27), channel_id=1, source_target_pairs={{0,32},{4,36},{16,48},{20,52},{32,64},{36,68},{40,8},{44,12},{48,8... | collective-permute-start | bytes 405512 | tf_op jit(solution)/shard_map/ppermute | solution.py:462
  72.2 0.8 collective-permute-done.4.part_b
  72.9 2.6 %collective-permute-done.5.part_c = f32[264,128]{1,0:T(8,128)S(1)} collective-permute-done((f32[264,128]{1,0:T(8,128)S(1)}, f32[264,128]{1,0:T(8,128)S(1)}, u32[]{:S(2)}, u32[]{:S(2)}) %collective-permute-start.5) | collective-permute-done | bytes 135200 | tf_op jit(solution)/shard_map/ppermute | solution.py:463
  75.5 1.8 %collective-permute-done.6.part_d = f32[264,128]{1,0:T(8,128)S(1)} collective-permute-done((f32[264,128]{1,0:T(8,128)S(1)}, f32[264,128]{1,0:T(8,128)S(1)}, u32[]{:S(2)}, u32[]{:S(2)}) %collective-permute-start.6) | collective-permute-done | bytes 135200 | tf_op jit(solution)/shard_map/ppermute | solution.py:462
  77.3 0.7 mean.1
  (12 shorter events, 1.4 us)
Async XLA Ops:
  0.6 8.9 %copy-start.4 = (s32[1,1,3]{2,1,0:T(1,128)S(1)}, s32[1,1,3]{2,1,0:T(1,128)}, u32[]{:S(2)}) copy-start(s32[1,1,3]{2,1,0:T(1,128)} %param.8) | copy-start | bytes 40
  0.6 0.9 %copy-start.1 = (f32[1,64,512]{2,1,0:T(8,128)S(1)}, f32[1,64,512]{2,1,0:T(8,128)}, u32[]{:S(2)}) copy-start(f32[1,64,512]{2,1,0:T(8,128)} %param.5) | copy-start | bytes 393220
  1.6 14.1 %copy-start.2 = (f32[1,1,64,512]{3,2,1,0:T(8,128)S(1)}, f32[1,1,64,512]{3,2,1,0:T(8,128)}, u32[]{:S(2)}) copy-start(f32[1,1,64,512]{3,2,1,0:T(8,128)} %param.6) | copy-start | bytes 393220
  2.6 22.8 %all-to-all-start = ((f32[8,256,128]{2,1,0:T(8,128)}), f32[8,256,128]{2,1,0:T(8,128)S(1)}, u32[]{:S(2)}, u32[]{:S(2)}) async-start(f32[8,256,128]{2,1,0:T(8,128)} %spread.1), calls=%async_computation | async-start | bytes 2097152 | tf_op jit(solution)/shard_map/all_to_all | solution.py:447
  9.5 8.7 %collective-permute-start.1 = (s32[1,3]{1,0:T(1,128)S(1)}, s32[1,3]{1,0:T(1,128)S(1)}, u32[]{:S(2)}, u32[]{:S(2)}) collective-permute-start(s32[1,3]{1,0:T(1,128)S(1)} %bitcast.12), channel_id=1, source_target_pairs={{32,0},{36,4},{40,8},{44,12},{48,16},{52,20},{56,24},{60,28},{64,3... | collective-permute-start | bytes 44 | tf_op jit(solution)/shard_map/ppermute | solution.py:443
  13.7 6.6 %collective-permute-start = (s32[1,3]{1,0:T(1,128)S(1)}, s32[1,3]{1,0:T(1,128)S(1)}, u32[]{:S(2)}, u32[]{:S(2)}) collective-permute-start(s32[1,3]{1,0:T(1,128)S(1)} %bitcast.13), channel_id=1, source_target_pairs={{0,32},{4,36},{8,40},{12,44},{16,48},{20,52},{24,56},{28,60},{32,6... | collective-permute-start | bytes 44 | tf_op jit(solution)/shard_map/ppermute | solution.py:442
  15.6 1.6 %copy-start = (bf16[704,1408]{1,0:T(8,128)(2,1)S(1)}, bf16[704,1408]{1,0:T(8,128)(2,1)}, u32[]{:S(2)}) copy-start(bf16[704,1408]{1,0:T(8,128)(2,1)} %constant.2.clone.table) | copy-start | bytes 5947396
  17.2 0.9 %copy-start.3 = (f32[1,1,64,512]{3,2,1,0:T(8,128)S(1)}, f32[1,1,64,512]{3,2,1,0:T(8,128)}, u32[]{:S(2)}) copy-start(f32[1,1,64,512]{3,2,1,0:T(8,128)} %param.7) | copy-start | bytes 393220
  25.8 7.4 %collective-permute-start.2 = (f32[88,512]{1,0:T(8,128)S(1)}, f32[88,512]{1,0:T(8,128)S(1)}, u32[]{:S(2)}, u32[]{:S(2)}) collective-permute-start(f32[88,512]{1,0:T(8,128)S(1)} %get-tuple-element.17), channel_id=1, source_target_pairs={{32,0},{36,4},{40,8},{44,12},{48,16},{52,20},{56,24},{60,28},{64,3... | collective-permute-start | bytes 540680 | tf_op jit(solution)/shard_map/ppermute | solution.py:449
  29.9 8.6 %collective-permute-start.3 = (f32[88,512]{1,0:T(8,128)S(1)}, f32[88,512]{1,0:T(8,128)S(1)}, u32[]{:S(2)}, u32[]{:S(2)}) collective-permute-start(f32[88,512]{1,0:T(8,128)S(1)} %get-tuple-element.18), channel_id=1, source_target_pairs={{0,32},{4,36},{8,40},{12,44},{16,48},{20,52},{24,56},{28,60},{32,6... | collective-permute-start | bytes 540680 | tf_op jit(solution)/shard_map/ppermute | solution.py:450
  62.4 10.5 %collective-permute-start.4 = (f32[264,128]{1,0:T(8,128)S(1)}, f32[264,128]{1,0:T(8,128)S(1)}, u32[]{:S(2)}, u32[]{:S(2)}) collective-permute-start(f32[264,128]{1,0:T(8,128)S(1)} %get-tuple-element.25), channel_id=1, source_target_pairs={{16,32},{20,36},{24,40},{28,44},{32,16},{36,20},{40,24},{44,28},{4... | collective-permute-start | bytes 405512 | tf_op jit(solution)/shard_map/ppermute | solution.py:464
  65.4 10.1 %collective-permute-start.5 = (f32[264,128]{1,0:T(8,128)S(1)}, f32[264,128]{1,0:T(8,128)S(1)}, u32[]{:S(2)}, u32[]{:S(2)}) collective-permute-start(f32[264,128]{1,0:T(8,128)S(1)} %get-tuple-element.26), channel_id=1, source_target_pairs={{0,16},{4,20},{8,24},{12,28},{16,0},{20,4},{24,8},{28,12},{32,48},... | collective-permute-start | bytes 405512 | tf_op jit(solution)/shard_map/ppermute | solution.py:463
  68.1 9.2 %collective-permute-start.6 = (f32[264,128]{1,0:T(8,128)S(1)}, f32[264,128]{1,0:T(8,128)S(1)}, u32[]{:S(2)}, u32[]{:S(2)}) collective-permute-start(f32[264,128]{1,0:T(8,128)S(1)} %get-tuple-element.27), channel_id=1, source_target_pairs={{0,32},{4,36},{16,48},{20,52},{32,64},{36,68},{40,8},{44,12},{48,8... | collective-permute-start | bytes 405512 | tf_op jit(solution)/shard_map/ppermute | solution.py:462

commit v10 on v9

--- a/solution.py
+++ b/solution.py
@@ -163,11 +163,9 @@
     )(entries, science, weight, table)
 
 
-def serve_kernel(window, sheet, below, above, piece_own, piece_up, piece_down, strips):
+def cut_rows(window, requests, pieces, strips):
     base = (lax.axis_index("visit") // PLANE) * PLANE
-    own = (noted_number(sheet, 0), noted_number(sheet, 1))
-    others = [(entries[...][0, 0], entries[...][0, 1]) for entries in (below, above)]
-    for (asked, row_move), piece in zip((own, *others), (piece_own, piece_down, piece_up)):
+    for (asked, row_move), piece in zip(requests, pieces):
         start = (asked - base) * ROWS + row_move - KHALF
         first = lax.shift_right_arithmetic(start, 3)
         for part in range(SPAN // 8):
@@ -185,17 +183,25 @@
         piece[...] = pltpu.roll(strips[...], shift, axis=0)[:SENT]
 
 
-def serve(window, sheet, below, above):
-    shape = jax.ShapeDtypeStruct((SENT, COLS), jnp.float32)
-    return pl.pallas_call(
-        serve_kernel,
-        out_shape=(shape, shape, shape),
-        in_specs=[VMEM] * 4,
-        out_specs=(VMEM, VMEM, VMEM),
+def serve_kernel(window, below, above, piece_down, piece_up, strips):
+    requests = [(entries[...][0, 0], entries[...][0, 1]) for entries in (below, above)]
+    cut_rows(window, requests, (piece_down, piece_up), strips)
+
+
+def serve_own_kernel(window, sheet, piece, strips):
+    cut_rows(window, [(noted_number(sheet, 0), noted_number(sheet, 1))], (piece,), strips)
+
+
+def serve(kernel, name, count, *operands):
+    return pl.pallas_call(
+        kernel,
+        out_shape=(jax.ShapeDtypeStruct((SENT, COLS), jnp.float32),) * count,
+        in_specs=[VMEM] * len(operands),
+        out_specs=(VMEM,) * count,
         scratch_shapes=[pltpu.VMEM((SPAN, COLS), jnp.float32)],
         compiler_params=pltpu.CompilerParams(vmem_limit_bytes=LIMIT),
-        name="serve",
-    )(window, sheet, below, above)
+        name=name,
+    )(*operands)
 
 
 def basis_kernel(
@@ -445,7 +451,8 @@
         own, science[0, 0], inverse_variance[0, 0], jnp.asarray(tables())
     )
     window = lax.all_to_all(spread(template[0]), "visit", 0, 0, axis_index_groups=groups)
-    piece_own, piece_up, piece_down = serve(window, sheet, below, above)
+    piece_down, piece_up = serve(serve_kernel, "serve", 2, window, below, above)
+    (piece_own,) = serve(serve_own_kernel, "serve_own", 1, window, sheet)
     from_above = lax.ppermute(piece_down, "visit", downward)
     from_below = lax.ppermute(piece_up, "visit", upward)
     planes, gram = basis((piece_own, from_above, from_below), sheet, table)

time: 78.5 us -> 78.4 us (level)
  local copies, waits for them, and re-layouts: 3.36 us -> 0.92 us
  waiting for transfers between devices: 18.9 us -> 21.1 us
    ppermute x1, waiting for transfers between devices: 2.04 us -> 4.71 us  [shards(): below = lax.ppermute(own, 'visit', upward)]
    unnamed x10, local copies, waits for them, and re-layouts: 3.36 us -> 0.92 us
  transfers between devices with their start and end apart: 8 -> 8, of which waited for: 7 -> 7; matrix products, arithmetic and copies ran while one was open for 1% -> 1% of each run, Pallas kernels for 0% -> 1%
where the time goes in v10:
time: 78.4 us; the launch traced here: 78 us
  starting transfers between devices  28.1 us (36%)
  waiting for transfers between devices  21.1 us (27%)
  blocking collectives  18.7 us (24%)
  Pallas kernels  7.73 us (10%)
  local copies, waits for them, and re-layouts  0.92 us (1%)
    all_to_all x1, blocking collectives, shards(): lax.all_to_all(stamps, 'visit', 0, 0, axis_index_groups=lines)  13.4 us
    all_to_all x1, starting transfers between devices, shards(): lax.all_to_all(spread(template[0]), 'visit', 0, 0, axis_index_groups=groups)  6.93 us
    ppermute x1, waiting for transfers between devices, shards(): from_below = lax.ppermute(piece_up, 'visit', upward)  5.34 us
    all_gather x1, blocking collectives, shards(): grams = lax.all_gather(gram, 'patch')  5.25 us
    all_to_all x1, waiting for transfers between devices, shards(): lax.all_to_all(spread(template[0]), 'visit', 0, 0, axis_index_groups=groups)  5.06 us
    ppermute x1, waiting for transfers between devices, shards(): below = lax.ppermute(own, 'visit', upward)  4.71 us
    ppermute x1, starting transfers between devices, shards(): above = lax.ppermute(own, 'visit', downward)  4.13 us
    ppermute x1, starting transfers between devices, shards(): from_above = lax.ppermute(piece_down, 'visit', downward)  4.13 us
  transfers between devices with their start and end apart: 8, of which 7 were waited for; matrix products, arithmetic and copies ran while one was open for 1% of the time, Pallas kernels for 1%

profile of v10, /device:TPU:384, one launch (start us, length us, event | category | flops | bytes accessed | tf_op | source)
XLA Modules:
  0.0 78.0 jit_solution(2857534159944356837)
XLA Ops:
  0.7 0.9 %copy-done.1 = f32[1,64,512]{2,1,0:T(8,128)S(1)} copy-done((f32[1,64,512]{2,1,0:T(8,128)S(1)}, f32[1,64,512]{2,1,0:T(8,128)}, u32[]{:S(2)}) %copy-start.1) | copy-done | bytes 131096
  1.6 1.0 %spread.1 = f32[8,256,128]{2,1,0:T(8,128)} custom-call(f32[64,512]{1,0:T(8,128)S(1)} %bitcast.9), custom_call_target="tpu_custom_call" | custom-call | tf_op jit(solution)/shard_map/spread/pallas_call | solution.py:123
  2.6 6.9 %all-to-all-start = ((f32[8,256,128]{2,1,0:T(8,128)}), f32[8,256,128]{2,1,0:T(8,128)S(1)}, u32[]{:S(2)}, u32[]{:S(2)}) async-start(f32[8,256,128]{2,1,0:T(8,128)} %spread.1), calls=%async_computation | async-start | bytes 2097152 | tf_op jit(solution)/shard_map/all_to_all | solution.py:453
  9.5 4.1 %collective-permute-start.1 = (s32[1,3]{1,0:T(1,128)S(1)}, s32[1,3]{1,0:T(1,128)S(1)}, u32[]{:S(2)}, u32[]{:S(2)}) collective-permute-start(s32[1,3]{1,0:T(1,128)S(1)} %bitcast.12), channel_id=1, source_target_pairs={{32,0},{36,4},{40,8},{44,12},{48,16},{52,20},{56,24},{60,28},{64,3... | collective-permute-start | bytes 44 | tf_op jit(solution)/shard_map/ppermute | solution.py:449
  13.7 1.9 %collective-permute-start = (s32[1,3]{1,0:T(1,128)S(1)}, s32[1,3]{1,0:T(1,128)S(1)}, u32[]{:S(2)}, u32[]{:S(2)}) collective-permute-start(s32[1,3]{1,0:T(1,128)S(1)} %bitcast.13), channel_id=1, source_target_pairs={{0,32},{4,36},{8,40},{12,44},{16,48},{20,52},{24,56},{28,60},{32,6... | collective-permute-start | bytes 44 | tf_op jit(solution)/shard_map/ppermute | solution.py:448
  15.6 4.7 %collective-permute-done.below = s32[1,3]{1,0:T(1,128)S(1)} collective-permute-done((s32[1,3]{1,0:T(1,128)S(1)}, s32[1,3]{1,0:T(1,128)S(1)}, u32[]{:S(2)}, u32[]{:S(2)}) %collective-permute-start) | collective-permute-done | bytes 44 | tf_op jit(solution)/shard_map/ppermute | solution.py:448
  20.3 5.1 %all-to-all-done.window = f32[8,256,128]{2,1,0:T(8,128)S(1)} async-done(((f32[8,256,128]{2,1,0:T(8,128)}), f32[8,256,128]{2,1,0:T(8,128)S(1)}, u32[]{:S(2)}, u32[]{:S(2)}) %all-to-all-start) | async-done | bytes 1048608 | tf_op jit(solution)/shard_map/all_to_all | solution.py:453
  25.4 0.3 serve.1
  25.7 4.1 %collective-permute-start.2 = (f32[88,512]{1,0:T(8,128)S(1)}, f32[88,512]{1,0:T(8,128)S(1)}, u32[]{:S(2)}, u32[]{:S(2)}) collective-permute-start(f32[88,512]{1,0:T(8,128)S(1)} %get-tuple-element.15), channel_id=1, source_target_pairs={{32,0},{36,4},{40,8},{44,12},{48,16},{52,20},{56,24},{60,28},{64,3... | collective-permute-start | bytes 540680 | tf_op jit(solution)/shard_map/ppermute | solution.py:456
  29.8 1.9 %collective-permute-start.3 = (f32[88,512]{1,0:T(8,128)S(1)}, f32[88,512]{1,0:T(8,128)S(1)}, u32[]{:S(2)}, u32[]{:S(2)}) collective-permute-start(f32[88,512]{1,0:T(8,128)S(1)} %get-tuple-element.16), channel_id=1, source_target_pairs={{0,32},{4,36},{8,40},{12,44},{16,48},{20,52},{24,56},{28,60},{32,6... | collective-permute-start | bytes 540680 | tf_op jit(solution)/shard_map/ppermute | solution.py:457
  32.2 0.9 %collective-permute-done.2.piece_b = f32[88,512]{1,0:T(8,128)S(1)} collective-permute-done((f32[88,512]{1,0:T(8,128)S(1)}, f32[88,512]{1,0:T(8,128)S(1)}, u32[]{:S(2)}, u32[]{:S(2)}) %collective-permute-start.2) | collective-permute-done | bytes 180256 | tf_op jit(solution)/shard_map/ppermute | solution.py:456
  33.1 5.3 %collective-permute-done.3.piece_c = f32[88,512]{1,0:T(8,128)S(1)} collective-permute-done((f32[88,512]{1,0:T(8,128)S(1)}, f32[88,512]{1,0:T(8,128)S(1)}, u32[]{:S(2)}, u32[]{:S(2)}) %collective-permute-start.3) | collective-permute-done | bytes 180256 | tf_op jit(solution)/shard_map/ppermute | solution.py:457
  38.4 3.5 %basis.1 = (f32[9216,128]{1,0:T(8,128)S(1)}, f32[32,128]{1,0:T(8,128)S(1)}) custom-call(f32[88,512]{1,0:T(8,128)S(1)} %serve_own.1.piece_a, f32[88,512]{1,0:T(8,128)S(1)} %collective-permute-done.2.piece_b, f32[88,512]{1,0:T(8,128)S(1)} %collective-permute-done.3.piece_c, f32[136,512]{1,0:T(8,128)S(1)} %get-tuple-element.14.sheet, ...), custom_call_target="tpu_custom_call" | custom-call | tf_op jit(solution)/shard_map/basis/pallas_call | solution.py:276
  41.9 5.2 %all-gather = f32[128,128]{1,0:T(8,128)S(1)} all-gather(f32[32,128]{1,0:T(8,128)S(1)} %get-tuple-element.18), channel_id=2, replica_groups=mesh['visit'=128,'patch'=4] {'patch'}, dimensions={0}, use_global_device_ids=true | all-gather | bytes 81920 | tf_op jit(solution)/shard_map/all_gather | solution.py:459
  47.2 1.6 %solve.1 = (f32[64,512]{1,0:T(8,128)S(1)}, f32[4,264,128]{2,1,0:T(8,128)S(1)}) custom-call(f32[4,32,128]{2,1,0:T(8,128)S(1)} %bitcast.8, f32[9216,128]{1,0:T(8,128)S(1)} %get-tuple-element.19.planes, f32[136,512]{1,0:T(8,128)S(1)} %get-tuple-element.14.sheet), custom_call_target="tpu_custom_call" | custom-call | tf_op jit(solution)/shard_map/solve/pallas_call | solution.py:371
  48.8 13.4 %all_to_all.10.stamps = f32[4,264,128]{2,1,0:T(8,128)S(1)} all-to-all(f32[4,264,128]{2,1,0:T(8,128)S(1)} %get-tuple-element.21), channel_id=1, replica_groups={{0,4,8,12},{16,20,24,28},{32,36,40,44},{48,52,56,60},{64,68,72,76},{80,..., dimensions={0} | all-to-all | bytes 1081344 | tf_op jit(solution)/shard_map/all_to_all | solution.py:463
  62.4 3.0 %collective-permute-start.4 = (f32[264,128]{1,0:T(8,128)S(1)}, f32[264,128]{1,0:T(8,128)S(1)}, u32[]{:S(2)}, u32[]{:S(2)}) collective-permute-start(f32[264,128]{1,0:T(8,128)S(1)} %get-tuple-element.23), channel_id=1, source_target_pairs={{16,32},{20,36},{24,40},{28,44},{32,16},{36,20},{40,24},{44,28},{4... | collective-permute-start | bytes 405512 | tf_op jit(solution)/shard_map/ppermute | solution.py:471
  65.4 2.7 %collective-permute-start.5 = (f32[264,128]{1,0:T(8,128)S(1)}, f32[264,128]{1,0:T(8,128)S(1)}, u32[]{:S(2)}, u32[]{:S(2)}) collective-permute-start(f32[264,128]{1,0:T(8,128)S(1)} %get-tuple-element.24), channel_id=1, source_target_pairs={{0,16},{4,20},{8,24},{12,28},{16,0},{20,4},{24,8},{28,12},{32,48},... | collective-permute-start | bytes 405512 | tf_op jit(solution)/shard_map/ppermute | solution.py:470
  68.1 3.4 %collective-permute-start.6 = (f32[264,128]{1,0:T(8,128)S(1)}, f32[264,128]{1,0:T(8,128)S(1)}, u32[]{:S(2)}, u32[]{:S(2)}) collective-permute-start(f32[264,128]{1,0:T(8,128)S(1)} %get-tuple-element.25), channel_id=1, source_target_pairs={{0,32},{4,36},{16,48},{20,52},{32,64},{36,68},{40,8},{44,12},{48,8... | collective-permute-start | bytes 405512 | tf_op jit(solution)/shard_map/ppermute | solution.py:469
  71.5 0.7 subtract_bitcast_fusion
  72.2 0.8 collective-permute-done.4.part_b
  72.9 2.6 %collective-permute-done.5.part_c = f32[264,128]{1,0:T(8,128)S(1)} collective-permute-done((f32[264,128]{1,0:T(8,128)S(1)}, f32[264,128]{1,0:T(8,128)S(1)}, u32[]{:S(2)}, u32[]{:S(2)}) %collective-permute-start.5) | collective-permute-done | bytes 135200 | tf_op jit(solution)/shard_map/ppermute | solution.py:470
  75.5 1.8 %collective-permute-done.6.part_d = f32[264,128]{1,0:T(8,128)S(1)} collective-permute-done((f32[264,128]{1,0:T(8,128)S(1)}, f32[264,128]{1,0:T(8,128)S(1)}, u32[]{:S(2)}, u32[]{:S(2)}) %collective-permute-start.6) | collective-permute-done | bytes 135200 | tf_op jit(solution)/shard_map/ppermute | solution.py:469
  77.3 0.7 mean.1
  (13 shorter events, 0.6 us)
Async XLA Ops:
  0.6 8.9 %copy-start.4 = (s32[1,1,3]{2,1,0:T(1,128)S(1)}, s32[1,1,3]{2,1,0:T(1,128)}, u32[]{:S(2)}) copy-start(s32[1,1,3]{2,1,0:T(1,128)} %param.8) | copy-start | bytes 40
  0.6 0.9 %copy-start.1 = (f32[1,64,512]{2,1,0:T(8,128)S(1)}, f32[1,64,512]{2,1,0:T(8,128)}, u32[]{:S(2)}) copy-start(f32[1,64,512]{2,1,0:T(8,128)} %param.5) | copy-start | bytes 393220
  1.6 30.2 %copy-start = (bf16[704,1408]{1,0:T(8,128)(2,1)S(1)}, bf16[704,1408]{1,0:T(8,128)(2,1)}, u32[]{:S(2)}) copy-start(bf16[704,1408]{1,0:T(8,128)(2,1)} %constant.2.clone.table) | copy-start | bytes 5947396
  1.6 30.2 %copy-start.2 = (f32[1,1,64,512]{3,2,1,0:T(8,128)S(1)}, f32[1,1,64,512]{3,2,1,0:T(8,128)}, u32[]{:S(2)}) copy-start(f32[1,1,64,512]{3,2,1,0:T(8,128)} %param.6) | copy-start | bytes 393220
  1.6 30.2 %copy-start.3 = (f32[1,1,64,512]{3,2,1,0:T(8,128)S(1)}, f32[1,1,64,512]{3,2,1,0:T(8,128)}, u32[]{:S(2)}) copy-start(f32[1,1,64,512]{3,2,1,0:T(8,128)} %param.7) | copy-start | bytes 393220
  2.6 22.8 %all-to-all-start = ((f32[8,256,128]{2,1,0:T(8,128)}), f32[8,256,128]{2,1,0:T(8,128)S(1)}, u32[]{:S(2)}, u32[]{:S(2)}) async-start(f32[8,256,128]{2,1,0:T(8,128)} %spread.1), calls=%async_computation | async-start | bytes 2097152 | tf_op jit(solution)/shard_map/all_to_all | solution.py:453
  9.5 6.1 %collective-permute-start.1 = (s32[1,3]{1,0:T(1,128)S(1)}, s32[1,3]{1,0:T(1,128)S(1)}, u32[]{:S(2)}, u32[]{:S(2)}) collective-permute-start(s32[1,3]{1,0:T(1,128)S(1)} %bitcast.12), channel_id=1, source_target_pairs={{32,0},{36,4},{40,8},{44,12},{48,16},{52,20},{56,24},{60,28},{64,3... | collective-permute-start | bytes 44 | tf_op jit(solution)/shard_map/ppermute | solution.py:449
  13.7 6.6 %collective-permute-start = (s32[1,3]{1,0:T(1,128)S(1)}, s32[1,3]{1,0:T(1,128)S(1)}, u32[]{:S(2)}, u32[]{:S(2)}) collective-permute-start(s32[1,3]{1,0:T(1,128)S(1)} %bitcast.13), channel_id=1, source_target_pairs={{0,32},{4,36},{8,40},{12,44},{16,48},{20,52},{24,56},{28,60},{32,6... | collective-permute-start | bytes 44 | tf_op jit(solution)/shard_map/ppermute | solution.py:448
  25.7 7.4 %collective-permute-start.2 = (f32[88,512]{1,0:T(8,128)S(1)}, f32[88,512]{1,0:T(8,128)S(1)}, u32[]{:S(2)}, u32[]{:S(2)}) collective-permute-start(f32[88,512]{1,0:T(8,128)S(1)} %get-tuple-element.15), channel_id=1, source_target_pairs={{32,0},{36,4},{40,8},{44,12},{48,16},{52,20},{56,24},{60,28},{64,3... | collective-permute-start | bytes 540680 | tf_op jit(solution)/shard_map/ppermute | solution.py:456
  29.8 8.6 %collective-permute-start.3 = (f32[88,512]{1,0:T(8,128)S(1)}, f32[88,512]{1,0:T(8,128)S(1)}, u32[]{:S(2)}, u32[]{:S(2)}) collective-permute-start(f32[88,512]{1,0:T(8,128)S(1)} %get-tuple-element.16), channel_id=1, source_target_pairs={{0,32},{4,36},{8,40},{12,44},{16,48},{20,52},{24,56},{28,60},{32,6... | collective-permute-start | bytes 540680 | tf_op jit(solution)/shard_map/ppermute | solution.py:457
  62.4 10.5 %collective-permute-start.4 = (f32[264,128]{1,0:T(8,128)S(1)}, f32[264,128]{1,0:T(8,128)S(1)}, u32[]{:S(2)}, u32[]{:S(2)}) collective-permute-start(f32[264,128]{1,0:T(8,128)S(1)} %get-tuple-element.23), channel_id=1, source_target_pairs={{16,32},{20,36},{24,40},{28,44},{32,16},{36,20},{40,24},{44,28},{4... | collective-permute-start | bytes 405512 | tf_op jit(solution)/shard_map/ppermute | solution.py:471
  65.4 10.1 %collective-permute-start.5 = (f32[264,128]{1,0:T(8,128)S(1)}, f32[264,128]{1,0:T(8,128)S(1)}, u32[]{:S(2)}, u32[]{:S(2)}) collective-permute-start(f32[264,128]{1,0:T(8,128)S(1)} %get-tuple-element.24), channel_id=1, source_target_pairs={{0,16},{4,20},{8,24},{12,28},{16,0},{20,4},{24,8},{28,12},{32,48},... | collective-permute-start | bytes 405512 | tf_op jit(solution)/shard_map/ppermute | solution.py:470
  68.1 9.2 %collective-permute-start.6 = (f32[264,128]{1,0:T(8,128)S(1)}, f32[264,128]{1,0:T(8,128)S(1)}, u32[]{:S(2)}, u32[]{:S(2)}) collective-permute-start(f32[264,128]{1,0:T(8,128)S(1)} %get-tuple-element.25), channel_id=1, source_target_pairs={{0,32},{4,36},{16,48},{20,52},{32,64},{36,68},{40,8},{44,12},{48,8... | collective-permute-start | bytes 405512 | tf_op jit(solution)/shard_map/ppermute | solution.py:469

commit v11 on v10

--- a/solution.py
+++ b/solution.py
@@ -183,7 +183,7 @@
         piece[...] = pltpu.roll(strips[...], shift, axis=0)[:SENT]
 
 
-def serve_kernel(window, below, above, piece_down, piece_up, strips):
+def serve_kernel(window, sheet, below, above, piece_down, piece_up, strips):
     requests = [(entries[...][0, 0], entries[...][0, 1]) for entries in (below, above)]
     cut_rows(window, requests, (piece_down, piece_up), strips)
 
@@ -451,7 +451,7 @@
         own, science[0, 0], inverse_variance[0, 0], jnp.asarray(tables())
     )
     window = lax.all_to_all(spread(template[0]), "visit", 0, 0, axis_index_groups=groups)
-    piece_down, piece_up = serve(serve_kernel, "serve", 2, window, below, above)
+    piece_down, piece_up = serve(serve_kernel, "serve", 2, window, sheet, below, above)
     (piece_own,) = serve(serve_own_kernel, "serve_own", 1, window, sheet)
     from_above = lax.ppermute(piece_down, "visit", downward)
     from_below = lax.ppermute(piece_up, "visit", upward)

time: 78.4 us -> 78.4 us (level)
  local copies, waits for them, and re-layouts: 0.92 us -> 3.36 us
  waiting for transfers between devices: 21.1 us -> 18.7 us
    ppermute x1, waiting for transfers between devices: 4.71 us -> 2.04 us  [shards(): below = lax.ppermute(own, 'visit', upward)]
    unnamed x10, local copies, waits for them, and re-layouts: 0.92 us -> 3.36 us
where the time goes in v11:
time: 78.4 us; the launch traced here: 78 us
  starting transfers between devices  28.1 us (36%)
  waiting for transfers between devices  18.7 us (24%)
  blocking collectives  18.7 us (24%)
  Pallas kernels  7.68 us (10%)
  local copies, waits for them, and re-layouts  3.36 us (4%)
    all_to_all x1, blocking collectives, shards(): lax.all_to_all(stamps, 'visit', 0, 0, axis_index_groups=lines)  13.4 us
    all_to_all x1, starting transfers between devices, shards(): lax.all_to_all(spread(template[0]), 'visit', 0, 0, axis_index_groups=groups)  6.93 us
    ppermute x1, waiting for transfers between devices, shards(): from_below = lax.ppermute(piece_up, 'visit', upward)  5.34 us
    all_gather x1, blocking collectives, shards(): grams = lax.all_gather(gram, 'patch')  5.25 us
    all_to_all x1, waiting for transfers between devices, shards(): lax.all_to_all(spread(template[0]), 'visit', 0, 0, axis_index_groups=groups)  5.06 us
    ppermute x1, starting transfers between devices, shards(): above = lax.ppermute(own, 'visit', downward)  4.13 us
    ppermute x1, starting transfers between devices, shards(): from_above = lax.ppermute(piece_down, 'visit', downward)  4.13 us
    pallas_call x1, Pallas kernels, basis(): pl.pallas_call(basis_kernel, out_shape=(jax.ShapeDtypeStruct((BLOCKS * SL...  3.44 us
  transfers between devices with their start and end apart: 8, of which 7 were waited for; matrix products, arithmetic and copies ran while one was open for 1% of the time, Pallas kernels for 1%

profile of v11, /device:TPU:384, one launch (start us, length us, event | category | flops | bytes accessed | tf_op | source)
XLA Modules:
  0.0 78.0 jit_solution(7312465133825051634)
XLA Ops:
  0.6 0.9 %copy-done.1 = f32[1,64,512]{2,1,0:T(8,128)S(1)} copy-done((f32[1,64,512]{2,1,0:T(8,128)S(1)}, f32[1,64,512]{2,1,0:T(8,128)}, u32[]{:S(2)}) %copy-start.1) | copy-done | bytes 131096
  1.6 1.0 %spread.1 = f32[8,256,128]{2,1,0:T(8,128)} custom-call(f32[64,512]{1,0:T(8,128)S(1)} %bitcast.9), custom_call_target="tpu_custom_call" | custom-call | tf_op jit(solution)/shard_map/spread/pallas_call | solution.py:123
  2.6 6.9 %all-to-all-start = ((f32[8,256,128]{2,1,0:T(8,128)}), f32[8,256,128]{2,1,0:T(8,128)S(1)}, u32[]{:S(2)}, u32[]{:S(2)}) async-start(f32[8,256,128]{2,1,0:T(8,128)} %spread.1), calls=%async_computation | async-start | bytes 2097152 | tf_op jit(solution)/shard_map/all_to_all | solution.py:453
  9.5 4.1 %collective-permute-start.1 = (s32[1,3]{1,0:T(1,128)S(1)}, s32[1,3]{1,0:T(1,128)S(1)}, u32[]{:S(2)}, u32[]{:S(2)}) collective-permute-start(s32[1,3]{1,0:T(1,128)S(1)} %bitcast.12), channel_id=1, source_target_pairs={{32,0},{36,4},{40,8},{44,12},{48,16},{52,20},{56,24},{60,28},{64,3... | collective-permute-start | bytes 44 | tf_op jit(solution)/shard_map/ppermute | solution.py:449
  13.7 1.9 %collective-permute-start = (s32[1,3]{1,0:T(1,128)S(1)}, s32[1,3]{1,0:T(1,128)S(1)}, u32[]{:S(2)}, u32[]{:S(2)}) collective-permute-start(s32[1,3]{1,0:T(1,128)S(1)} %bitcast.13), channel_id=1, source_target_pairs={{0,32},{4,36},{8,40},{12,44},{16,48},{20,52},{24,56},{28,60},{32,6... | collective-permute-start | bytes 44 | tf_op jit(solution)/shard_map/ppermute | solution.py:448
  15.6 1.5 %copy-done = bf16[704,1408]{1,0:T(8,128)(2,1)S(1)} copy-done((bf16[704,1408]{1,0:T(8,128)(2,1)S(1)}, bf16[704,1408]{1,0:T(8,128)(2,1)}, u32[]{:S(2)}) %copy-start) | copy-done | bytes 1982488
  17.2 0.9 %copy-done.3 = f32[1,1,64,512]{3,2,1,0:T(8,128)S(1)} copy-done((f32[1,1,64,512]{3,2,1,0:T(8,128)S(1)}, f32[1,1,64,512]{3,2,1,0:T(8,128)}, u32[]{:S(2)}) %copy-start.3) | copy-done | bytes 131096
  18.3 2.0 %collective-permute-done.below = s32[1,3]{1,0:T(1,128)S(1)} collective-permute-done((s32[1,3]{1,0:T(1,128)S(1)}, s32[1,3]{1,0:T(1,128)S(1)}, u32[]{:S(2)}, u32[]{:S(2)}) %collective-permute-start) | collective-permute-done | bytes 44 | tf_op jit(solution)/shard_map/ppermute | solution.py:448
  20.3 5.1 %all-to-all-done.window = f32[8,256,128]{2,1,0:T(8,128)S(1)} async-done(((f32[8,256,128]{2,1,0:T(8,128)}), f32[8,256,128]{2,1,0:T(8,128)S(1)}, u32[]{:S(2)}, u32[]{:S(2)}) %all-to-all-start) | async-done | bytes 1048608 | tf_op jit(solution)/shard_map/all_to_all | solution.py:453
  25.7 4.1 %collective-permute-start.2 = (f32[88,512]{1,0:T(8,128)S(1)}, f32[88,512]{1,0:T(8,128)S(1)}, u32[]{:S(2)}, u32[]{:S(2)}) collective-permute-start(f32[88,512]{1,0:T(8,128)S(1)} %get-tuple-element.15), channel_id=1, source_target_pairs={{32,0},{36,4},{40,8},{44,12},{48,16},{52,20},{56,24},{60,28},{64,3... | collective-permute-start | bytes 540680 | tf_op jit(solution)/shard_map/ppermute | solution.py:456
  29.8 1.9 %collective-permute-start.3 = (f32[88,512]{1,0:T(8,128)S(1)}, f32[88,512]{1,0:T(8,128)S(1)}, u32[]{:S(2)}, u32[]{:S(2)}) collective-permute-start(f32[88,512]{1,0:T(8,128)S(1)} %get-tuple-element.16), channel_id=1, source_target_pairs={{0,32},{4,36},{8,40},{12,44},{16,48},{20,52},{24,56},{28,60},{32,6... | collective-permute-start | bytes 540680 | tf_op jit(solution)/shard_map/ppermute | solution.py:457
  32.0 1.1 %collective-permute-done.2.piece_b = f32[88,512]{1,0:T(8,128)S(1)} collective-permute-done((f32[88,512]{1,0:T(8,128)S(1)}, f32[88,512]{1,0:T(8,128)S(1)}, u32[]{:S(2)}, u32[]{:S(2)}) %collective-permute-start.2) | collective-permute-done | bytes 180256 | tf_op jit(solution)/shard_map/ppermute | solution.py:456
  33.1 5.3 %collective-permute-done.3.piece_c = f32[88,512]{1,0:T(8,128)S(1)} collective-permute-done((f32[88,512]{1,0:T(8,128)S(1)}, f32[88,512]{1,0:T(8,128)S(1)}, u32[]{:S(2)}, u32[]{:S(2)}) %collective-permute-start.3) | collective-permute-done | bytes 180256 | tf_op jit(solution)/shard_map/ppermute | solution.py:457
  38.4 3.4 %basis.1 = (f32[9216,128]{1,0:T(8,128)S(1)}, f32[32,128]{1,0:T(8,128)S(1)}) custom-call(f32[88,512]{1,0:T(8,128)S(1)} %serve_own.1.piece_a, f32[88,512]{1,0:T(8,128)S(1)} %collective-permute-done.2.piece_b, f32[88,512]{1,0:T(8,128)S(1)} %collective-permute-done.3.piece_c, f32[136,512]{1,0:T(8,128)S(1)} %get-tuple-element.14.sheet, ...), custom_call_target="tpu_custom_call" | custom-call | tf_op jit(solution)/shard_map/basis/pallas_call | solution.py:276
  41.9 5.2 %all-gather = f32[128,128]{1,0:T(8,128)S(1)} all-gather(f32[32,128]{1,0:T(8,128)S(1)} %get-tuple-element.18), channel_id=2, replica_groups=mesh['visit'=128,'patch'=4] {'patch'}, dimensions={0}, use_global_device_ids=true | all-gather | bytes 81920 | tf_op jit(solution)/shard_map/all_gather | solution.py:459
  47.1 1.6 %solve.1 = (f32[64,512]{1,0:T(8,128)S(1)}, f32[4,264,128]{2,1,0:T(8,128)S(1)}) custom-call(f32[4,32,128]{2,1,0:T(8,128)S(1)} %bitcast.8, f32[9216,128]{1,0:T(8,128)S(1)} %get-tuple-element.19.planes, f32[136,512]{1,0:T(8,128)S(1)} %get-tuple-element.14.sheet), custom_call_target="tpu_custom_call" | custom-call | tf_op jit(solution)/shard_map/solve/pallas_call | solution.py:371
  48.7 13.4 %all_to_all.10.stamps = f32[4,264,128]{2,1,0:T(8,128)S(1)} all-to-all(f32[4,264,128]{2,1,0:T(8,128)S(1)} %get-tuple-element.21), channel_id=1, replica_groups={{0,4,8,12},{16,20,24,28},{32,36,40,44},{48,52,56,60},{64,68,72,76},{80,..., dimensions={0} | all-to-all | bytes 1081344 | tf_op jit(solution)/shard_map/all_to_all | solution.py:463
  62.3 3.0 %collective-permute-start.4 = (f32[264,128]{1,0:T(8,128)S(1)}, f32[264,128]{1,0:T(8,128)S(1)}, u32[]{:S(2)}, u32[]{:S(2)}) collective-permute-start(f32[264,128]{1,0:T(8,128)S(1)} %get-tuple-element.23), channel_id=1, source_target_pairs={{16,32},{20,36},{24,40},{28,44},{32,16},{36,20},{40,24},{44,28},{4... | collective-permute-start | bytes 405512 | tf_op jit(solution)/shard_map/ppermute | solution.py:471
  65.3 2.7 %collective-permute-start.5 = (f32[264,128]{1,0:T(8,128)S(1)}, f32[264,128]{1,0:T(8,128)S(1)}, u32[]{:S(2)}, u32[]{:S(2)}) collective-permute-start(f32[264,128]{1,0:T(8,128)S(1)} %get-tuple-element.24), channel_id=1, source_target_pairs={{0,16},{4,20},{8,24},{12,28},{16,0},{20,4},{24,8},{28,12},{32,48},... | collective-permute-start | bytes 405512 | tf_op jit(solution)/shard_map/ppermute | solution.py:470
  68.0 3.4 %collective-permute-start.6 = (f32[264,128]{1,0:T(8,128)S(1)}, f32[264,128]{1,0:T(8,128)S(1)}, u32[]{:S(2)}, u32[]{:S(2)}) collective-permute-start(f32[264,128]{1,0:T(8,128)S(1)} %get-tuple-element.25), channel_id=1, source_target_pairs={{0,32},{4,36},{16,48},{20,52},{32,64},{36,68},{40,8},{44,12},{48,8... | collective-permute-start | bytes 405512 | tf_op jit(solution)/shard_map/ppermute | solution.py:469
  72.1 0.8 collective-permute-done.4.part_b
  72.9 2.6 %collective-permute-done.5.part_c = f32[264,128]{1,0:T(8,128)S(1)} collective-permute-done((f32[264,128]{1,0:T(8,128)S(1)}, f32[264,128]{1,0:T(8,128)S(1)}, u32[]{:S(2)}, u32[]{:S(2)}) %collective-permute-start.5) | collective-permute-done | bytes 135200 | tf_op jit(solution)/shard_map/ppermute | solution.py:470
  75.5 1.8 %collective-permute-done.6.part_d = f32[264,128]{1,0:T(8,128)S(1)} collective-permute-done((f32[264,128]{1,0:T(8,128)S(1)}, f32[264,128]{1,0:T(8,128)S(1)}, u32[]{:S(2)}, u32[]{:S(2)}) %collective-permute-start.6) | collective-permute-done | bytes 135200 | tf_op jit(solution)/shard_map/ppermute | solution.py:469
  77.3 0.7 mean.1
  (13 shorter events, 1.6 us)
Async XLA Ops:
  0.6 8.9 %copy-start.4 = (s32[1,1,3]{2,1,0:T(1,128)S(1)}, s32[1,1,3]{2,1,0:T(1,128)}, u32[]{:S(2)}) copy-start(s32[1,1,3]{2,1,0:T(1,128)} %param.8) | copy-start | bytes 40
  0.6 0.9 %copy-start.1 = (f32[1,64,512]{2,1,0:T(8,128)S(1)}, f32[1,64,512]{2,1,0:T(8,128)}, u32[]{:S(2)}) copy-start(f32[1,64,512]{2,1,0:T(8,128)} %param.5) | copy-start | bytes 393220
  1.6 14.1 %copy-start.2 = (f32[1,1,64,512]{3,2,1,0:T(8,128)S(1)}, f32[1,1,64,512]{3,2,1,0:T(8,128)}, u32[]{:S(2)}) copy-start(f32[1,1,64,512]{3,2,1,0:T(8,128)} %param.6) | copy-start | bytes 393220
  2.6 22.8 %all-to-all-start = ((f32[8,256,128]{2,1,0:T(8,128)}), f32[8,256,128]{2,1,0:T(8,128)S(1)}, u32[]{:S(2)}, u32[]{:S(2)}) async-start(f32[8,256,128]{2,1,0:T(8,128)} %spread.1), calls=%async_computation | async-start | bytes 2097152 | tf_op jit(solution)/shard_map/all_to_all | solution.py:453
  9.5 8.7 %collective-permute-start.1 = (s32[1,3]{1,0:T(1,128)S(1)}, s32[1,3]{1,0:T(1,128)S(1)}, u32[]{:S(2)}, u32[]{:S(2)}) collective-permute-start(s32[1,3]{1,0:T(1,128)S(1)} %bitcast.12), channel_id=1, source_target_pairs={{32,0},{36,4},{40,8},{44,12},{48,16},{52,20},{56,24},{60,28},{64,3... | collective-permute-start | bytes 44 | tf_op jit(solution)/shard_map/ppermute | solution.py:449
  13.7 6.6 %collective-permute-start = (s32[1,3]{1,0:T(1,128)S(1)}, s32[1,3]{1,0:T(1,128)S(1)}, u32[]{:S(2)}, u32[]{:S(2)}) collective-permute-start(s32[1,3]{1,0:T(1,128)S(1)} %bitcast.13), channel_id=1, source_target_pairs={{0,32},{4,36},{8,40},{12,44},{16,48},{20,52},{24,56},{28,60},{32,6... | collective-permute-start | bytes 44 | tf_op jit(solution)/shard_map/ppermute | solution.py:448
  15.6 1.6 %copy-start = (bf16[704,1408]{1,0:T(8,128)(2,1)S(1)}, bf16[704,1408]{1,0:T(8,128)(2,1)}, u32[]{:S(2)}) copy-start(bf16[704,1408]{1,0:T(8,128)(2,1)} %constant.2.clone.table) | copy-start | bytes 5947396
  17.2 0.9 %copy-start.3 = (f32[1,1,64,512]{3,2,1,0:T(8,128)S(1)}, f32[1,1,64,512]{3,2,1,0:T(8,128)}, u32[]{:S(2)}) copy-start(f32[1,1,64,512]{3,2,1,0:T(8,128)} %param.7) | copy-start | bytes 393220
  25.7 7.4 %collective-permute-start.2 = (f32[88,512]{1,0:T(8,128)S(1)}, f32[88,512]{1,0:T(8,128)S(1)}, u32[]{:S(2)}, u32[]{:S(2)}) collective-permute-start(f32[88,512]{1,0:T(8,128)S(1)} %get-tuple-element.15), channel_id=1, source_target_pairs={{32,0},{36,4},{40,8},{44,12},{48,16},{52,20},{56,24},{60,28},{64,3... | collective-permute-start | bytes 540680 | tf_op jit(solution)/shard_map/ppermute | solution.py:456
  29.8 8.6 %collective-permute-start.3 = (f32[88,512]{1,0:T(8,128)S(1)}, f32[88,512]{1,0:T(8,128)S(1)}, u32[]{:S(2)}, u32[]{:S(2)}) collective-permute-start(f32[88,512]{1,0:T(8,128)S(1)} %get-tuple-element.16), channel_id=1, source_target_pairs={{0,32},{4,36},{8,40},{12,44},{16,48},{20,52},{24,56},{28,60},{32,6... | collective-permute-start | bytes 540680 | tf_op jit(solution)/shard_map/ppermute | solution.py:457
  62.3 10.5 %collective-permute-start.4 = (f32[264,128]{1,0:T(8,128)S(1)}, f32[264,128]{1,0:T(8,128)S(1)}, u32[]{:S(2)}, u32[]{:S(2)}) collective-permute-start(f32[264,128]{1,0:T(8,128)S(1)} %get-tuple-element.23), channel_id=1, source_target_pairs={{16,32},{20,36},{24,40},{28,44},{32,16},{36,20},{40,24},{44,28},{4... | collective-permute-start | bytes 405512 | tf_op jit(solution)/shard_map/ppermute | solution.py:471
  65.3 10.1 %collective-permute-start.5 = (f32[264,128]{1,0:T(8,128)S(1)}, f32[264,128]{1,0:T(8,128)S(1)}, u32[]{:S(2)}, u32[]{:S(2)}) collective-permute-start(f32[264,128]{1,0:T(8,128)S(1)} %get-tuple-element.24), channel_id=1, source_target_pairs={{0,16},{4,20},{8,24},{12,28},{16,0},{20,4},{24,8},{28,12},{32,48},... | collective-permute-start | bytes 405512 | tf_op jit(solution)/shard_map/ppermute | solution.py:470
  68.0 9.2 %collective-permute-start.6 = (f32[264,128]{1,0:T(8,128)S(1)}, f32[264,128]{1,0:T(8,128)S(1)}, u32[]{:S(2)}, u32[]{:S(2)}) collective-permute-start(f32[264,128]{1,0:T(8,128)S(1)} %get-tuple-element.25), channel_id=1, source_target_pairs={{0,32},{4,36},{16,48},{20,52},{32,64},{36,68},{40,8},{44,12},{48,8... | collective-permute-start | bytes 405512 | tf_op jit(solution)/shard_map/ppermute | solution.py:469

commit v12 on v9

--- a/solution.py
+++ b/solution.py
@@ -415,11 +415,11 @@
 def mean_kernel(part_a, part_b, part_c, part_d, coadd):
     parts = (part_a, part_b, part_c, part_d)
     count = sum(part[TALL:, :] for part in parts)
-    count = jnp.maximum(count[:1], 1.0)
+    inverse = 1.0 / jnp.maximum(count[:1], 1.0)
     for block in range(BLOCKS):
         rows = slice(block * ROWS, (block + 1) * ROWS)
         total = sum(part[rows, :] for part in parts)
-        coadd[:, block * BLOCK : (block + 1) * BLOCK] = total / count
+        coadd[:, block * BLOCK : (block + 1) * BLOCK] = total * inverse
 
 
 def mean(*parts):

time: 78.5 us -> 78.5 us (level)
  no operation moved by 1% of the time
where the time goes in v12:
time: 78.5 us; the launch traced here: 78 us
  starting transfers between devices  28.1 us (36%)
  waiting for transfers between devices  18.9 us (24%)
  blocking collectives  18.7 us (24%)
  Pallas kernels  7.53 us (10%)
  local copies, waits for them, and re-layouts  3.36 us (4%)
    all_to_all x1, blocking collectives, shards(): lax.all_to_all(stamps, 'visit', 0, 0, axis_index_groups=lines)  13.4 us
    all_to_all x1, starting transfers between devices, shards(): lax.all_to_all(spread(template[0]), 'visit', 0, 0, axis_index_groups=groups)  6.93 us
    ppermute x1, waiting for transfers between devices, shards(): from_below = lax.ppermute(piece_up, 'visit', upward)  5.34 us
    all_gather x1, blocking collectives, shards(): grams = lax.all_gather(gram, 'patch')  5.25 us
    all_to_all x1, waiting for transfers between devices, shards(): lax.all_to_all(spread(template[0]), 'visit', 0, 0, axis_index_groups=groups)  5.06 us
    ppermute x1, starting transfers between devices, shards(): above = lax.ppermute(own, 'visit', downward)  4.13 us
    ppermute x1, starting transfers between devices, shards(): from_above = lax.ppermute(piece_down, 'visit', downward)  4.13 us
    pallas_call x1, Pallas kernels, basis(): pl.pallas_call(basis_kernel, out_shape=(jax.ShapeDtypeStruct((BLOCKS * SL...  3.44 us
  transfers between devices with their start and end apart: 8, of which 7 were waited for; matrix products, arithmetic and copies ran while one was open for 1% of the time, Pallas kernels for 0%

profile of v12, /device:TPU:384, one launch (start us, length us, event | category | flops | bytes accessed | tf_op | source)
XLA Modules:
  0.0 78.0 jit_solution(773510587183993489)
XLA Ops:
  0.6 0.9 %copy-done.1 = f32[1,64,512]{2,1,0:T(8,128)S(1)} copy-done((f32[1,64,512]{2,1,0:T(8,128)S(1)}, f32[1,64,512]{2,1,0:T(8,128)}, u32[]{:S(2)}) %copy-start.1) | copy-done | bytes 131096
  1.6 1.0 %spread.1 = f32[8,256,128]{2,1,0:T(8,128)} custom-call(f32[64,512]{1,0:T(8,128)S(1)} %bitcast.9), custom_call_target="tpu_custom_call" | custom-call | tf_op jit(solution)/shard_map/spread/pallas_call | solution.py:123
  2.6 6.9 %all-to-all-start = ((f32[8,256,128]{2,1,0:T(8,128)}), f32[8,256,128]{2,1,0:T(8,128)S(1)}, u32[]{:S(2)}, u32[]{:S(2)}) async-start(f32[8,256,128]{2,1,0:T(8,128)} %spread.1), calls=%async_computation | async-start | bytes 2097152 | tf_op jit(solution)/shard_map/all_to_all | solution.py:447
  9.5 4.1 %collective-permute-start.1 = (s32[1,3]{1,0:T(1,128)S(1)}, s32[1,3]{1,0:T(1,128)S(1)}, u32[]{:S(2)}, u32[]{:S(2)}) collective-permute-start(s32[1,3]{1,0:T(1,128)S(1)} %bitcast.12), channel_id=1, source_target_pairs={{32,0},{36,4},{40,8},{44,12},{48,16},{52,20},{56,24},{60,28},{64,3... | collective-permute-start | bytes 44 | tf_op jit(solution)/shard_map/ppermute | solution.py:443
  13.7 1.9 %collective-permute-start = (s32[1,3]{1,0:T(1,128)S(1)}, s32[1,3]{1,0:T(1,128)S(1)}, u32[]{:S(2)}, u32[]{:S(2)}) collective-permute-start(s32[1,3]{1,0:T(1,128)S(1)} %bitcast.13), channel_id=1, source_target_pairs={{0,32},{4,36},{8,40},{12,44},{16,48},{20,52},{24,56},{28,60},{32,6... | collective-permute-start | bytes 44 | tf_op jit(solution)/shard_map/ppermute | solution.py:442
  15.6 1.5 %copy-done = bf16[704,1408]{1,0:T(8,128)(2,1)S(1)} copy-done((bf16[704,1408]{1,0:T(8,128)(2,1)S(1)}, bf16[704,1408]{1,0:T(8,128)(2,1)}, u32[]{:S(2)}) %copy-start) | copy-done | bytes 1982488
  17.2 0.9 %copy-done.3 = f32[1,1,64,512]{3,2,1,0:T(8,128)S(1)} copy-done((f32[1,1,64,512]{3,2,1,0:T(8,128)S(1)}, f32[1,1,64,512]{3,2,1,0:T(8,128)}, u32[]{:S(2)}) %copy-start.3) | copy-done | bytes 131096
  18.3 2.0 %collective-permute-done.below = s32[1,3]{1,0:T(1,128)S(1)} collective-permute-done((s32[1,3]{1,0:T(1,128)S(1)}, s32[1,3]{1,0:T(1,128)S(1)}, u32[]{:S(2)}, u32[]{:S(2)}) %collective-permute-start) | collective-permute-done | bytes 44 | tf_op jit(solution)/shard_map/ppermute | solution.py:442
  20.3 5.1 %all-to-all-done.window = f32[8,256,128]{2,1,0:T(8,128)S(1)} async-done(((f32[8,256,128]{2,1,0:T(8,128)}), f32[8,256,128]{2,1,0:T(8,128)S(1)}, u32[]{:S(2)}, u32[]{:S(2)}) %all-to-all-start) | async-done | bytes 1048608 | tf_op jit(solution)/shard_map/all_to_all | solution.py:447
  25.8 4.1 %collective-permute-start.2 = (f32[88,512]{1,0:T(8,128)S(1)}, f32[88,512]{1,0:T(8,128)S(1)}, u32[]{:S(2)}, u32[]{:S(2)}) collective-permute-start(f32[88,512]{1,0:T(8,128)S(1)} %get-tuple-element.17), channel_id=1, source_target_pairs={{32,0},{36,4},{40,8},{44,12},{48,16},{52,20},{56,24},{60,28},{64,3... | collective-permute-start | bytes 540680 | tf_op jit(solution)/shard_map/ppermute | solution.py:449
  29.9 1.9 %collective-permute-start.3 = (f32[88,512]{1,0:T(8,128)S(1)}, f32[88,512]{1,0:T(8,128)S(1)}, u32[]{:S(2)}, u32[]{:S(2)}) collective-permute-start(f32[88,512]{1,0:T(8,128)S(1)} %get-tuple-element.18), channel_id=1, source_target_pairs={{0,32},{4,36},{8,40},{12,44},{16,48},{20,52},{24,56},{28,60},{32,6... | collective-permute-start | bytes 540680 | tf_op jit(solution)/shard_map/ppermute | solution.py:450
  31.8 1.3 %collective-permute-done.2.piece_b = f32[88,512]{1,0:T(8,128)S(1)} collective-permute-done((f32[88,512]{1,0:T(8,128)S(1)}, f32[88,512]{1,0:T(8,128)S(1)}, u32[]{:S(2)}, u32[]{:S(2)}) %collective-permute-start.2) | collective-permute-done | bytes 180256 | tf_op jit(solution)/shard_map/ppermute | solution.py:449
  33.1 5.3 %collective-permute-done.3.piece_c = f32[88,512]{1,0:T(8,128)S(1)} collective-permute-done((f32[88,512]{1,0:T(8,128)S(1)}, f32[88,512]{1,0:T(8,128)S(1)}, u32[]{:S(2)}, u32[]{:S(2)}) %collective-permute-start.3) | collective-permute-done | bytes 180256 | tf_op jit(solution)/shard_map/ppermute | solution.py:450
  38.5 3.4 %basis.1 = (f32[9216,128]{1,0:T(8,128)S(1)}, f32[32,128]{1,0:T(8,128)S(1)}) custom-call(f32[88,512]{1,0:T(8,128)S(1)} %get-tuple-element.16.piece_a, f32[88,512]{1,0:T(8,128)S(1)} %collective-permute-done.2.piece_b, f32[88,512]{1,0:T(8,128)S(1)} %collective-permute-done.3.piece_c, f32[136,512]{1,0:T(8,128)S(1)} %get-tuple-element.15.sheet, ...), custom_call_target="tpu_custom_call" | custom-call | tf_op jit(solution)/shard_map/basis/pallas_call | solution.py:270
  41.9 5.2 %all-gather = f32[128,128]{1,0:T(8,128)S(1)} all-gather(f32[32,128]{1,0:T(8,128)S(1)} %get-tuple-element.20), channel_id=2, replica_groups=mesh['visit'=128,'patch'=4] {'patch'}, dimensions={0}, use_global_device_ids=true | all-gather | bytes 81920 | tf_op jit(solution)/shard_map/all_gather | solution.py:452
  47.2 1.6 %solve.1 = (f32[64,512]{1,0:T(8,128)S(1)}, f32[4,264,128]{2,1,0:T(8,128)S(1)}) custom-call(f32[4,32,128]{2,1,0:T(8,128)S(1)} %bitcast.8, f32[9216,128]{1,0:T(8,128)S(1)} %get-tuple-element.21.planes, f32[136,512]{1,0:T(8,128)S(1)} %get-tuple-element.15.sheet), custom_call_target="tpu_custom_call" | custom-call | tf_op jit(solution)/shard_map/solve/pallas_call | solution.py:365
  48.8 13.4 %all_to_all.10.stamps = f32[4,264,128]{2,1,0:T(8,128)S(1)} all-to-all(f32[4,264,128]{2,1,0:T(8,128)S(1)} %get-tuple-element.23), channel_id=1, replica_groups={{0,4,8,12},{16,20,24,28},{32,36,40,44},{48,52,56,60},{64,68,72,76},{80,..., dimensions={0} | all-to-all | bytes 1081344 | tf_op jit(solution)/shard_map/all_to_all | solution.py:456
  62.4 3.0 %collective-permute-start.4 = (f32[264,128]{1,0:T(8,128)S(1)}, f32[264,128]{1,0:T(8,128)S(1)}, u32[]{:S(2)}, u32[]{:S(2)}) collective-permute-start(f32[264,128]{1,0:T(8,128)S(1)} %get-tuple-element.25), channel_id=1, source_target_pairs={{16,32},{20,36},{24,40},{28,44},{32,16},{36,20},{40,24},{44,28},{4... | collective-permute-start | bytes 405512 | tf_op jit(solution)/shard_map/ppermute | solution.py:464
  65.4 2.7 %collective-permute-start.5 = (f32[264,128]{1,0:T(8,128)S(1)}, f32[264,128]{1,0:T(8,128)S(1)}, u32[]{:S(2)}, u32[]{:S(2)}) collective-permute-start(f32[264,128]{1,0:T(8,128)S(1)} %get-tuple-element.26), channel_id=1, source_target_pairs={{0,16},{4,20},{8,24},{12,28},{16,0},{20,4},{24,8},{28,12},{32,48},... | collective-permute-start | bytes 405512 | tf_op jit(solution)/shard_map/ppermute | solution.py:463
  68.1 3.4 %collective-permute-start.6 = (f32[264,128]{1,0:T(8,128)S(1)}, f32[264,128]{1,0:T(8,128)S(1)}, u32[]{:S(2)}, u32[]{:S(2)}) collective-permute-start(f32[264,128]{1,0:T(8,128)S(1)} %get-tuple-element.27), channel_id=1, source_target_pairs={{0,32},{4,36},{16,48},{20,52},{32,64},{36,68},{40,8},{44,12},{48,8... | collective-permute-start | bytes 405512 | tf_op jit(solution)/shard_map/ppermute | solution.py:462
  72.2 0.8 collective-permute-done.4.part_b
  72.9 2.6 %collective-permute-done.5.part_c = f32[264,128]{1,0:T(8,128)S(1)} collective-permute-done((f32[264,128]{1,0:T(8,128)S(1)}, f32[264,128]{1,0:T(8,128)S(1)}, u32[]{:S(2)}, u32[]{:S(2)}) %collective-permute-start.5) | collective-permute-done | bytes 135200 | tf_op jit(solution)/shard_map/ppermute | solution.py:463
  75.5 1.8 %collective-permute-done.6.part_d = f32[264,128]{1,0:T(8,128)S(1)} collective-permute-done((f32[264,128]{1,0:T(8,128)S(1)}, f32[264,128]{1,0:T(8,128)S(1)}, u32[]{:S(2)}, u32[]{:S(2)}) %collective-permute-start.6) | collective-permute-done | bytes 135200 | tf_op jit(solution)/shard_map/ppermute | solution.py:462
  77.3 0.7 mean.1
  (12 shorter events, 1.4 us)
Async XLA Ops:
  0.6 8.9 %copy-start.4 = (s32[1,1,3]{2,1,0:T(1,128)S(1)}, s32[1,1,3]{2,1,0:T(1,128)}, u32[]{:S(2)}) copy-start(s32[1,1,3]{2,1,0:T(1,128)} %param.8) | copy-start | bytes 40
  0.6 0.9 %copy-start.1 = (f32[1,64,512]{2,1,0:T(8,128)S(1)}, f32[1,64,512]{2,1,0:T(8,128)}, u32[]{:S(2)}) copy-start(f32[1,64,512]{2,1,0:T(8,128)} %param.5) | copy-start | bytes 393220
  1.6 14.1 %copy-start.2 = (f32[1,1,64,512]{3,2,1,0:T(8,128)S(1)}, f32[1,1,64,512]{3,2,1,0:T(8,128)}, u32[]{:S(2)}) copy-start(f32[1,1,64,512]{3,2,1,0:T(8,128)} %param.6) | copy-start | bytes 393220
  2.6 22.8 %all-to-all-start = ((f32[8,256,128]{2,1,0:T(8,128)}), f32[8,256,128]{2,1,0:T(8,128)S(1)}, u32[]{:S(2)}, u32[]{:S(2)}) async-start(f32[8,256,128]{2,1,0:T(8,128)} %spread.1), calls=%async_computation | async-start | bytes 2097152 | tf_op jit(solution)/shard_map/all_to_all | solution.py:447
  9.5 8.7 %collective-permute-start.1 = (s32[1,3]{1,0:T(1,128)S(1)}, s32[1,3]{1,0:T(1,128)S(1)}, u32[]{:S(2)}, u32[]{:S(2)}) collective-permute-start(s32[1,3]{1,0:T(1,128)S(1)} %bitcast.12), channel_id=1, source_target_pairs={{32,0},{36,4},{40,8},{44,12},{48,16},{52,20},{56,24},{60,28},{64,3... | collective-permute-start | bytes 44 | tf_op jit(solution)/shard_map/ppermute | solution.py:443
  13.7 6.6 %collective-permute-start = (s32[1,3]{1,0:T(1,128)S(1)}, s32[1,3]{1,0:T(1,128)S(1)}, u32[]{:S(2)}, u32[]{:S(2)}) collective-permute-start(s32[1,3]{1,0:T(1,128)S(1)} %bitcast.13), channel_id=1, source_target_pairs={{0,32},{4,36},{8,40},{12,44},{16,48},{20,52},{24,56},{28,60},{32,6... | collective-permute-start | bytes 44 | tf_op jit(solution)/shard_map/ppermute | solution.py:442
  15.6 1.6 %copy-start = (bf16[704,1408]{1,0:T(8,128)(2,1)S(1)}, bf16[704,1408]{1,0:T(8,128)(2,1)}, u32[]{:S(2)}) copy-start(bf16[704,1408]{1,0:T(8,128)(2,1)} %constant.2.clone.table) | copy-start | bytes 5947396
  17.2 0.9 %copy-start.3 = (f32[1,1,64,512]{3,2,1,0:T(8,128)S(1)}, f32[1,1,64,512]{3,2,1,0:T(8,128)}, u32[]{:S(2)}) copy-start(f32[1,1,64,512]{3,2,1,0:T(8,128)} %param.7) | copy-start | bytes 393220
  25.8 7.4 %collective-permute-start.2 = (f32[88,512]{1,0:T(8,128)S(1)}, f32[88,512]{1,0:T(8,128)S(1)}, u32[]{:S(2)}, u32[]{:S(2)}) collective-permute-start(f32[88,512]{1,0:T(8,128)S(1)} %get-tuple-element.17), channel_id=1, source_target_pairs={{32,0},{36,4},{40,8},{44,12},{48,16},{52,20},{56,24},{60,28},{64,3... | collective-permute-start | bytes 540680 | tf_op jit(solution)/shard_map/ppermute | solution.py:449
  29.9 8.6 %collective-permute-start.3 = (f32[88,512]{1,0:T(8,128)S(1)}, f32[88,512]{1,0:T(8,128)S(1)}, u32[]{:S(2)}, u32[]{:S(2)}) collective-permute-start(f32[88,512]{1,0:T(8,128)S(1)} %get-tuple-element.18), channel_id=1, source_target_pairs={{0,32},{4,36},{8,40},{12,44},{16,48},{20,52},{24,56},{28,60},{32,6... | collective-permute-start | bytes 540680 | tf_op jit(solution)/shard_map/ppermute | solution.py:450
  62.4 10.5 %collective-permute-start.4 = (f32[264,128]{1,0:T(8,128)S(1)}, f32[264,128]{1,0:T(8,128)S(1)}, u32[]{:S(2)}, u32[]{:S(2)}) collective-permute-start(f32[264,128]{1,0:T(8,128)S(1)} %get-tuple-element.25), channel_id=1, source_target_pairs={{16,32},{20,36},{24,40},{28,44},{32,16},{36,20},{40,24},{44,28},{4... | collective-permute-start | bytes 405512 | tf_op jit(solution)/shard_map/ppermute | solution.py:464
  65.4 10.1 %collective-permute-start.5 = (f32[264,128]{1,0:T(8,128)S(1)}, f32[264,128]{1,0:T(8,128)S(1)}, u32[]{:S(2)}, u32[]{:S(2)}) collective-permute-start(f32[264,128]{1,0:T(8,128)S(1)} %get-tuple-element.26), channel_id=1, source_target_pairs={{0,16},{4,20},{8,24},{12,28},{16,0},{20,4},{24,8},{28,12},{32,48},... | collective-permute-start | bytes 405512 | tf_op jit(solution)/shard_map/ppermute | solution.py:463
  68.1 9.2 %collective-permute-start.6 = (f32[264,128]{1,0:T(8,128)S(1)}, f32[264,128]{1,0:T(8,128)S(1)}, u32[]{:S(2)}, u32[]{:S(2)}) collective-permute-start(f32[264,128]{1,0:T(8,128)S(1)} %get-tuple-element.27), channel_id=1, source_target_pairs={{0,32},{4,36},{16,48},{20,52},{32,64},{36,68},{40,8},{44,12},{48,8... | collective-permute-start | bytes 405512 | tf_op jit(solution)/shard_map/ppermute | solution.py:462
